TPU v7x, 128 devices: a whole 4x4x4 slice. The times are simulated.
128 devices in a mesh: group: 16 (over z, x), shard: 8 (over y, core).
Axes of the slice: x: 4, y: 4, z: 4, core: 2. Of those that a mesh axis runs over, the one named last changes fastest.
Arguments:
- replay: float32 [1048576, 42], P(('group', 'shard')), may hold values from -6 to 6
- sample_index: int32 [128, 128, 32], P(('group', 'shard')), may hold values from 0 to 8191
- pair_count: int32 [128, 128], P(('group', 'shard')), may hold values from 0 to 32, as said below
- noise: float32 [128, 128, 32, 6], P(('group', 'shard')), may hold values from -5 to 5
- actor: float32 [71942], replicated
- critic: float32 [2, 72193], replicated
- actor_momentum: float32 [71942], replicated, may hold values from -0.3125 to 0.3125
- critic_momentum: float32 [2, 72193], replicated, may hold values from -0.3125 to 0.3125
- actor_average: float32 [71942], replicated
- critic_average: float32 [2, 72193], replicated
- actor_target: float32 [71942], replicated
- critic_target: float32 [2, 72193], replicated
Outputs:
- loss_parts: float32 [2], replicated
- priority: float32 [128, 128, 32], P(('group', 'shard'))
- actor_new: float32 [71942], replicated
- critic_new: float32 [2, 72193], replicated
- actor_momentum_new: float32 [71942], replicated
- critic_momentum_new: float32 [2, 72193], replicated
- actor_average_new: float32 [71942], replicated
- critic_average_new: float32 [2, 72193], replicated
- actor_target_new: float32 [71942], replicated
- critic_target_new: float32 [2, 72193], replicated
- actor_low: bfloat16 [71942], replicated
- critic_low: bfloat16 [2, 72193], replicated
Inputs may be any that keep to these rules, and one draw needn't show every extreme that they name: `pair_count`: at most 32; the last shard fills all 32 slots to the last device.
All inputs are finite; a program needn't handle non-finite values.
Results may differ from a plain program's by a relative error of at most 0.001.
Values sent between devices are 32-bit elements; how exact they have to be, the bound alone decides.
A program may use at most 128 MiB of HBM per device.

v0:
```python
import math

import jax
import jax.numpy as jnp
from jax import lax
from jax.sharding import PartitionSpec as P

OBS = 17
ACT = 6
UNITS = 256
CAP = 32


def matmul(a, b):
    return jnp.dot(a, b, precision=lax.Precision.HIGHEST)


def unpack(flat, width_in, width_out):
    shapes = [
        (width_in, UNITS),
        (UNITS,),
        (UNITS, UNITS),
        (UNITS,),
        (UNITS, width_out),
        (width_out,),
    ]
    pieces = []
    start = 0
    for shape in shapes:
        number = math.prod(shape)
        pieces.append(flat[start : start + number].reshape(shape))
        start = start + number
    return pieces


def network(flat, inputs, width_out):
    w_one, b_one, w_two, b_two, w_three, b_three = unpack(flat, inputs.shape[1], width_out)
    hidden = jax.nn.silu(matmul(inputs, w_one) + b_one)
    hidden = jax.nn.silu(matmul(hidden, w_two) + b_two)
    return matmul(hidden, w_three) + b_three


def bootstrap(actor_target, critic_target, next_state, reward, weight, noise):
    smooth = 0.5 * jnp.tanh(0.4 * noise)
    next_action = jnp.tanh(network(actor_target, next_state, ACT) + smooth)
    joined = jnp.concatenate([next_state, next_action], 1)
    first = network(critic_target[0], joined, 1)[:, 0]
    second = network(critic_target[1], joined, 1)[:, 0]
    return reward + 0.99 * weight * jnp.minimum(first, second)


def numerator(actor, critic, critic_fixed, state, action, target, valid):
    joined = jnp.concatenate([state, action], 1)
    first = network(critic[0], joined, 1)[:, 0]
    second = network(critic[1], joined, 1)[:, 0]
    policy = jnp.tanh(network(actor, state, ACT))
    policy_value = network(critic_fixed[0], jnp.concatenate([state, policy], 1), 1)[:, 0]
    terms = valid * ((first - target) ** 2 + (second - target) ** 2 - policy_value)
    return (jnp.sum(terms), first - target)


def update(weight, grad, momentum, average, target):
    momentum_new = 0.9 * momentum + grad
    weight_new = weight - 0.1 * (grad + 0.9 * momentum_new)
    average_new = 0.99 * average + 0.01 * weight_new
    target_new = 0.005 * weight_new + 0.995 * target
    return (weight_new, momentum_new, average_new, target_new, weight_new.astype(jnp.bfloat16))


def local(
    replay,
    sample_index,
    pair_count,
    noise,
    actor,
    critic,
    actor_momentum,
    critic_momentum,
    actor_average,
    critic_average,
    actor_target,
    critic_target,
):
    peers = lax.axis_size(("group", "shard"))
    width = replay.shape[1]
    outgoing = replay[sample_index[0]]
    count_col = pair_count.reshape(peers, 1)
    arrived, arrived_count = (
        lax.all_to_all(outgoing, ("group", "shard"), split_axis=0, concat_axis=0, tiled=True),
        lax.all_to_all(count_col, ("group", "shard"), split_axis=0, concat_axis=0, tiled=True),
    )
    slots = lax.broadcasted_iota(jnp.int32, (peers, CAP), 1)
    valid = (slots < arrived_count).astype(jnp.float32).reshape(-1)
    batch = arrived.reshape(peers * CAP, width)
    noise_rows = noise.reshape(peers * CAP, ACT)
    state = batch[:, :OBS]
    action = batch[:, OBS : OBS + ACT]
    reward = batch[:, OBS + ACT]
    weight = batch[:, OBS + ACT + 1]
    next_state = batch[:, OBS + ACT + 2 :]
    target = bootstrap(actor_target, critic_target, next_state, reward, weight, noise_rows)
    local_count = jnp.sum(valid)
    count = lax.psum(local_count, ("group", "shard"))

    def scaled(actor_in, critic_in):
        total, delta = numerator(actor_in, critic_in, critic, state, action, target, valid)
        return (total / count, (total, delta))

    value, pull, extra = jax.vjp(scaled, actor, critic, has_aux=True)
    part_actor, part_critic = pull(jnp.float32(1.0))
    grad_actor, grad_critic, total = lax.psum(
        (part_actor, part_critic, extra[0]), ("group", "shard")
    )
    delta = extra[1]
    priority_here = (valid * jnp.sqrt(delta * delta + 1.0)).reshape(peers, CAP)
    priority = lax.all_to_all(
        priority_here, ("group", "shard"), split_axis=0, concat_axis=0, tiled=True
    )
    actor_out = update(actor, grad_actor, actor_momentum, actor_average, actor_target)
    critic_out = update(critic, grad_critic, critic_momentum, critic_average, critic_target)
    loss_parts = jnp.stack([total, count])
    return (
        loss_parts,
        priority.reshape(1, peers, CAP),
        actor_out[0],
        critic_out[0],
        actor_out[1],
        critic_out[1],
        actor_out[2],
        critic_out[2],
        actor_out[3],
        critic_out[3],
        actor_out[4],
        critic_out[4],
    )


def solution(mesh):
    in_specs = (
        P(("group", "shard"), None),
        P(("group", "shard"), None, None),
        P(("group", "shard"), None),
        P(("group", "shard"), None, None, None),
        P(),
        P(),
        P(),
        P(),
        P(),
        P(),
        P(),
        P(),
    )
    out_specs = (
        P(),
        P(("group", "shard"), None, None),
        P(),
        P(),
        P(),
        P(),
        P(),
        P(),
        P(),
        P(),
        P(),
        P(),
    )
    return jax.shard_map(local, mesh=mesh, in_specs=in_specs, out_specs=out_specs, check_vma=False)
```

profile of v0, /device:TPU:1, one launch (start us, length us, event | category | flops | bytes accessed | tf_op | source)
XLA Modules:
  0.0 527.9 jit_solution(12048224809431595212)
XLA Ops:
  8.6 11.5 %all-to-all-start = ((s32[128,1,1]{2,1,0:T(1,128)}), s32[128,1,1]{2,1,0:T(1,128)S(1)}, u32[]{:S(2)}, u32[]{:S(2)}) async-start(s32[128,1,1]{2,1,0:T(1,128)} %copy.48), calls=%async_computation | async-start | bytes 131072 | tf_op jit(solution)/shard_map/all_to_all | solution.py:90
  21.7 5.4 %slice_reduce_fusion = (f32[65536]{0:T(1024)}, f32[65536]{0:T(1024)}, f32[65536]{0:T(1024)}, f32[65536]{0:T(1024)}) fusion(f32[2,72193]{1,0:T(2,128)} %param.17, f32[2,72193]{1,0:T(2,128)} %param.23), kind=kLoop, calls=%fused_computation.145 | loop fusion | bytes 2097152 | tf_op jit(solution)/shard_map/jvp()/slice | solution.py:31
  37.6 13.0 %gather_fusion = f32[4096,42]{1,0:T(8,128)S(1)} fusion(f32[8192,42]{1,0:T(8,128)} %copy.50, s32[4096]{0:T(1024)S(1)} %broadcast_clamp_fusion), kind=kCustom, calls=%fused_computation | custom fusion | bytes 1392640 | tf_op jit(solution)/shard_map/gather | solution.py:86
  54.5 9.8 %all-to-all-start.1 = ((f32[128,1,1344]{2,1,0:T(1,128)}), f32[128,1,1344]{2,1,0:T(1,128)S(1)}, u32[]{:S(2)}, u32[]{:S(2)}) async-start(f32[128,1,1344]{2,1,0:T(1,128)} %reshape.586), calls=%async_computation.1 | async-start | bytes 1441792 | tf_op jit(solution)/shard_map/all_to_all | solution.py:89
  162.2 5.1 fusion.32
  175.3 5.1 fusion.43
  196.3 67.2 %all-reduce.20 = (f32[]{:T(128)}, f32[1]{0:T(128)}) all-reduce(f32[]{:T(128)} %convert_reduce_fusion, f32[1]{0:T(128)} %bitcast.32), channel_id=1, replica_groups=mesh['group'=16,'shard'=8] {'group','shard'}, use_global_device_ids=true, to_apply=%region_3.4 | all-reduce | flops 2 | bytes 16 | tf_op jit(solution)/shard_map/psum | solution.py:103
  264.5 6.8 %fusion.4 = f32[4096,256]{1,0:T(8,128)S(1)} fusion(f32[256,256]{1,0:T(8,128)S(1)} %copy-done.27, f32[4096,256]{1,0:T(8,128)} %copy-done.64, f32[256]{0:T(256)S(1)} %bitcast.132, f32[4096]{0:T(1024)S(1)} %neg.72), kind=kOutput, calls=%fused_computation.36 | convolution fusion | flops 3231711232 | bytes 8668160 | tf_op jit(solution)/shard_map/transpose(jvp())/dot_general | solution.py:15
  271.3 5.1 fusion.169
  276.5 4.7 fusion.168
  281.2 6.3 %fusion.159 = (f32[256]{0:T(256)S(1)}, f32[4096,256]{1,0:T(8,128)}) fusion(f32[4096,256]{1,0:T(8,128)S(1)} %copy-done.8, f32[4096,256]{1,0:T(8,128)S(1)} %get-tuple-element.132, f32[256,256]{1,0:T(8,128)S(1)} %copy-done.31), kind=kOutput, calls=%fused_computation.224 | convolution fusion | flops 3231710976 | bytes 12846080 | tf_op jit(solution)/shard_map/transpose(jvp())/dot_general | solution.py:15
  287.6 7.9 %convolution_bitcast_fusion.2 = f32[32,2,8,128]{3,2,1,0:T(8,128)} fusion(f32[4096,256]{1,0:T(8,128)S(1)} %get-tuple-element.132, f32[4096,256]{1,0:T(8,128)S(1)} %copy-done.8), kind=kOutput, calls=%fused_computation.123 | convolution fusion | flops 3225419776 | bytes 8650752 | tf_op jit(solution)/shard_map/transpose(jvp())/dot_general | solution.py:15
  295.5 7.1 %fusion.90 = f32[256,6]{1,0:T(8,128)S(1)} fusion(f32[4096,6]{0,1:T(8,128)S(1)} %get-tuple-element.134, f32[4096,256]{1,0:T(8,128)S(1)} %copy-done.63), kind=kOutput, calls=%fused_computation.124 | convolution fusion | flops 79691776 | bytes 4298752 | tf_op jit(solution)/shard_map/transpose(jvp())/dot_general | solution.py:15
  305.0 6.0 %fusion.157 = (f32[256]{0:T(256)S(1)}, f32[4096,256]{1,0:T(8,128)}) fusion(f32[4096,256]{1,0:T(8,128)S(1)} %copy-done.6, f32[4096,256]{1,0:T(8,128)S(1)} %get-tuple-element.87, f32[256,256]{1,0:T(8,128)S(1)} %copy-done.27), kind=kOutput, calls=%fused_computation.223 | convolution fusion | flops 3231710976 | bytes 12846080 | tf_op jit(solution)/shard_map/transpose(jvp())/dot_general | solution.py:15
  311.0 7.9 %convolution_bitcast_fusion = f32[32,2,8,128]{3,2,1,0:T(8,128)} fusion(f32[4096,256]{1,0:T(8,128)S(1)} %get-tuple-element.87, f32[4096,256]{1,0:T(8,128)S(1)} %copy-done.6), kind=kOutput, calls=%fused_computation.121 | convolution fusion | flops 3225419776 | bytes 8650752 | tf_op jit(solution)/shard_map/transpose(jvp())/dot_general | solution.py:15
  321.3 6.3 %fusion.152 = (f32[256]{0:T(256)S(1)}, f32[4096,256]{1,0:T(8,128)}) fusion(f32[4096,256]{1,0:T(8,128)S(1)} %copy-done.12, f32[4096,256]{1,0:T(8,128)S(1)} %get-tuple-element.81, f32[256,256]{1,0:T(8,128)S(1)} %copy-done.29), kind=kOutput, calls=%fused_computation.220 | convolution fusion | flops 3231710976 | bytes 12846080 | tf_op jit(solution)/shard_map/transpose(jvp())/dot_general | solution.py:15
  327.6 7.9 %convolution_bitcast_fusion.1 = f32[32,2,8,128]{3,2,1,0:T(8,128)} fusion(f32[4096,256]{1,0:T(8,128)S(1)} %get-tuple-element.81, f32[4096,256]{1,0:T(8,128)S(1)} %copy-done.12), kind=kOutput, calls=%fused_computation.122 | convolution fusion | flops 3225419776 | bytes 8650752 | tf_op jit(solution)/shard_map/transpose(jvp())/dot_general | solution.py:15
  335.6 5.7 %fusion.144 = f32[17,256]{1,0:T(8,128)S(1)} fusion(f32[4096,256]{1,0:T(8,128)} %get-tuple-element.91, f32[4096,42]{1,0:T(8,128)S(1)} %bitcast.111), kind=kOutput, calls=%fused_computation.213 | convolution fusion | flops 213909504 | bytes 4899840 | tf_op jit(solution)/shard_map/transpose(jvp())/dot_general | solution.py:15
  342.4 5.9 %fusion.82 = f32[23,256]{1,0:T(8,128)S(1)} fusion(f32[4096,256]{1,0:T(8,128)} %get-tuple-element.89, f32[4096,42]{1,0:T(8,128)S(1)} %bitcast.112), kind=kOutput, calls=%fused_computation.119 | convolution fusion | flops 289406976 | bytes 4905984 | tf_op jit(solution)/shard_map/transpose(jvp())/dot_general | solution.py:15
  350.1 4.8 fusion.93
  360.6 4.7 fusion.97
  369.5 4.7 all-to-all-start.2
  376.2 7.7 %all-to-all-done.2 = f32[128,1,32]{2,1,0:T(1,128)S(1)} async-done(((f32[128,1,32]{2,1,0:T(1,128)}), f32[128,1,32]{2,1,0:T(1,128)S(1)}, u32[]{:S(2)}, u32[]{:S(2)}) %all-to-all-start.2) | async-done | bytes 16416 | tf_op jit(solution)/shard_map/all_to_all | solution.py:116
  384.5 127.5 %all-reduce.24.cloned.1.call-done = (f32[71942]{0:T(1024)}, f32[2,72193]{1,0:T(2,128)}) async-done(((f32[71942]{0:T(1024)}, f32[2,72193]{1,0:T(2,128)}), (f32[71942]{0:T(1024)}, f32[2,72193]{1,0:T(2,128)})) %all-reduce.24.cloned.1.call-update) | async-done | bytes 865328 | tf_op jit(solution)/shard_map/psum | solution.py:111
  (242 shorter events, 167.6 us)
Async XLA Ops:
  8.6 45.9 %all-to-all-start = ((s32[128,1,1]{2,1,0:T(1,128)}), s32[128,1,1]{2,1,0:T(1,128)S(1)}, u32[]{:S(2)}, u32[]{:S(2)}) async-start(s32[128,1,1]{2,1,0:T(1,128)} %copy.48), calls=%async_computation | async-start | bytes 131072 | tf_op jit(solution)/shard_map/all_to_all | solution.py:90
  50.6 14.0 %copy-start.13 = (f32[2,72193]{1,0:T(2,128)S(1)}, f32[2,72193]{1,0:T(2,128)}, u32[]{:S(2)}) copy-start(f32[2,72193]{1,0:T(2,128)} %param.17) | copy-start | bytes 1732636
  50.6 14.6 %copy-start.16 = (f32[71942]{0:T(1024)S(1)}, f32[71942]{0:T(1024)}, u32[]{:S(2)}) copy-start(f32[71942]{0:T(1024)} %param.16) | copy-start | bytes 863308
  50.6 15.1 %copy-start.18 = (f32[71942]{0:T(1024)S(1)}, f32[71942]{0:T(1024)}, u32[]{:S(2)}) copy-start(f32[71942]{0:T(1024)} %param.22) | copy-start | bytes 863308
  50.6 19.0 %slice-start = ((f32[71942]{0:T(1024)}), f32[4352]{0:T(1024)S(1)}, s32[]{:S(2)}) async-start(f32[71942]{0:T(1024)} %param.16), calls=%async_computation.4 | async-start | bytes 40960 | tf_op jit(solution)/shard_map/jvp()/slice | solution.py:31
  50.6 24.6 %slice-start.1 = ((f32[71942]{0:T(1024)}), f32[4352]{0:T(1024)S(1)}, s32[]{:S(2)}) async-start(f32[71942]{0:T(1024)} %param.22), calls=%async_computation.5 | async-start | bytes 40960 | tf_op jit(solution)/shard_map/slice | solution.py:31
  54.5 20.7 %copy-start.23 = (f32[65536]{0:T(1024)S(1)}, f32[65536]{0:T(1024)}, u32[]{:S(2)}) copy-start(f32[65536]{0:T(1024)} %get-tuple-element.136) | copy-start | bytes 786436
  54.5 21.5 %copy-start.44 = (f32[5888]{0:T(1024)S(1)}, f32[5888]{0:T(1024)}, u32[]{:S(2)}) copy-start(f32[5888]{0:T(1024)} %get-tuple-element.60) | copy-start | bytes 70660
  54.5 22.1 %copy-start.22 = (f32[65536]{0:T(1024)S(1)}, f32[65536]{0:T(1024)}, u32[]{:S(2)}) copy-start(f32[65536]{0:T(1024)} %get-tuple-element.66) | copy-start | bytes 786436
  54.5 22.9 %copy-start.43 = (f32[5888]{0:T(1024)S(1)}, f32[5888]{0:T(1024)}, u32[]{:S(2)}) copy-start(f32[5888]{0:T(1024)} %get-tuple-element.64) | copy-start | bytes 70660
  54.5 28.1 %all-to-all-start.1 = ((f32[128,1,1344]{2,1,0:T(1,128)}), f32[128,1,1344]{2,1,0:T(1,128)S(1)}, u32[]{:S(2)}, u32[]{:S(2)}) async-start(f32[128,1,1344]{2,1,0:T(1,128)} %reshape.586), calls=%async_computation.1 | async-start | bytes 1441792 | tf_op jit(solution)/shard_map/all_to_all | solution.py:89
  64.3 447.7 %all-reduce.24.cloned.1.call-start = ((), (), s32[]{:S(2)}) async-start(), calls=%async_computation.3 | async-start | bytes 1738752 | tf_op jit(solution)/shard_map/psum | solution.py:111
  104.4 21.2 %copy-start.5 = (f32[4096,256]{1,0:T(8,128)}, f32[4096,256]{1,0:T(8,128)S(1)}, u32[]{:S(2)}) copy-start(f32[4096,256]{1,0:T(8,128)S(1)} %convolution_add_fusion.13) | copy-start | bytes 12582916
  188.6 75.6 %copy-start.49 = (s32[128]{0:T(128)S(1)}, s32[128]{0:T(128)}, u32[]{:S(2)}) copy-start(s32[128]{0:T(128)} %copy-done.48) | copy-start | bytes 1540
  188.6 75.8 %copy-start.27 = (f32[256,256]{1,0:T(8,128)S(1)}, f32[256,256]{1,0:T(8,128)}, u32[]{:S(2)}) copy-start(f32[256,256]{1,0:T(8,128)} %reshape.501) | copy-start | bytes 786436
  188.6 75.8 %copy-start.51 = (f32[1,256]{1,0:T(1,128)S(1)}, f32[1,256]{1,0:T(1,128)}, u32[]{:S(2)}) copy-start(f32[1,256]{1,0:T(1,128)} %get-tuple-element.107) | copy-start | bytes 3076
  311.0 7.9 %copy-start.50 = (f32[1,256]{1,0:T(1,128)S(1)}, f32[1,256]{1,0:T(1,128)}, u32[]{:S(2)}) copy-start(f32[1,256]{1,0:T(1,128)} %get-tuple-element.104) | copy-start | bytes 3076
  360.6 8.1 %copy-start.47 = (f32[4096]{0:T(1024)S(1)}, f32[4096]{0:T(1024)}, u32[]{:S(2)}) copy-start(f32[4096]{0:T(1024)} %get-tuple-element.97) | copy-start | bytes 49156
  365.3 146.7 %copy-start.17 = (f32[71942]{0:T(1024)S(1)}, f32[71942]{0:T(1024)}, u32[]{:S(2)}) copy-start(f32[71942]{0:T(1024)} %param.16) | copy-start | bytes 863308
  365.3 148.6 %copy-start.24 = (f32[2,72193]{1,0:T(2,128)S(1)}, f32[2,72193]{1,0:T(2,128)}, u32[]{:S(2)}) copy-start(f32[2,72193]{1,0:T(2,128)} %param.19) | copy-start | bytes 1732636
  366.3 150.6 %copy-start.19 = (f32[71942]{0:T(1024)S(1)}, f32[71942]{0:T(1024)}, u32[]{:S(2)}) copy-start(f32[71942]{0:T(1024)} %param.22) | copy-start | bytes 863308
  367.7 149.2 %copy-start.25 = (f32[71942]{0:T(1024)S(1)}, f32[71942]{0:T(1024)}, u32[]{:S(2)}) copy-start(f32[71942]{0:T(1024)} %param.20) | copy-start | bytes 863308
  367.7 150.1 %copy-start.15 = (f32[2,72193]{1,0:T(2,128)S(1)}, f32[2,72193]{1,0:T(2,128)}, u32[]{:S(2)}) copy-start(f32[2,72193]{1,0:T(2,128)} %param.23) | copy-start | bytes 1732636
  369.5 14.3 %all-to-all-start.2 = ((f32[128,1,32]{2,1,0:T(1,128)}), f32[128,1,32]{2,1,0:T(1,128)S(1)}, u32[]{:S(2)}, u32[]{:S(2)}) async-start(f32[128,1,32]{2,1,0:T(1,128)} %bitcast.34), calls=%async_computation.2 | async-start | bytes 131072 | tf_op jit(solution)/shard_map/all_to_all | solution.py:116
  (47 other events, 225.2 us)
Sparse Core Ops, SparseCore 0:
  368.6 143.3 all-reduce.23
where the time goes:
time: 536 us; the launch traced here: 528 us
  matrix products  180 us (34%)
  waiting for transfers between devices  135 us (25%)
  local copies, waits for them, and re-layouts  72.7 us (14%)
  blocking collectives  67.2 us (13%)
  other arithmetic  30.9 us (6%)
  starting transfers between devices  26.2 us (5%)
  between operations  16.1 us (3%)
    dot_general x36, matrix products, matmul(): return jnp.dot(a, b, precision=lax.Precision.HIGHEST)  180 us
    psum x1, waiting for transfers between devices, local(): lax.psum((part_actor, part_critic, extra[0]), ('group', 'shard'))  128 us
    psum x1, blocking collectives, local(): count = lax.psum(local_count, ('group', 'shard'))  67.2 us
    unnamed x143, local copies, waits for them, and re-layouts  29.8 us
    slice x19, local copies, waits for them, and re-layouts, unpack(): pieces.append(flat[start:start + number].reshape(shape))  15.7 us
    gather x1, local copies, waits for them, and re-layouts, local(): outgoing = replay[sample_index[0]]  13 us
    all_to_all x1, starting transfers between devices, local(): lax.all_to_all(count_col, ('group', 'shard'), split_axis=0, concat_axis=0...  11.5 us
  transfers between devices with their start and end apart: 4, of which 2 were waited for; matrix products, arithmetic and copies ran while one was open for 11% of the time, Pallas kernels for 0%

commit v1 on v0

v1 whole, which is shorter than its diff:
```python
import functools

import jax
import jax.numpy as jnp
from jax import lax
from jax.experimental import pallas as pl
from jax.experimental.pallas import tpu as pltpu
from jax.sharding import PartitionSpec as P

OBS = 17
ACT = 6
UNITS = 256
CAP = 32
DEVS = 128
R_DEV = 8192
ROW = 42
PA = 71942
PC = 72193
N = DEVS * CAP

bf = jnp.bfloat16
f32 = jnp.float32
MESH = pl.DeviceIdType.MESH
VM = pl.BlockSpec(memory_space=pltpu.VMEM)
SM = pl.BlockSpec(memory_space=pltpu.SMEM)
SDS = jax.ShapeDtypeStruct

SCALE = 2.0**-19
C0, C1, A, AT, T0, T1 = range(6)
FEAT = 48
ONE = 42
NEXT = 25

ROWS_A = 568
STAT = 564
TILES_C = 565
PACK = 1728
HALF = PACK // 2
CHUNK = 16
OWNERS = HALF // CHUNK
CHIPS = DEVS // 2


def dot(a, b):
    return lax.dot_general(a, b, (((1,), (0,)), ((), ())), preferred_element_type=f32)


def dot_nt(a, b):
    return lax.dot_general(a, b, (((1,), (1,)), ((), ())), preferred_element_type=f32)


def dot_exact(a, b, dims):
    return lax.dot_general(a, b, (dims, ((), ())), precision=lax.Precision.HIGHEST, preferred_element_type=f32)


def split(v):
    hi = v.astype(bf)
    return hi, (v - hi.astype(f32)).astype(bf)


def three(v):
    hi, lo = split(v)
    return jnp.concatenate([hi, lo, hi], 0)


def lanes(tile, width):
    return jnp.concatenate([tile] * (width // 128), 1)


def fold(v):
    out = v[:, :128]
    for i in range(1, v.shape[1] // 128):
        out = out + v[:, 128 * i : 128 * (i + 1)]
    return out


def column(row):
    return jnp.transpose(jnp.broadcast_to(row, (128, 128)))


def exchange_start(me, group_size, shard_size, noise_ref, q_ref, nsend, nrecv, send_sem, recv_sem):
    q_ref[...] = jnp.zeros_like(q_ref)
    for j in range(ACT):
        q_ref[pl.ds(j + 1, CAP, stride=8), :] = 0.5 * jnp.tanh(0.4 * noise_ref[j])
    turned = jnp.transpose(q_ref[...])
    nsend[:, 0, :] = turned[:, :128]
    nsend[:, 1, :] = turned[:, 128:]
    nrecv[pl.ds(me, 1)] = nsend[pl.ds(me, 1)]

    def send(k, carry):
        peer = lax.rem(me + k, DEVS)
        pltpu.make_async_remote_copy(
            src_ref=nsend.at[peer],
            dst_ref=nrecv.at[me],
            send_sem=send_sem,
            recv_sem=recv_sem,
            device_id=(peer // shard_size, lax.rem(peer, shard_size)),
            device_id_type=MESH,
        ).start()
        return carry

    lax.fori_loop(1, DEVS, send, 0)


def exchange_wait(nsend, nrecv, send_sem, recv_sem, nz_ref):
    pltpu.make_async_copy(nsend.at[pl.ds(0, DEVS - 1)], nsend.at[pl.ds(0, DEVS - 1)], send_sem).wait()
    pltpu.make_async_copy(nrecv.at[pl.ds(0, DEVS - 1)], nrecv.at[pl.ds(0, DEVS - 1)], recv_sem).wait()
    back = jnp.transpose(jnp.concatenate([nrecv[:, 0, :], nrecv[:, 1, :]], 1))
    for c in range(CAP):
        nz_ref[:, 128 * c : 128 * (c + 1)] = back[8 * c : 8 * (c + 1), :]


def turn_table(table_ref, rows_ref):
    width = 512

    def body(i, carry):
        s = pl.ds(pl.multiple_of(i * width, width), width)
        v = jnp.concatenate([table_ref[:, s], jnp.zeros((128 - ROW, width), f32)], 0)
        rows_ref[s, :] = jnp.transpose(v)
        return carry

    lax.fori_loop(0, R_DEV // width, body, 0)


def pick_rows(index_ref, rows_ref, picked_ref, x_ref):
    ones = lax.broadcasted_iota(jnp.int32, (8, 128), 0) == (ONE - 40)

    def body(c, carry):
        for d in range(DEVS):
            picked_ref[d : d + 1, :] = rows_ref[pl.ds(index_ref[c, d], 1), :]
        turned = jnp.transpose(picked_ref[...])
        s = pl.ds(pl.multiple_of(c * 128, 128), 128)
        x_ref[0:40, s] = turned[0:40]
        x_ref[40:48, s] = jnp.where(ones, 1.0, turned[40:48])
        return carry

    lax.fori_loop(0, CAP, body, 0)


def gather_kernel(
    group_size, shard_size, table_ref, index_ref, noise_ref, x_ref, nz_ref, rows_ref, picked_ref, q_ref, nsend, nrecv, send_sem, recv_sem
):
    me = lax.axis_index("group") * shard_size + lax.axis_index("shard")
    barrier = pltpu.get_barrier_semaphore()

    def greet(k, carry):
        peer = lax.rem(me + k, DEVS)
        pl.semaphore_signal(
            barrier, inc=1, device_id=(peer // shard_size, lax.rem(peer, shard_size)), device_id_type=MESH
        )
        return carry

    lax.fori_loop(1, DEVS, greet, 0)
    turn_table(table_ref, rows_ref)
    pl.semaphore_wait(barrier, DEVS - 1)
    exchange_start(me, group_size, shard_size, noise_ref, q_ref, nsend, nrecv, send_sem, recv_sem)
    pick_rows(index_ref, rows_ref, picked_ref, x_ref)
    exchange_wait(nsend, nrecv, send_sem, recv_sem, nz_ref)


def put_square(net, w2, w2f_ref, w2b_ref):
    w2 = 0.5 * w2
    turned = jnp.transpose(w2)
    hi, lo = split(turned)
    w2f_ref[net] = jnp.concatenate([hi, hi, lo], 1)
    if net in (C0, C1, A):
        hi, lo = split(w2)
        w2b_ref[net] = jnp.concatenate([hi, hi, lo], 1)


def put_first(net, pad_ref, w1_ref):
    w1 = 0.5 * pad_ref[...]
    hi = w1.astype(bf).astype(f32)
    lo = w1 - hi
    stacked = jnp.concatenate([hi, hi, lo, jnp.zeros((256 - 3 * FEAT, 256), f32)], 0)
    w1_ref[net] = jnp.transpose(stacked).astype(bf)


def put_column(ref, net, left, right, factor):
    ref[net] = jnp.concatenate([column(left * factor), column(right * factor)], 0)


def prepare_critics(critic_ref, rows_ref, pad_ref, first, w1_ref, w2f_ref, w2b_ref, b2_ref, w3_ref, b3_ref, w1a_ref):
    for t in range(TILES_C - 1):
        rows_ref[2 * t : 2 * t + 2, :] = critic_ref[:, 128 * t : 128 * (t + 1)]
    for c in range(2):
        net = first + c
        start = NEXT if first == T0 else 0
        pad_ref[...] = jnp.zeros_like(pad_ref)
        for half in range(2):
            s = pl.ds(128 * half, 128)
            pad_ref[pl.ds(start, OBS), s] = rows_ref[pl.ds(c + 2 * half, OBS, stride=4), :]
            pad_ref[pl.ds(OBS, ACT), s] = rows_ref[pl.ds(c + 2 * half + 4 * OBS, ACT, stride=4), :]
            pad_ref[pl.ds(ONE, 1), s] = rows_ref[pl.ds(92 + c + 2 * half, 1), :]
        put_first(net, pad_ref, w1_ref)
        if net == C0:
            hi = pad_ref[16:24, :].astype(bf).astype(f32)
            lo = pad_ref[16:24, :] - hi
            block = jnp.concatenate([hi, hi, lo], 1)
            w1a_ref[...] = jnp.concatenate([block, jnp.zeros_like(block)], 0).astype(bf)
        w2 = jnp.concatenate(
            [rows_ref[pl.ds(96 + c, UNITS, stride=4), :], rows_ref[pl.ds(98 + c, UNITS, stride=4), :]], 1
        )
        put_square(net, w2, w2f_ref, w2b_ref)
        put_column(b2_ref, net, rows_ref[1120 + c : 1121 + c, :], rows_ref[1122 + c : 1123 + c, :], 0.5)
        put_column(w3_ref, net, rows_ref[1124 + c : 1125 + c, :], rows_ref[1126 + c : 1127 + c, :], 1.0)
        b3_ref[net] = jnp.broadcast_to(critic_ref[c : c + 1, PC - 1 : PC], (1, 128))


def head_maps(j):
    k = lax.broadcasted_iota(jnp.int32, (UNITS, 16), 0)
    r = lax.broadcasted_iota(jnp.int32, (UNITS, 16), 1)
    row = ((k * ACT + j) // 128) == r
    k = lax.broadcasted_iota(jnp.int32, (UNITS, 128), 0)
    l = lax.broadcasted_iota(jnp.int32, (UNITS, 128), 1)
    lane = ((k * ACT + j) % 128) == l
    return row.astype(f32), lane


def head_of(flat):
    hi = flat.astype(bf).astype(f32)
    out = []
    for part in (hi, flat - hi):
        part = part.astype(bf)
        spread = []
        for j in range(ACT):
            row, lane = head_maps(j)
            spread.append(jnp.where(lane, dot(row.astype(bf), part), 0.0).astype(bf))
        r = lax.broadcasted_iota(jnp.int32, (16, 128 * ACT), 0)
        l = lax.broadcasted_iota(jnp.int32, (16, 128 * ACT), 1)
        take = ((l // 128) == (r - 1)).astype(f32).astype(bf)
        out.append(dot_nt(take, jnp.concatenate(spread, 1))[:8])
    return out


def head_back(turned):
    out = jnp.zeros((16, 128), f32)
    for j in range(ACT):
        row, lane = head_maps(j)
        picked = jnp.transpose(row) * turned[j + 1 : j + 2, :]
        out = out + dot_exact(picked, lane.astype(f32), ((1,), (0,)))
    return out


def prepare_actor(net, rows_ref, pad_ref, w1_ref, w2f_ref, w2b_ref, b2_ref, w3t_ref, w3b_ref, b3a_ref):
    start = NEXT if net == AT else 0
    pad_ref[...] = jnp.zeros_like(pad_ref)
    for half in range(2):
        s = pl.ds(128 * half, 128)
        pad_ref[pl.ds(start, OBS), s] = rows_ref[pl.ds(half, OBS, stride=2), :]
        pad_ref[pl.ds(ONE, 1), s] = rows_ref[pl.ds(34 + half, 1), :]
    put_first(net, pad_ref, w1_ref)
    w2 = jnp.concatenate([rows_ref[pl.ds(36, UNITS, stride=2), :], rows_ref[pl.ds(37, UNITS, stride=2), :]], 1)
    put_square(net, w2, w2f_ref, w2b_ref)
    put_column(b2_ref, net, rows_ref[548:549, :], rows_ref[549:550, :], 0.5)
    flat = jnp.concatenate([rows_ref[550:562, :], jnp.zeros((4, 128), f32)], 0)
    hi, lo = head_of(flat)
    block = jnp.concatenate([hi, hi, lo], 1)
    w3t_ref[net - A] = jnp.concatenate([block, jnp.zeros_like(block)], 0).astype(bf)
    if net == A:
        stacked = jnp.concatenate([hi, hi, lo, jnp.zeros((104, UNITS), f32)], 0)
        w3b_ref[...] = (0.5 * jnp.transpose(stacked)).astype(bf)
    bias = column(rows_ref[562:563, :])
    b3a_ref[net - A] = jnp.zeros((8, 128), f32)
    b3a_ref[net - A, 1 : 1 + ACT, :] = bias[:ACT]


def act(zh):
    u = jnp.tanh(zh) + 1.0
    return u, zh * u


def slope(u, s):
    return u + s * (2.0 - u)


def train_rows(
    width,
    x_ref,
    nz_ref,
    count_ref,
    w1_ref,
    w2f_ref,
    w2b_ref,
    b2_ref,
    w3_ref,
    b3_ref,
    w3t_ref,
    w3b_ref,
    b3a_ref,
    w1a_ref,
    prio_ref,
    g2_ref,
    g1_ref,
    g3a_ref,
    db2_ref,
    dw3_ref,
    st_ref,
):
    for ref in (g2_ref, g1_ref, g3a_ref, db2_ref, dw3_ref, st_ref):
        ref[...] = jnp.zeros_like(ref)
    rows8 = lax.broadcasted_iota(jnp.int32, (8, width), 0)
    is_action = (rows8 >= 1) & (rows8 <= ACT)

    def body(i, carry):
        s_ = pl.ds(pl.multiple_of(i * width, width), width)
        x = x_ref[:, s_]
        x3 = three(x)
        xhi, xlo = x3[:FEAT], x3[FEAT : 2 * FEAT]
        x_left = jnp.concatenate(
            [jnp.concatenate([xhi, xlo], 0), jnp.concatenate([xhi, jnp.zeros_like(xlo)], 0)], 1
        )

        def with_action(a):
            return three(jnp.concatenate([x[:16], jnp.where(is_action, a, x[16:24]), x[24:]], 0))

        def first(net, xx):
            return act(dot(w1_ref[net, :, : 3 * FEAT], xx))

        def second(net, h3):
            return act(dot(w2f_ref[net], h3) + lanes(b2_ref[net], width))

        def value(net, s):
            return jnp.sum(s * lanes(w3_ref[net], width), 0, keepdims=True) + lanes(b3_ref[net], width)

        def head(net, s3):
            return dot(w3t_ref[net - A], s3)[:8] + lanes(b3a_ref[net - A], width)

        u, s = first(AT, x3)
        u, s = second(AT, three(s))
        next_action = jnp.tanh(head(AT, three(s)) + nz_ref[:, s_])

        u, s = first(A, x3)
        h1a, d1a = three(s), slope(u, s)
        u, s = second(A, h1a)
        h2a, d2a = three(s), slope(u, s)
        policy = jnp.tanh(head(A, h2a))

        kept = []
        for net in (C0, C1):
            u, s = first(net, x3)
            h1, d1 = three(s), slope(u, s)
            u, s = second(net, h1)
            kept.append((h1, d1, s, slope(u, s), value(net, s)))

        xt = with_action(next_action)
        targets = []
        for net in (T0, T1):
            u, s = first(net, xt)
            u, s = second(net, three(s))
            targets.append(value(net, s))

        u, s = first(C0, with_action(policy))
        d1f = slope(u, s)
        u, s = second(C0, three(s))
        d2f, q_policy = slope(u, s), value(C0, s)

        y = x[23:24] + 0.99 * x[24:25] * jnp.minimum(targets[0], targets[1])
        tiles = width // 128
        valid = jnp.concatenate([((i * tiles + t) < count_ref[...]).astype(f32) for t in range(tiles)], 1)
        delta = [k[4] - y for k in kept]
        prio_ref[:, s_] = valid * jnp.sqrt(delta[0] * delta[0] + 1.0)
        st_ref[0:1, :] += fold(valid * (delta[0] * delta[0] + delta[1] * delta[1] - q_policy))
        st_ref[1:2, :] += fold(valid)
        scaled = valid * SCALE

        def back(net, dz2):
            hi, lo = split(dz2)
            return hi, lo, dot(w2b_ref[net], jnp.concatenate([hi, lo, hi], 0))

        def weight_grads(net, h1, hi, lo, dz1):
            left = jnp.concatenate([h1[:UNITS], h1[UNITS : 2 * UNITS], h1[:UNITS]], 1)
            g2_ref[net] += dot_nt(left, jnp.concatenate([hi, hi, lo], 1))
            a, b = split(dz1)
            g1_ref[net] += dot_nt(x_left, jnp.concatenate([a, b], 1))

        for net in (C0, C1):
            h1, d1, s2, d2, _ = kept[net]
            dq = (2.0 * scaled) * delta[net]
            st_ref[2 + net : 3 + net, :] += fold(dq)
            dw3_ref[net] += fold(s2 * dq)
            dz2 = lanes(w3_ref[net], width) * (0.5 * dq) * d2
            db2_ref[net] += fold(dz2)
            hi, lo, dh1 = back(net, dz2)
            weight_grads(net, h1, hi, lo, dh1 * d1)

        dz2 = lanes(w3_ref[C0], width) * (-0.5 * scaled) * d2f
        hi, lo, dh1 = back(C0, dz2)
        da = dot(w1a_ref[...], three(dh1 * d1f))[:8]
        dp = jnp.where(is_action, da * (1.0 - policy * policy), 0.0)
        st_ref[8:16, :] += fold(dp)
        hi = dp.astype(bf).astype(f32)
        lo = dp - hi
        zero = jnp.zeros_like(hi)
        stacked = jnp.concatenate([hi, lo, hi, zero], 0).astype(bf)
        left = jnp.concatenate(
            [jnp.concatenate([hi, lo], 0), jnp.concatenate([hi, zero], 0)], 1
        ).astype(bf)
        g3a_ref[...] += dot_nt(left, jnp.concatenate([h2a[:UNITS], h2a[UNITS : 2 * UNITS]], 1))
        dz2 = dot(w3b_ref[:, :32], stacked) * d2a
        db2_ref[A] += fold(dz2)
        hi, lo, dh1 = back(A, dz2)
        weight_grads(A, h1a, hi, lo, dh1 * d1a)
        return carry

    lax.fori_loop(0, N // width, body, 0)


def lane_sums(tile):
    return dot_exact(jnp.ones((8, 128), f32), tile, ((1,), (1,)))


def pack_grads(pack_ref, g2_ref, g1_ref, g3a_ref, db2_ref, dw3_ref, st_ref):
    lane = lax.broadcasted_iota(jnp.int32, (1, 128), 1)
    sums = jnp.sum(st_ref[...], 1, keepdims=True)

    g1 = g1_ref[A, :FEAT, :] + g1_ref[A, FEAT:, :]
    b2 = lane_sums(db2_ref[A])[0:1]
    for half in range(2):
        s = slice(128 * half, 128 * (half + 1))
        pack_ref[pl.ds(half, OBS, stride=2), :] = g1[:OBS, s]
        pack_ref[34 + half : 35 + half, :] = g1[ONE : ONE + 1, s]
        pack_ref[pl.ds(36 + half, UNITS, stride=2), :] = g2_ref[A, :, s]
        pack_ref[548 + half : 549 + half, :] = b2[:, s]
    pack_ref[550:562, :] = head_back(g3a_ref[:8, :] + g3a_ref[8:, :])[:12]
    e = lax.broadcasted_iota(jnp.int32, (8, 128), 1) == lax.broadcasted_iota(jnp.int32, (8, 128), 0) - 1
    pack_ref[562:563, :] = jnp.sum(jnp.where(e, sums[8:16], 0.0), 0, keepdims=True)
    pack_ref[563:ROWS_A, :] = jnp.zeros((ROWS_A - 563, 128), f32)
    pack_ref[STAT : STAT + 1, :] = jnp.where(lane == 0, sums[0:1], jnp.where(lane == 1, sums[1:2], 0.0))

    for c in range(2):
        base = ROWS_A + c
        g1 = g1_ref[c, :FEAT, :] + g1_ref[c, FEAT:, :]
        b2 = lane_sums(db2_ref[c])[0:1]
        w3 = lane_sums(dw3_ref[c])[0:1]
        for half in range(2):
            s = slice(128 * half, 128 * (half + 1))
            at = base + 2 * half
            pack_ref[pl.ds(at, OBS + ACT, stride=4), :] = g1[: OBS + ACT, s]
            pack_ref[at + 92 : at + 93, :] = g1[ONE : ONE + 1, s]
            pack_ref[pl.ds(at + 96, UNITS, stride=4), :] = g2_ref[c, :, s]
            pack_ref[at + 1120 : at + 1121, :] = b2[:, s]
            pack_ref[at + 1124 : at + 1125, :] = w3[:, s]
        pack_ref[base + 1128 : base + 1129, :] = jnp.where(lane == 0, sums[2 + c : 3 + c], 0.0)
    last = ROWS_A + 2 * TILES_C
    pack_ref[last:PACK, :] = jnp.zeros((PACK - last, 128), f32)


def train_kernel(
    width, x_ref, nz_ref, count_ref, actor_ref, actor_t_ref, critic_ref, critic_t_ref, prio_ref, pack_ref, rows_ref, pad_ref, *scratch
):
    weights, grads = scratch[:10], scratch[10:]
    w1_ref, w2f_ref, w2b_ref, b2_ref, w3_ref, b3_ref, w3t_ref, w3b_ref, b3a_ref, w1a_ref = weights
    for first, ref in ((C0, critic_ref), (T0, critic_t_ref)):
        prepare_critics(
            ref, rows_ref, pad_ref, first, w1_ref, w2f_ref, w2b_ref, b2_ref, w3_ref, b3_ref, w1a_ref
        )
    for net, ref in ((A, actor_ref), (AT, actor_t_ref)):
        prepare_actor(net, ref, pad_ref, w1_ref, w2f_ref, w2b_ref, b2_ref, w3t_ref, w3b_ref, b3a_ref)
    train_rows(width, x_ref, nz_ref, count_ref, *weights, prio_ref, *grads)
    pack_grads(pack_ref, *grads)


WEIGHTS = [
    pltpu.VMEM((6, UNITS, 256), bf),
    pltpu.VMEM((6, UNITS, 3 * UNITS), bf),
    pltpu.VMEM((3, UNITS, 3 * UNITS), bf),
    pltpu.VMEM((6, UNITS, 128), f32),
    pltpu.VMEM((6, UNITS, 128), f32),
    pltpu.VMEM((6, 1, 128), f32),
    pltpu.VMEM((2, 16, 3 * UNITS), bf),
    pltpu.VMEM((UNITS, 128), bf),
    pltpu.VMEM((2, 8, 128), f32),
    pltpu.VMEM((16, 3 * UNITS), bf),
]
GRADS = [
    pltpu.VMEM((3, UNITS, UNITS), f32),
    pltpu.VMEM((3, 2 * FEAT, UNITS), f32),
    pltpu.VMEM((16, UNITS), f32),
    pltpu.VMEM((3, UNITS, 128), f32),
    pltpu.VMEM((2, UNITS, 128), f32),
    pltpu.VMEM((16, 128), f32),
]


def reduce_kernel(shard_size, pack_ref, ga_ref, gc_ref, stat_ref, other, half, parts, mine, gathered, whole, sems):
    group, shard = lax.axis_index("group"), lax.axis_index("shard")
    core = lax.rem(shard, 2)
    per = shard_size // 2
    chip = group * per + shard // 2

    def at(c):
        return (c // per, lax.rem(c, per) * 2 + core)

    sibling = (group, shard + 1 - 2 * core)
    barrier = pltpu.get_barrier_semaphore()
    pl.semaphore_signal(barrier, inc=1, device_id=sibling, device_id_type=MESH)

    def greet(k, carry):
        peer = lax.rem(chip + k, CHIPS)
        pl.semaphore_signal(barrier, inc=1, device_id=at(peer), device_id_type=MESH)
        return carry

    lax.fori_loop(1, CHIPS, greet, 0)
    pl.semaphore_wait(barrier, CHIPS)

    def remote(src, dst, n, to):
        return pltpu.make_async_remote_copy(
            src_ref=src, dst_ref=dst, send_sem=sems.at[2 * n], recv_sem=sems.at[2 * n + 1], device_id=to, device_id_type=MESH
        )

    def drain(ref, n, copies):
        view = ref.at[pl.ds(0, copies)]
        pltpu.make_async_copy(view, view, sems.at[n]).wait()

    keep = pl.multiple_of(core * HALF, HALF)
    give = pl.multiple_of((1 - core) * HALF, HALF)
    swap = remote(pack_ref.at[pl.ds(give, HALF)], other, 0, sibling)
    swap.start()
    swap.wait()
    total = pack_ref[pl.ds(keep, HALF), :] + other[...]
    half[...] = total.reshape(OWNERS, CHUNK, 128)

    def scatter(k, carry):
        peer = lax.rem(chip + k, CHIPS)

        @pl.when(peer < OWNERS)
        def _():
            remote(half.at[peer], parts.at[chip], 1, at(peer)).start()

        return carry

    lax.fori_loop(1, CHIPS, scatter, 0)
    owner = chip < OWNERS

    @pl.when(owner)
    def _():
        drain(half, 2, OWNERS - 1)
        parts[pl.ds(chip, 1)] = half[pl.ds(chip, 1)]
        drain(parts, 3, CHIPS - 1)
        mine[...] = jnp.sum(parts[...], 0)
        gathered[pl.ds(chip, 1)] = mine[...][None]

        def spread(k, carry):
            peer = lax.rem(chip + k, CHIPS)
            remote(mine, gathered.at[chip], 2, at(peer)).start()
            return carry

        lax.fori_loop(1, CHIPS, spread, 0)
        drain(parts, 4, CHIPS - 1)
        drain(gathered, 5, OWNERS - 1)

    @pl.when(jnp.logical_not(owner))
    def _():
        drain(half, 2, OWNERS)
        drain(gathered, 5, OWNERS)

    whole[pl.ds(core, 1)] = gathered[...].reshape(1, HALF, 128)
    back = remote(whole.at[core], whole.at[core], 3, sibling)
    back.start()
    back.wait()

    stat = whole[0, STAT : STAT + 1, :]
    factor = (1.0 / SCALE) / stat[:, 1:2]
    stat_ref[...] = stat
    ga_ref[...] = whole[0, :ROWS_A, :] * factor
    for t in range(TILES_C):
        r = ROWS_A + 2 * t
        h, r = r // HALF, r % HALF
        gc_ref[:, 128 * t : 128 * (t + 1)] = whole[h, r : r + 2, :] * factor


def update(weight, grad, momentum, average, target):
    momentum_new = 0.9 * momentum + grad
    weight_new = weight - 0.1 * (grad + 0.9 * momentum_new)
    average_new = 0.99 * average + 0.01 * weight_new
    target_new = 0.005 * weight_new + 0.995 * target
    return (weight_new, momentum_new, average_new, target_new, weight_new.astype(bf))


def actor_rows(flat):
    return jnp.pad(flat, (0, ROWS_A * 128 - PA)).reshape(ROWS_A, 128)


def local(
    group_size,
    shard_size,
    replay,
    sample_index,
    pair_count,
    noise,
    actor,
    critic,
    actor_momentum,
    critic_momentum,
    actor_average,
    critic_average,
    actor_target,
    critic_target,
):
    table = replay.T
    index = sample_index[0].T
    noise = jnp.transpose(noise[0], (2, 1, 0))
    x, nz = pl.pallas_call(
        functools.partial(gather_kernel, group_size, shard_size),
        out_shape=(SDS((FEAT, N), f32), SDS((8, N), f32)),
        in_specs=[VM, SM, VM],
        out_specs=(VM, VM),
        scratch_shapes=[
            pltpu.VMEM((R_DEV, 128), f32),
            pltpu.VMEM((128, 128), f32),
            pltpu.VMEM((256, 128), f32),
            pltpu.VMEM((DEVS, 2, 128), f32),
            pltpu.VMEM((DEVS, 2, 128), f32),
            pltpu.SemaphoreType.DMA,
            pltpu.SemaphoreType.DMA,
        ],
        compiler_params=pltpu.CompilerParams(
            collective_id=0, has_side_effects=True, vmem_limit_bytes=32 << 20
        ),
        name="gather_rows",
    )(table, index, noise)
    prio, pack = pl.pallas_call(
        functools.partial(train_kernel, 1024),
        out_shape=(SDS((1, N), f32), SDS((PACK, 128), f32)),
        in_specs=[VM] * 7,
        out_specs=(VM, VM),
        scratch_shapes=[pltpu.VMEM((2 * TILES_C + 6, 128), f32), pltpu.VMEM((FEAT, 256), f32)] + WEIGHTS + GRADS,
        compiler_params=pltpu.CompilerParams(vmem_limit_bytes=56 << 20),
        name="train_rows",
    )(x, nz, pair_count, actor_rows(actor), actor_rows(actor_target), critic, critic_target)
    ga, gc, stat = pl.pallas_call(
        functools.partial(reduce_kernel, shard_size),
        out_shape=(SDS((ROWS_A, 128), f32), SDS((2, TILES_C * 128), f32), SDS((1, 128), f32)),
        in_specs=[VM],
        out_specs=(VM, VM, VM),
        scratch_shapes=[
            pltpu.VMEM((HALF, 128), f32),
            pltpu.VMEM((OWNERS, CHUNK, 128), f32),
            pltpu.VMEM((CHIPS, CHUNK, 128), f32),
            pltpu.VMEM((CHUNK, 128), f32),
            pltpu.VMEM((OWNERS, CHUNK, 128), f32),
            pltpu.VMEM((2, HALF, 128), f32),
            pltpu.SemaphoreType.DMA((8,)),
        ],
        compiler_params=pltpu.CompilerParams(
            collective_id=1, has_side_effects=True, vmem_limit_bytes=32 << 20
        ),
        name="sum_grads",
    )(pack)
    actor_out = update(actor, ga.reshape(-1)[:PA], actor_momentum, actor_average, actor_target)
    critic_out = update(critic, gc[:, :PC], critic_momentum, critic_average, critic_target)
    outs = [stat[0, :2], prio.reshape(CAP, DEVS).T[None]]
    for one, two in zip(actor_out, critic_out):
        outs += [one, two]
    return tuple(outs)


def solution(mesh):
    rows = ("group", "shard")
    in_specs = (P(rows, None), P(rows, None, None), P(rows, None), P(rows, None, None, None)) + (P(),) * 8
    out_specs = (P(), P(rows, None, None)) + (P(),) * 10
    body = functools.partial(local, mesh.shape["group"], mesh.shape["shard"])
    return jax.shard_map(body, mesh=mesh, in_specs=in_specs, out_specs=out_specs, check_vma=False)
```

time: 536 us -> 110 us (0.21); the launches traced: 528 us -> 110 us
  matrix products: 180 us -> 0 us
  waiting for transfers between devices: 135 us -> 0 us
  Pallas kernels: 0 us -> 95.5 us
  blocking collectives: 67.2 us -> 0 us
  local copies, waits for them, and re-layouts: 72.7 us -> 8.22 us
  starting transfers between devices: 26.2 us -> 0 us
  other arithmetic: 30.9 us -> 5.45 us
  between operations: 16.1 us -> 0.71 us
    dot_general x36 -> x0, matrix products: 180 us -> none  [matmul(): return jnp.dot(a, b, precision=lax.Precision.HIGHEST)]
    psum x1 -> x0, waiting for transfers between devices: 128 us -> none  [local(): lax.psum((part_actor, part_critic, extra[0]), ('group', 'shard'))]
    pallas_call x0 -> x3, Pallas kernels: none -> 95.5 us  [the longest x1 48.6 us: local(): pl.pallas_call(functools.partial(train_kernel, 1024), out_shape=(SDS((1,...]
    psum x1 -> x0, blocking collectives: 67.2 us -> none  [local(): count = lax.psum(local_count, ('group', 'shard'))]
    all_to_all x3 -> x0, starting transfers between devices: 26 us -> none  [the longest x1 11.5 us: local(): lax.all_to_all(count_col, ('group', 'shard'), split_axis=0, concat_axis=0...]
    unnamed x143 -> x32, local copies, waits for them, and re-layouts: 29.8 us -> 5.81 us
    slice x19 -> x0, local copies, waits for them, and re-layouts: 15.7 us -> none  [unpack(): pieces.append(flat[start:start + number].reshape(shape))]
    gather x1 -> x0, local copies, waits for them, and re-layouts: 13 us -> none  [local(): outgoing = replay[sample_index[0]]]
  transfers between devices with their start and end apart: 4 -> 0, of which waited for: 2 -> 0; matrix products, arithmetic and copies ran while one was open for 11% -> 0% of each run, Pallas kernels for 0% -> 0%
where the time goes in v1:
time: 110 us
  Pallas kernels  95.5 us (87%)
  local copies, waits for them, and re-layouts  8.22 us (7%)
  other arithmetic  5.45 us (5%)
    pallas_call x1, Pallas kernels, local(): pl.pallas_call(functools.partial(train_kernel, 1024), out_shape=(SDS((1,...  48.6 us
    pallas_call x1, Pallas kernels, local(): pl.pallas_call(functools.partial(reduce_kernel, shard_size), out_shape=(S...  26.5 us
    pallas_call x1, Pallas kernels, local(): pl.pallas_call(functools.partial(gather_kernel, group_size, shard_size),...  20.3 us
    unnamed x32, local copies, waits for them, and re-layouts  5.81 us
    add x2, other arithmetic, update(): target_new = 0.005 * weight_new + 0.995 * target  2.81 us
    convert_element_type x2, other arithmetic, update(): weight_new.astype(bf)  2.64 us

profile of v1, /device:TPU:1, one launch (start us, length us, event | category | flops | bytes accessed | tf_op | source)
XLA Modules:
  0.0 109.9 jit_solution(16456955314231881322)
XLA Ops:
  0.6 1.9 %pad_bitcast_fusion = (f32[568,128]{1,0:T(8,128)}, f32[568,128]{1,0:T(8,128)}) fusion(f32[71942]{0:T(1024)} %param.22, f32[71942]{0:T(1024)} %param.16), kind=kLoop, calls=%fused_computation.8 | loop fusion | bytes 1157168 | tf_op jit(solution)/shard_map/reshape | solution.py:582
  2.5 1.4 %copy-done = f32[8192,42]{0,1:T(8,128)S(1)} copy-done((f32[8192,42]{0,1:T(8,128)S(1)}, f32[8192,42]{0,1:T(8,128)}, u32[]{:S(2)}) %copy-start) | copy-done | bytes 1376280
  3.9 0.9 copy-done.4
  4.8 0.7 copy-done.5
  5.6 20.3 %gather_rows.1 = (f32[48,4096]{1,0:T(8,128)S(1)}, f32[8,4096]{1,0:T(8,128)S(1)}) custom-call(f32[42,8192]{1,0:T(8,128)S(1)} %bitcast.19, s32[32,128]{1,0:T(8,128)S(1)} %bitcast.22, f32[6,32,128]{2,1,0:T(8,128)S(1)} %bitcast.21), custom_call_target="tpu_custom_call" | custom-call | tf_op jit(solution)/shard_map/gather_rows/pallas_call | solution.py:604
  25.9 0.0 copy-start.2
  25.9 0.9 copy-done.2
  26.8 0.7 copy-done.3
  27.5 48.6 %train_rows.1 = (f32[1,4096]{1,0:T(1,128)}, f32[1728,128]{1,0:T(8,128)}) custom-call(f32[48,4096]{1,0:T(8,128)} %copy-done.2, f32[8,4096]{1,0:T(8,128)} %copy-done.3, s32[1,128]{1,0:T(1,128)} %count_ref.1, f32[568,128]{1,0:T(8,128)} %get-tuple-element.37.actor_ref, f32[568,128]{1,0:T(8,128)} %get-tuple-element.36.actor_t_ref, f32[2,72193]{1,0:T(2,128)} %critic_ref.1, ...), custom_call_target="tpu_custom_call" | custom-call | tf_op jit(solution)/shard_map/train_rows/pallas_call | solution.py:623
  76.1 1.2 %copy-done.1 = f32[1728,128]{1,0:T(8,128)S(1)} copy-done((f32[1728,128]{1,0:T(8,128)S(1)}, f32[1728,128]{1,0:T(8,128)}, u32[]{:S(2)}) %copy-start.1) | copy-done | bytes 884760
  77.3 26.5 %sum_grads.1 = (f32[568,128]{1,0:T(8,128)S(1)}, f32[2,72320]{1,0:T(2,128)S(1)}, f32[1,128]{1,0:T(1,128)S(1)}) custom-call(f32[1728,128]{1,0:T(8,128)S(1)} %copy-done.1), custom_call_target="tpu_custom_call" | custom-call | tf_op jit(solution)/shard_map/sum_grads/pallas_call | solution.py:632
  103.8 0.0 copy-start.6
  103.8 0.0 copy-start.12
  103.9 0.5 slice_bitcast_fusion
  104.4 0.0 copy-done.9
  104.4 0.0 copy-done.14
  104.4 0.8 fusion.1
  105.2 0.0 copy-done.10
  105.2 0.0 copy-done.15
  105.2 0.9 multiply_add_fusion.3
  106.1 0.0 copy-done.6
  106.1 0.0 copy-done.12
  106.1 1.8 %fusion = (bf16[2,72193]{1,0:T(2,128)(2,1)}, f32[2,72193]{1,0:T(2,128)S(1)}, f32[2,72193]{1,0:T(2,128)}) fusion(f32[2,72193]{1,0:T(2,128)S(1)} %copy-done.6, f32[2,72320]{1,0:T(2,128)S(1)} %get-tuple-element.25, f32[2,72193]{1,0:T(2,128)S(1)} %copy-done.12), kind=kLoop, calls=%fused_computation.11 | loop fusion | flops 1010702 | bytes 3176492 | tf_op jit(solution)/shard_map/convert_element_type | solution.py:578
  108.0 1.9 %multiply_add_fusion = (f32[2,72193]{1,0:T(2,128)}, f32[2,72193]{1,0:T(2,128)}) fusion(f32[2,72193]{1,0:T(2,128)S(1)} %copy-done.7, f32[2,72193]{1,0:T(2,128)S(1)} %get-tuple-element.27, f32[2,72193]{1,0:T(2,128)S(1)} %copy-done.13), kind=kLoop, calls=%fused_computation | loop fusion | flops 866316 | bytes 2887720 | tf_op jit(solution)/shard_map/add | solution.py:577
  (17 shorter events, 0.0 us)
Async XLA Ops:
  2.5 1.4 %copy-start = (f32[8192,42]{0,1:T(8,128)S(1)}, f32[8192,42]{0,1:T(8,128)}, u32[]{:S(2)}) copy-start(f32[8192,42]{0,1:T(8,128)} %param.12) | copy-start | bytes 4128772
  3.9 0.9 copy-start.4
  4.8 0.7 copy-start.5
  25.9 0.9 copy-start.2
  26.8 0.7 copy-start.3
  27.5 76.9 %copy-start.9 = (f32[71942]{0:T(1024)S(1)}, f32[71942]{0:T(1024)}, u32[]{:S(2)}) copy-start(f32[71942]{0:T(1024)} %param.16) | copy-start | bytes 863308
  27.5 76.9 %copy-start.14 = (f32[71942]{0:T(1024)S(1)}, f32[71942]{0:T(1024)}, u32[]{:S(2)}) copy-start(f32[71942]{0:T(1024)} %param.18) | copy-start | bytes 863308
  27.5 77.7 %copy-start.10 = (f32[71942]{0:T(1024)S(1)}, f32[71942]{0:T(1024)}, u32[]{:S(2)}) copy-start(f32[71942]{0:T(1024)} %param.22) | copy-start | bytes 863308
  27.5 77.7 %copy-start.15 = (f32[71942]{0:T(1024)S(1)}, f32[71942]{0:T(1024)}, u32[]{:S(2)}) copy-start(f32[71942]{0:T(1024)} %param.20) | copy-start | bytes 863308
  76.1 1.2 %copy-start.1 = (f32[1728,128]{1,0:T(8,128)S(1)}, f32[1728,128]{1,0:T(8,128)}, u32[]{:S(2)}) copy-start(f32[1728,128]{1,0:T(8,128)} %get-tuple-element.21.pack_ref) | copy-start | bytes 2654212
  103.8 2.3 %copy-start.6 = (f32[2,72193]{1,0:T(2,128)S(1)}, f32[2,72193]{1,0:T(2,128)}, u32[]{:S(2)}) copy-start(f32[2,72193]{1,0:T(2,128)} %critic_ref.1) | copy-start | bytes 1732636
  103.8 2.3 %copy-start.12 = (f32[2,72193]{1,0:T(2,128)S(1)}, f32[2,72193]{1,0:T(2,128)}, u32[]{:S(2)}) copy-start(f32[2,72193]{1,0:T(2,128)} %param.19) | copy-start | bytes 1732636
  105.2 2.7 %copy-start.11 = (f32[71942]{0:T(1024)}, f32[71942]{0:T(1024)S(1)}, u32[]{:S(2)}) copy-start(f32[71942]{0:T(1024)S(1)} %get-tuple-element.30) | copy-start | bytes 863308
  106.1 1.8 %copy-start.7 = (f32[2,72193]{1,0:T(2,128)S(1)}, f32[2,72193]{1,0:T(2,128)}, u32[]{:S(2)}) copy-start(f32[2,72193]{1,0:T(2,128)} %critic_t_ref.1) | copy-start | bytes 1732636
  106.1 1.8 %copy-start.13 = (f32[2,72193]{1,0:T(2,128)S(1)}, f32[2,72193]{1,0:T(2,128)}, u32[]{:S(2)}) copy-start(f32[2,72193]{1,0:T(2,128)} %param.21) | copy-start | bytes 1732636
  107.9 1.9 %copy-start.8 = (f32[2,72193]{1,0:T(2,128)}, f32[2,72193]{1,0:T(2,128)S(1)}, u32[]{:S(2)}) copy-start(f32[2,72193]{1,0:T(2,128)S(1)} %get-tuple-element.27) | copy-start | bytes 1732636

commit v2 on v1

v2 whole, which is shorter than its diff:
```python
import functools

import jax
import jax.numpy as jnp
from jax import lax
from jax.experimental import pallas as pl
from jax.experimental.pallas import tpu as pltpu
from jax.sharding import PartitionSpec as P

OBS = 17
ACT = 6
UNITS = 256
CAP = 32
DEVS = 128
R_DEV = 8192
ROW = 42
PA = 71942
PC = 72193
N = DEVS * CAP

bf = jnp.bfloat16
f32 = jnp.float32
MESH = pl.DeviceIdType.MESH
VM = pl.BlockSpec(memory_space=pltpu.VMEM)
SDS = jax.ShapeDtypeStruct

SCALE = 2.0**-19
C0, C1, A, AT, T0, T1 = range(6)
FEAT = 48
ONE = 42
NEXT = 25

TILES_C = 565
ROWS_A = 568
AT_ACTOR = 1136
STAT = AT_ACTOR + 564
CHIPS = DEVS // 2
CHUNK = 8
HALF = CHIPS * CHUNK
PACK = 4 * HALF
TURN = 512
WIDTH = 1024


def dot(a, b):
    return lax.dot_general(a, b, (((1,), (0,)), ((), ())), preferred_element_type=f32)


def dot_nt(a, b):
    return lax.dot_general(a, b, (((1,), (1,)), ((), ())), preferred_element_type=f32)


def dot_exact(a, b, dims):
    return lax.dot_general(a, b, (dims, ((), ())), precision=lax.Precision.HIGHEST, preferred_element_type=f32)


def split(v):
    hi = v.astype(bf)
    return hi, (v - hi.astype(f32)).astype(bf)


def three(v):
    hi, lo = split(v)
    return jnp.concatenate([hi, lo, hi], 0)


def lanes(tile, width):
    return jnp.concatenate([tile] * (width // 128), 1)


def fold(v):
    out = v[:, :128]
    for i in range(1, v.shape[1] // 128):
        out = out + v[:, 128 * i : 128 * (i + 1)]
    return out


def column(row):
    return jnp.transpose(jnp.broadcast_to(row, (128, 128)))


def turn_noise(noise_ref, q_ref, nsend):
    q_ref[...] = jnp.zeros_like(q_ref)
    for j in range(ACT):
        q_ref[pl.ds(j + 1, CAP, stride=8), :] = 0.5 * jnp.tanh(0.4 * noise_ref[j])
    turned = jnp.transpose(q_ref[...])
    nsend[:, 0, :] = turned[:, :128]
    nsend[:, 1, :] = turned[:, 128:]


def noise_back(nrecv, nz_ref):
    back = jnp.transpose(jnp.concatenate([nrecv[:, 0, :], nrecv[:, 1, :]], 1))
    for c in range(CAP):
        nz_ref[:, 128 * c : 128 * (c + 1)] = back[8 * c : 8 * (c + 1), :]


def turn_table(i, table_ref, rows_ref):
    s = pl.ds(pl.multiple_of(i * TURN, TURN), TURN)
    v = jnp.concatenate([table_ref[:, s], jnp.zeros((128 - ROW, TURN), f32)], 0)
    rows_ref[s, :] = jnp.transpose(v)


def pick_rows(index_ref, rows_ref, picked_ref, x_ref):
    ones = lax.broadcasted_iota(jnp.int32, (8, 128), 0) == (ONE - 40)

    def body(c, carry):
        for d in range(DEVS):
            picked_ref[d : d + 1, :] = rows_ref[pl.ds(index_ref[c, d], 1), :]
        turned = jnp.transpose(picked_ref[...])
        s = pl.ds(pl.multiple_of(c * 128, 128), 128)
        x_ref[0:40, s] = turned[0:40]
        x_ref[40:48, s] = jnp.where(ones, 1.0, turned[40:48])
        return carry

    lax.fori_loop(0, CAP, body, 0)


def put_square(net, w2, w2f_ref, w2b_ref):
    w2 = 0.5 * w2
    turned = jnp.transpose(w2)
    hi, lo = split(turned)
    w2f_ref[net] = jnp.concatenate([hi, hi, lo], 1)
    if net in (C0, C1, A):
        hi, lo = split(w2)
        w2b_ref[net] = jnp.concatenate([hi, hi, lo], 1)


def put_first(net, pad_ref, w1_ref):
    w1 = 0.5 * pad_ref[...]
    hi = w1.astype(bf).astype(f32)
    lo = w1 - hi
    stacked = jnp.concatenate([hi, hi, lo, jnp.zeros((256 - 3 * FEAT, 256), f32)], 0)
    w1_ref[net] = jnp.transpose(stacked).astype(bf)


def put_column(ref, net, left, right, factor):
    ref[net] = jnp.concatenate([column(left * factor), column(right * factor)], 0)


def prepare_critics(critic_ref, rows_ref, pad_ref, first, w1_ref, w2f_ref, w2b_ref, b2_ref, w3_ref, b3_ref, w1a_ref):
    for t in range(TILES_C - 1):
        rows_ref[2 * t : 2 * t + 2, :] = critic_ref[:, 128 * t : 128 * (t + 1)]
    for c in range(2):
        net = first + c
        start = NEXT if first == T0 else 0
        pad_ref[...] = jnp.zeros_like(pad_ref)
        for half in range(2):
            s = pl.ds(128 * half, 128)
            pad_ref[pl.ds(start, OBS), s] = rows_ref[pl.ds(c + 2 * half, OBS, stride=4), :]
            pad_ref[pl.ds(OBS, ACT), s] = rows_ref[pl.ds(c + 2 * half + 4 * OBS, ACT, stride=4), :]
            pad_ref[pl.ds(ONE, 1), s] = rows_ref[pl.ds(92 + c + 2 * half, 1), :]
        put_first(net, pad_ref, w1_ref)
        if net == C0:
            hi = pad_ref[16:24, :].astype(bf).astype(f32)
            lo = pad_ref[16:24, :] - hi
            block = jnp.concatenate([hi, hi, lo], 1)
            w1a_ref[...] = jnp.concatenate([block, jnp.zeros_like(block)], 0).astype(bf)
        w2 = jnp.concatenate(
            [rows_ref[pl.ds(96 + c, UNITS, stride=4), :], rows_ref[pl.ds(98 + c, UNITS, stride=4), :]], 1
        )
        put_square(net, w2, w2f_ref, w2b_ref)
        put_column(b2_ref, net, rows_ref[1120 + c : 1121 + c, :], rows_ref[1122 + c : 1123 + c, :], 0.5)
        put_column(w3_ref, net, rows_ref[1124 + c : 1125 + c, :], rows_ref[1126 + c : 1127 + c, :], 1.0)
        b3_ref[net] = jnp.broadcast_to(critic_ref[c : c + 1, PC - 1 : PC], (1, 128))


def head_maps(j):
    k = lax.broadcasted_iota(jnp.int32, (UNITS, 16), 0)
    r = lax.broadcasted_iota(jnp.int32, (UNITS, 16), 1)
    row = ((k * ACT + j) // 128) == r
    k = lax.broadcasted_iota(jnp.int32, (UNITS, 128), 0)
    l = lax.broadcasted_iota(jnp.int32, (UNITS, 128), 1)
    lane = ((k * ACT + j) % 128) == l
    return row.astype(f32), lane


def head_of(flat):
    hi = flat.astype(bf).astype(f32)
    out = []
    for part in (hi, flat - hi):
        part = part.astype(bf)
        spread = []
        for j in range(ACT):
            row, lane = head_maps(j)
            spread.append(jnp.where(lane, dot(row.astype(bf), part), 0.0).astype(bf))
        r = lax.broadcasted_iota(jnp.int32, (16, 128 * ACT), 0)
        l = lax.broadcasted_iota(jnp.int32, (16, 128 * ACT), 1)
        take = ((l // 128) == (r - 1)).astype(f32).astype(bf)
        out.append(dot_nt(take, jnp.concatenate(spread, 1))[:8])
    return out


def head_back(turned):
    out = jnp.zeros((16, 128), f32)
    for j in range(ACT):
        row, lane = head_maps(j)
        picked = jnp.transpose(row) * turned[j + 1 : j + 2, :]
        out = out + dot_exact(picked, lane.astype(f32), ((1,), (0,)))
    return out


def prepare_actor(net, actor_ref, rows_ref, pad_ref, w1_ref, w2f_ref, w2b_ref, b2_ref, w3t_ref, w3b_ref, b3a_ref):
    whole = PA // 1024
    for t in range(whole):
        rows_ref[8 * t : 8 * t + 8, :] = actor_ref[pl.ds(1024 * t, 1024)].reshape(8, 128)
    rest = (PA - 1024 * whole) // 128
    rows_ref[8 * whole : 8 * whole + rest, :] = actor_ref[pl.ds(1024 * whole, 128 * rest)].reshape(rest, 128)
    rows_ref[562:563, 0:ACT] = actor_ref[pl.ds(562 * 128, ACT)].reshape(1, ACT)
    start = NEXT if net == AT else 0
    pad_ref[...] = jnp.zeros_like(pad_ref)
    for half in range(2):
        s = pl.ds(128 * half, 128)
        pad_ref[pl.ds(start, OBS), s] = rows_ref[pl.ds(half, OBS, stride=2), :]
        pad_ref[pl.ds(ONE, 1), s] = rows_ref[pl.ds(34 + half, 1), :]
    put_first(net, pad_ref, w1_ref)
    w2 = jnp.concatenate([rows_ref[pl.ds(36, UNITS, stride=2), :], rows_ref[pl.ds(37, UNITS, stride=2), :]], 1)
    put_square(net, w2, w2f_ref, w2b_ref)
    put_column(b2_ref, net, rows_ref[548:549, :], rows_ref[549:550, :], 0.5)
    flat = jnp.concatenate([rows_ref[550:562, :], jnp.zeros((4, 128), f32)], 0)
    hi, lo = head_of(flat)
    block = jnp.concatenate([hi, hi, lo], 1)
    w3t_ref[net - A] = jnp.concatenate([block, jnp.zeros_like(block)], 0).astype(bf)
    if net == A:
        stacked = jnp.concatenate([hi, hi, lo, jnp.zeros((104, UNITS), f32)], 0)
        w3b_ref[...] = (0.5 * jnp.transpose(stacked)).astype(bf)
    bias = column(rows_ref[562:563, :])
    b3a_ref[net - A] = jnp.zeros((8, 128), f32)
    b3a_ref[net - A, 1 : 1 + ACT, :] = bias[:ACT]


def act(zh):
    u = jnp.tanh(zh) + 1.0
    return u, zh * u


def slope(u, s):
    return u + s * (2.0 - u)


class Step:
    def __init__(self, i, width, x_ref, weights):
        (
            self.w1, self.w2f, self.w2b, self.b2, self.w3, self.b3, self.w3t, self.w3b, self.b3a, self.w1a,
        ) = weights
        self.i, self.width = i, width
        self.lanes = pl.ds(pl.multiple_of(i * width, width), width)
        self.x = x_ref[:, self.lanes]
        self.x3 = three(self.x)
        rows8 = lax.broadcasted_iota(jnp.int32, (8, width), 0)
        self.is_action = (rows8 >= 1) & (rows8 <= ACT)

    def with_action(self, a):
        x = self.x
        return three(jnp.concatenate([x[:16], jnp.where(self.is_action, a, x[16:24]), x[24:]], 0))

    def first(self, net, xx):
        return act(dot(self.w1[net, :, : 3 * FEAT], xx))

    def second(self, net, h3):
        return act(dot(self.w2f[net], h3) + lanes(self.b2[net], self.width))

    def value(self, net, s):
        return jnp.sum(s * lanes(self.w3[net], self.width), 0, keepdims=True) + lanes(self.b3[net], self.width)

    def head(self, net, s3):
        return dot(self.w3t[net - A], s3)[:8] + lanes(self.b3a[net - A], self.width)

    def valid(self, count_ref):
        tiles = self.width // 128
        return jnp.concatenate([((self.i * tiles + t) < count_ref[...]).astype(f32) for t in range(tiles)], 1)

    def back(self, net, dz2):
        hi, lo = split(dz2)
        return hi, lo, dot(self.w2b[net], jnp.concatenate([hi, lo, hi], 0))

    def weight_grads(self, net, h1, hi, lo, dz1, g2_ref, g1_ref):
        left = jnp.concatenate([h1[:UNITS], h1[UNITS : 2 * UNITS], h1[:UNITS]], 1)
        g2_ref[net] += dot_nt(left, jnp.concatenate([hi, hi, lo], 1))
        xhi, xlo = self.x3[:FEAT], self.x3[FEAT : 2 * FEAT]
        left = jnp.concatenate(
            [jnp.concatenate([xhi, xlo], 0), jnp.concatenate([xhi, jnp.zeros_like(xlo)], 0)], 1
        )
        a, b = split(dz1)
        g1_ref[net] += dot_nt(left, jnp.concatenate([a, b], 1))


def critic_block(i, width, x_ref, nz_ref, count_ref, weights, prio_ref, grads):
    g2_ref, g1_ref, g3a_ref, db2_ref, dw3_ref, st_ref = grads
    st = Step(i, width, x_ref, weights)
    x, x3 = st.x, st.x3

    u, s = st.first(AT, x3)
    u, s = st.second(AT, three(s))
    next_action = jnp.tanh(st.head(AT, three(s)) + nz_ref[:, st.lanes])

    kept = []
    for net in (C0, C1):
        u, s = st.first(net, x3)
        h1, d1 = three(s), slope(u, s)
        u, s = st.second(net, h1)
        kept.append((h1, d1, s, slope(u, s), st.value(net, s)))

    xt = st.with_action(next_action)
    targets = []
    for net in (T0, T1):
        u, s = st.first(net, xt)
        u, s = st.second(net, three(s))
        targets.append(st.value(net, s))

    y = x[23:24] + 0.99 * x[24:25] * jnp.minimum(targets[0], targets[1])
    valid = st.valid(count_ref)
    delta = [k[4] - y for k in kept]
    prio = valid * jnp.sqrt(delta[0] * delta[0] + 1.0)
    tiles = width // 128
    for t in range(tiles):
        prio_ref[pl.ds(i * tiles + t, 1), :] = prio[:, 128 * t : 128 * (t + 1)]
    st_ref[0:1, :] += fold(valid * (delta[0] * delta[0] + delta[1] * delta[1]))
    st_ref[1:2, :] += fold(valid)
    scaled = valid * SCALE

    for net in (C0, C1):
        h1, d1, s2, d2, _ = kept[net]
        dq = (2.0 * scaled) * delta[net]
        st_ref[2 + net : 3 + net, :] += fold(dq)
        dw3_ref[net] += fold(s2 * dq)
        dz2 = lanes(st.w3[net], width) * (0.5 * dq) * d2
        db2_ref[net] += fold(dz2)
        hi, lo, dh1 = st.back(net, dz2)
        st.weight_grads(net, h1, hi, lo, dh1 * d1, g2_ref, g1_ref)


def actor_block(i, width, x_ref, count_ref, weights, grads):
    g2_ref, g1_ref, g3a_ref, db2_ref, dw3_ref, st_ref = grads
    st = Step(i, width, x_ref, weights)

    u, s = st.first(A, st.x3)
    h1a, d1a = three(s), slope(u, s)
    u, s = st.second(A, h1a)
    h2a, d2a = three(s), slope(u, s)
    policy = jnp.tanh(st.head(A, h2a))

    u, s = st.first(C0, st.with_action(policy))
    d1f = slope(u, s)
    u, s = st.second(C0, three(s))
    d2f, q_policy = slope(u, s), st.value(C0, s)
    valid = st.valid(count_ref)
    st_ref[0:1, :] -= fold(valid * q_policy)

    dz2 = lanes(st.w3[C0], width) * (-0.5 * SCALE * valid) * d2f
    hi, lo, dh1 = st.back(C0, dz2)
    da = dot(st.w1a[...], three(dh1 * d1f))[:8]
    dp = jnp.where(st.is_action, da * (1.0 - policy * policy), 0.0)
    st_ref[8:16, :] += fold(dp)
    hi = dp.astype(bf).astype(f32)
    lo = dp - hi
    zero = jnp.zeros_like(hi)
    stacked = jnp.concatenate([hi, lo, hi, zero], 0).astype(bf)
    left = jnp.concatenate([jnp.concatenate([hi, lo], 0), jnp.concatenate([hi, zero], 0)], 1).astype(bf)
    g3a_ref[...] += dot_nt(left, jnp.concatenate([h2a[:UNITS], h2a[UNITS : 2 * UNITS]], 1))
    dz2 = dot(st.w3b[:, :32], stacked) * d2a
    db2_ref[A] += fold(dz2)
    hi, lo, dh1 = st.back(A, dz2)
    st.weight_grads(A, h1a, hi, lo, dh1 * d1a, g2_ref, g1_ref)


def lane_sums(tile):
    return dot_exact(jnp.ones((8, 128), f32), tile, ((1,), (1,)))


def pack_critics(pack_ref, grads):
    g2_ref, g1_ref, g3a_ref, db2_ref, dw3_ref, st_ref = grads
    lane = lax.broadcasted_iota(jnp.int32, (1, 128), 1)
    sums = jnp.sum(st_ref[...], 1, keepdims=True)
    for c in range(2):
        g1 = g1_ref[c, :FEAT, :] + g1_ref[c, FEAT:, :]
        b2 = lane_sums(db2_ref[c])[0:1]
        w3 = lane_sums(dw3_ref[c])[0:1]
        for half in range(2):
            s = slice(128 * half, 128 * (half + 1))
            at = c + 2 * half
            pack_ref[pl.ds(at, OBS + ACT, stride=4), :] = g1[: OBS + ACT, s]
            pack_ref[at + 92 : at + 93, :] = g1[ONE : ONE + 1, s]
            pack_ref[pl.ds(at + 96, UNITS, stride=4), :] = g2_ref[c, :, s]
            pack_ref[at + 1120 : at + 1121, :] = b2[:, s]
            pack_ref[at + 1124 : at + 1125, :] = w3[:, s]
        pack_ref[c + 1128 : c + 1129, :] = jnp.where(lane == 0, sums[2 + c : 3 + c], 0.0)
    pack_ref[2 * TILES_C : AT_ACTOR, :] = jnp.zeros((AT_ACTOR - 2 * TILES_C, 128), f32)


def pack_actor(pack_ref, grads):
    g2_ref, g1_ref, g3a_ref, db2_ref, dw3_ref, st_ref = grads
    lane = lax.broadcasted_iota(jnp.int32, (1, 128), 1)
    sums = jnp.sum(st_ref[...], 1, keepdims=True)
    g1 = g1_ref[A, :FEAT, :] + g1_ref[A, FEAT:, :]
    b2 = lane_sums(db2_ref[A])[0:1]
    o = AT_ACTOR
    for half in range(2):
        s = slice(128 * half, 128 * (half + 1))
        pack_ref[pl.ds(o + half, OBS, stride=2), :] = g1[:OBS, s]
        pack_ref[o + 34 + half : o + 35 + half, :] = g1[ONE : ONE + 1, s]
        pack_ref[pl.ds(o + 36 + half, UNITS, stride=2), :] = g2_ref[A, :, s]
        pack_ref[o + 548 + half : o + 549 + half, :] = b2[:, s]
    pack_ref[o + 550 : o + 562, :] = head_back(g3a_ref[:8, :] + g3a_ref[8:, :])[:12]
    e = lax.broadcasted_iota(jnp.int32, (8, 128), 1) == lax.broadcasted_iota(jnp.int32, (8, 128), 0) - 1
    pack_ref[o + 562 : o + 563, :] = jnp.sum(jnp.where(e, sums[8:16], 0.0), 0, keepdims=True)
    pack_ref[o + 563 : STAT, :] = jnp.zeros((STAT - o - 563, 128), f32)
    pack_ref[STAT : STAT + 1, :] = jnp.where(lane == 0, sums[0:1], jnp.where(lane == 1, sums[1:2], 0.0))
    pack_ref[STAT + 1 : PACK, :] = jnp.zeros((PACK - STAT - 1, 128), f32)


WEIGHTS = [
    pltpu.VMEM((6, UNITS, 256), bf),
    pltpu.VMEM((6, UNITS, 3 * UNITS), bf),
    pltpu.VMEM((3, UNITS, 3 * UNITS), bf),
    pltpu.VMEM((6, UNITS, 128), f32),
    pltpu.VMEM((6, UNITS, 128), f32),
    pltpu.VMEM((6, 1, 128), f32),
    pltpu.VMEM((2, 16, 3 * UNITS), bf),
    pltpu.VMEM((UNITS, 128), bf),
    pltpu.VMEM((2, 8, 128), f32),
    pltpu.VMEM((16, 3 * UNITS), bf),
]
GRADS = [
    pltpu.VMEM((3, UNITS, UNITS), f32),
    pltpu.VMEM((3, 2 * FEAT, UNITS), f32),
    pltpu.VMEM((16, UNITS), f32),
    pltpu.VMEM((3, UNITS, 128), f32),
    pltpu.VMEM((2, UNITS, 128), f32),
    pltpu.VMEM((16, 128), f32),
]


def drain(ref, sem, copies):
    view = ref.at[pl.ds(0, copies)]
    pltpu.make_async_copy(view, view, sem).wait()


class Sum:
    def __init__(self, g, shard_size, pack_ref, buffers, sems):
        group, shard = lax.axis_index("group"), lax.axis_index("shard")
        self.g, self.per = g, shard_size // 2
        self.core = lax.rem(shard, 2)
        self.chip = group * self.per + shard // 2
        self.sibling = (group, shard + 1 - 2 * self.core)
        self.pack_ref = pack_ref
        self.other, self.half, self.parts, self.mine, self.whole = (b.at[g] for b in buffers)
        self.sems = sems.at[g]

    def remote(self, src, dst, n, to):
        return pltpu.make_async_remote_copy(
            src_ref=src,
            dst_ref=dst,
            send_sem=self.sems.at[2 * n],
            recv_sem=self.sems.at[2 * n + 1],
            device_id=to,
            device_id_type=MESH,
        )

    def to_all(self, src_of, dst, n):
        def send(k, carry):
            peer = lax.rem(self.chip + k, CHIPS)
            to = (peer // self.per, lax.rem(peer, self.per) * 2 + self.core)
            self.remote(src_of(peer), dst, n, to).start()
            return carry

        lax.fori_loop(1, CHIPS, send, 0)

    def swap(self):
        give = pl.multiple_of(self.g * 2 * HALF + (1 - self.core) * HALF, HALF)
        return self.remote(self.pack_ref.at[pl.ds(give, HALF)], self.other, 0, self.sibling)

    def scatter(self):
        keep = pl.multiple_of(self.g * 2 * HALF + self.core * HALF, HALF)
        total = self.pack_ref[pl.ds(keep, HALF), :] + self.other[...]
        self.half[...] = total.reshape(CHIPS, CHUNK, 128)
        self.to_all(lambda peer: self.half.at[peer], self.parts.at[self.chip], 1)

    def spread(self):
        drain(self.half, self.sems.at[2], CHIPS - 1)
        drain(self.parts, self.sems.at[3], CHIPS - 1)
        self.parts[pl.ds(self.chip, 1)] = self.half[pl.ds(self.chip, 1)]
        self.mine[...] = jnp.sum(self.parts[...], 0)
        self.to_all(lambda peer: self.mine, self.whole.at[self.core, self.chip], 2)

    def back(self):
        drain(self.parts, self.sems.at[4], CHIPS - 1)
        drain(self.whole.at[0], self.sems.at[5], CHIPS - 1)
        self.whole[pl.ds(self.core, 1), pl.ds(self.chip, 1)] = self.mine[...][None, None]
        return self.remote(self.whole.at[self.core], self.whole.at[self.core], 3, self.sibling)


def step_kernel(
    group_size,
    shard_size,
    width,
    table_hbm,
    index_hbm,
    noise_hbm,
    count_hbm,
    actor_hbm,
    actor_t_hbm,
    critic_hbm,
    critic_t_hbm,
    prio_ref,
    sum_ref,
    table_ref,
    index_ref,
    noise_ref,
    count_ref,
    actor_ref,
    actor_t_ref,
    critic_ref,
    critic_t_ref,
    in_sems,
    rows_ref,
    picked_ref,
    q_ref,
    nsend,
    nrecv,
    noise_sems,
    x_ref,
    nz_ref,
    flat_ref,
    pad_ref,
    pack_ref,
    other,
    half,
    parts,
    mine,
    whole,
    sems,
    *scratch,
):
    weights, grads = scratch[: len(WEIGHTS)], scratch[len(WEIGHTS) :]
    w1_ref, w2f_ref, w2b_ref, b2_ref, w3_ref, b3_ref, w3t_ref, w3b_ref, b3a_ref, w1a_ref = weights
    me = lax.axis_index("group") * shard_size + lax.axis_index("shard")

    def device(k):
        peer = lax.rem(me + k, DEVS)
        return peer, (peer // shard_size, lax.rem(peer, shard_size))

    loads = [
        pltpu.make_async_copy(src, dst, in_sems.at[n])
        for n, (src, dst) in enumerate(
            (
                (noise_hbm, noise_ref),
                (critic_t_hbm, critic_t_ref),
                (actor_t_hbm, actor_t_ref),
                (critic_hbm, critic_ref),
                (actor_hbm, actor_ref),
                (count_hbm, count_ref),
                (table_hbm, table_ref),
                (index_hbm, index_ref),
            )
        )
    ]
    for load in loads:
        load.start()

    barrier = pltpu.get_barrier_semaphore()

    def greet(k, carry):
        pl.semaphore_signal(barrier, inc=1, device_id=device(k)[1], device_id_type=MESH)
        return carry

    lax.fori_loop(1, DEVS, greet, 0)
    for ref in grads:
        ref[...] = jnp.zeros_like(ref)
    loads[0].wait()
    turn_noise(noise_ref, q_ref, nsend)
    for n, first, ref in ((1, T0, critic_t_ref), (3, C0, critic_ref)):
        loads[n].wait()
        prepare_critics(
            ref, flat_ref, pad_ref, first, w1_ref, w2f_ref, w2b_ref, b2_ref, w3_ref, b3_ref, w1a_ref
        )
    for n, net, ref in ((2, AT, actor_t_ref), (4, A, actor_ref)):
        loads[n].wait()
        prepare_actor(net, ref, flat_ref, pad_ref, w1_ref, w2f_ref, w2b_ref, b2_ref, w3t_ref, w3b_ref, b3a_ref)
    for n in (5, 6, 7):
        loads[n].wait()

    pl.semaphore_wait(barrier, DEVS - 1)

    def send(k):
        peer, to = device(k)
        pltpu.make_async_remote_copy(
            src_ref=nsend.at[peer],
            dst_ref=nrecv.at[me],
            send_sem=noise_sems.at[0],
            recv_sem=noise_sems.at[1],
            device_id=to,
            device_id_type=MESH,
        ).start()

    steps = R_DEV // TURN
    each = DEVS // steps

    def turn(i, carry):
        turn_table(i, table_ref, rows_ref)
        for j in range(each):
            send(1 + i * each + j)
        return carry

    lax.fori_loop(0, steps - 1, turn, 0)
    turn_table(steps - 1, table_ref, rows_ref)
    for j in range(each - 1):
        send(1 + (steps - 1) * each + j)
    pick_rows(index_ref, rows_ref, picked_ref, x_ref)
    drain(nsend, noise_sems.at[0], DEVS - 1)
    drain(nrecv, noise_sems.at[1], DEVS - 1)
    nrecv[pl.ds(me, 1)] = nsend[pl.ds(me, 1)]
    noise_back(nrecv, nz_ref)

    def critics(i, carry):
        critic_block(i, width, x_ref, nz_ref, count_ref, weights, prio_ref, grads)
        return carry

    blocks = N // width
    lax.fori_loop(0, blocks, critics, 0)
    pack_critics(pack_ref, grads)

    buffers = (other, half, parts, mine, whole)
    early = Sum(0, shard_size, pack_ref, buffers, sems)
    late = Sum(1, shard_size, pack_ref, buffers, sems)
    swap = early.swap()
    swap.start()
    back = early.back
    for i in range(blocks):
        actor_block(i, width, x_ref, count_ref, weights, grads)
        if i == 0:
            swap.wait()
            early.scatter()
        elif i == 1:
            early.spread()
        elif i == 2:
            back = early.back()
            back.start()
    pack_actor(pack_ref, grads)
    swap = late.swap()
    swap.start()
    back.wait()
    swap.wait()
    late.scatter()
    sum_ref[: 2 * HALF, :] = whole[0].reshape(2 * HALF, 128)
    late.spread()
    back = late.back()
    back.start()
    back.wait()
    sum_ref[2 * HALF :, :] = whole[1].reshape(2 * HALF, 128)


def update(weight, grad, momentum, average, target):
    momentum_new = 0.9 * momentum + grad
    weight_new = weight - 0.1 * (grad + 0.9 * momentum_new)
    average_new = 0.99 * average + 0.01 * weight_new
    target_new = 0.005 * weight_new + 0.995 * target
    return (weight_new, momentum_new, average_new, target_new, weight_new.astype(bf))


def grads_kernel(sum_ref, prio_in, ga_ref, gc_ref, stat_ref, prio_ref):
    stat = sum_ref[STAT : STAT + 1, :]
    factor = (1.0 / SCALE) / stat[:, 1:2]
    stat_ref[...] = stat
    prio_ref[...] = prio_in[...]
    ga_ref[...] = sum_ref[AT_ACTOR : AT_ACTOR + ROWS_A, :] * factor
    for t in range(TILES_C):
        gc_ref[:, 128 * t : 128 * (t + 1)] = sum_ref[2 * t : 2 * t + 2, :] * factor


def local(
    group_size,
    shard_size,
    replay,
    sample_index,
    pair_count,
    noise,
    actor,
    critic,
    actor_momentum,
    critic_momentum,
    actor_average,
    critic_average,
    actor_target,
    critic_target,
):
    any_ = pl.BlockSpec(memory_space=pl.ANY)
    prio, total = pl.pallas_call(
        functools.partial(step_kernel, group_size, shard_size, WIDTH),
        out_shape=(SDS((CAP, DEVS), f32), SDS((PACK, 128), f32)),
        in_specs=[any_] * 8,
        out_specs=(VM, VM),
        scratch_shapes=[
            pltpu.VMEM((ROW, R_DEV), f32),
            pltpu.SMEM((CAP, DEVS), jnp.int32),
            pltpu.VMEM((ACT, CAP, DEVS), f32),
            pltpu.VMEM((1, DEVS), jnp.int32),
            pltpu.VMEM((PA,), f32),
            pltpu.VMEM((PA,), f32),
            pltpu.VMEM((2, PC), f32),
            pltpu.VMEM((2, PC), f32),
            pltpu.SemaphoreType.DMA((8,)),
            pltpu.VMEM((R_DEV, 128), f32),
            pltpu.VMEM((128, 128), f32),
            pltpu.VMEM((256, 128), f32),
            pltpu.VMEM((DEVS, 2, 128), f32),
            pltpu.VMEM((DEVS, 2, 128), f32),
            pltpu.SemaphoreType.DMA((2,)),
            pltpu.VMEM((FEAT, N), f32),
            pltpu.VMEM((8, N), f32),
            pltpu.VMEM((2 * TILES_C + 6, 128), f32),
            pltpu.VMEM((FEAT, 256), f32),
            pltpu.VMEM((PACK, 128), f32),
            pltpu.VMEM((2, HALF, 128), f32),
            pltpu.VMEM((2, CHIPS, CHUNK, 128), f32),
            pltpu.VMEM((2, CHIPS, CHUNK, 128), f32),
            pltpu.VMEM((2, CHUNK, 128), f32),
            pltpu.VMEM((2, 2, CHIPS, CHUNK, 128), f32),
            pltpu.SemaphoreType.DMA((2, 8)),
        ]
        + WEIGHTS
        + GRADS,
        compiler_params=pltpu.CompilerParams(
            collective_id=0, has_side_effects=True, vmem_limit_bytes=56 << 20
        ),
        name="td3_step",
    )(
        replay.T,
        sample_index[0].T,
        jnp.transpose(noise[0], (2, 1, 0)),
        pair_count,
        actor,
        actor_target,
        critic,
        critic_target,
    )
    ga, gc, stat, prio = pl.pallas_call(
        grads_kernel,
        out_shape=(
            SDS((ROWS_A, 128), f32),
            SDS((2, TILES_C * 128), f32),
            SDS((1, 128), f32),
            SDS((CAP, DEVS), f32),
        ),
        in_specs=[VM, VM],
        out_specs=(VM, VM, VM, VM),
        name="unpack_grads",
    )(total, prio)
    actor_out = update(actor, ga.reshape(-1)[:PA], actor_momentum, actor_average, actor_target)
    critic_out = update(critic, gc[:, :PC], critic_momentum, critic_average, critic_target)
    outs = [stat[0, :2], prio.T[None]]
    for one, two in zip(actor_out, critic_out):
        outs += [one, two]
    return tuple(outs)


def solution(mesh):
    rows = ("group", "shard")
    in_specs = (P(rows, None), P(rows, None, None), P(rows, None), P(rows, None, None, None)) + (P(),) * 8
    out_specs = (P(), P(rows, None, None)) + (P(),) * 10
    body = functools.partial(local, mesh.shape["group"], mesh.shape["shard"])
    return jax.shard_map(body, mesh=mesh, in_specs=in_specs, out_specs=out_specs, check_vma=False)
```

time: 110 us -> 101 us (0.918)
  local copies, waits for them, and re-layouts: 8.22 us -> 1.35 us
  Pallas kernels: 95.5 us -> 92.1 us
    unnamed x32 -> x22, local copies, waits for them, and re-layouts: 5.81 us -> 0.05 us
    pallas_call x3 -> x2, Pallas kernels: 95.5 us -> 92.1 us  [the longest x1 89.6 us: local(): pl.pallas_call(functools.partial(step_kernel, group_size, shard_size, WID...]
    reshape x1 -> x0, local copies, waits for them, and re-layouts: 1.9 us -> none  [actor_rows(): return jnp.pad(flat, (0, ROWS_A * 128 - PA)).reshape(ROWS_A, 128)]
where the time goes in v2:
time: 101 us
  Pallas kernels  92.1 us (91%)
  other arithmetic  6.4 us (6%)
  local copies, waits for them, and re-layouts  1.35 us (1%)
    pallas_call x1, Pallas kernels, local(): pl.pallas_call(functools.partial(step_kernel, group_size, shard_size, WID...  89.6 us
    convert_element_type x2, other arithmetic, update(): weight_new.astype(bf)  3.59 us
    add x2, other arithmetic, update(): target_new = 0.005 * weight_new + 0.995 * target  2.81 us
    pallas_call x1, Pallas kernels, local(): pl.pallas_call(grads_kernel, out_shape=(SDS((ROWS_A, 128), f32), SDS((2,...  2.5 us

profile of v2, /device:TPU:1, one launch (start us, length us, event | category | flops | bytes accessed | tf_op | source)
XLA Modules:
  0.0 100.6 jit_solution(9163043470184468957)
XLA Ops:
  0.6 0.0 copy-start.3
  0.7 0.0 copy-start.9
  0.7 89.6 %td3_step.1 = (f32[32,128]{1,0:T(8,128)}, f32[2048,128]{1,0:T(8,128)}) custom-call(f32[42,8192]{1,0:T(8,128)} %bitcast.13, s32[32,128]{1,0:T(8,128)} %bitcast.16, f32[6,32,128]{2,1,0:T(8,128)} %bitcast.15, s32[1,128]{1,0:T(1,128)} %count_hbm.1, f32[71942]{0:T(1024)} %actor_hbm.1, f32[71942]{0:T(1024)} %actor_t_hbm.1, f32[2,72193]{1,0:T(2,128)} %critic_hbm.1, ...), custom_call_target="tpu_custom_call" | custom-call | tf_op jit(solution)/shard_map/td3_step/pallas_call | solution.py:687
  90.2 0.0 copy-start.4
  90.3 0.0 copy-start.10
  90.3 2.5 %unpack_grads.1 = (f32[568,128]{1,0:T(8,128)}, f32[2,72320]{1,0:T(2,128)}, f32[1,128]{1,0:T(1,128)}, f32[32,128]{1,0:T(8,128)}) custom-call(f32[2048,128]{1,0:T(8,128)} %get-tuple-element.18.sum_ref, f32[32,128]{1,0:T(8,128)} %get-tuple-element.19.prio_in), custom_call_target="tpu_custom_call" | custom-call | tf_op jit(solution)/shard_map/unpack_grads/pallas_call | solution.py:736
  92.8 0.0 copy-start.8
  92.8 1.3 %slice_bitcast_fusion = f32[2]{0:T(128)} fusion(f32[1,128]{1,0:T(1,128)} %get-tuple-element.20), kind=kLoop, calls=%fused_computation.8 | loop fusion | bytes 16 | tf_op jit(solution)/shard_map/squeeze | solution.py:750
  94.1 0.0 copy-done.3
  94.1 0.0 copy-done.9
  94.1 1.8 %fusion.1 = (bf16[71942]{0:T(1024)(128)(2,1)}, f32[71942]{0:T(1024)S(1)}, f32[71942]{0:T(1024)}) fusion(f32[71942]{0:T(1024)S(1)} %copy-done.3, f32[72704]{0:T(1024)} %bitcast.14, f32[71942]{0:T(1024)S(1)} %copy-done.9), kind=kLoop, calls=%fused_computation.10 | loop fusion | flops 503594 | bytes 1582724 | tf_op jit(solution)/shard_map/convert_element_type | solution.py:657
  95.9 0.0 copy-done.4
  95.9 0.0 copy-done.10
  95.9 0.9 multiply_add_fusion.3
  96.8 0.0 copy-done
  96.8 0.0 copy-done.6
  96.8 0.0 copy-done.8
  96.8 0.0 copy-start.1
  96.8 0.0 copy-start.7
  96.8 1.8 %fusion = (bf16[2,72193]{1,0:T(2,128)(2,1)}, f32[2,72193]{1,0:T(2,128)S(1)}, f32[2,72193]{1,0:T(2,128)}) fusion(f32[2,72193]{1,0:T(2,128)S(1)} %copy-done, f32[2,72320]{1,0:T(2,128)S(1)} %copy-done.8, f32[2,72193]{1,0:T(2,128)S(1)} %copy-done.6), kind=kLoop, calls=%fused_computation.9 | loop fusion | flops 1010702 | bytes 3176492 | tf_op jit(solution)/shard_map/convert_element_type | solution.py:657
  98.6 0.0 copy-done.5
  98.6 0.0 copy-done.1
  98.6 0.0 copy-done.7
  98.7 1.9 %multiply_add_fusion = (f32[2,72193]{1,0:T(2,128)}, f32[2,72193]{1,0:T(2,128)}) fusion(f32[2,72193]{1,0:T(2,128)S(1)} %copy-done.1, f32[2,72193]{1,0:T(2,128)S(1)} %get-tuple-element.25, f32[2,72193]{1,0:T(2,128)S(1)} %copy-done.7), kind=kLoop, calls=%fused_computation | loop fusion | flops 866316 | bytes 2887720 | tf_op jit(solution)/shard_map/add | solution.py:656
  (5 shorter events, 0.0 us)
Async XLA Ops:
  0.6 93.4 %copy-start.3 = (f32[71942]{0:T(1024)S(1)}, f32[71942]{0:T(1024)}, u32[]{:S(2)}) copy-start(f32[71942]{0:T(1024)} %actor_hbm.1) | copy-start | bytes 863308
  0.7 93.4 %copy-start.9 = (f32[71942]{0:T(1024)S(1)}, f32[71942]{0:T(1024)}, u32[]{:S(2)}) copy-start(f32[71942]{0:T(1024)} %param.18) | copy-start | bytes 863308
  90.2 5.6 %copy-start.4 = (f32[71942]{0:T(1024)S(1)}, f32[71942]{0:T(1024)}, u32[]{:S(2)}) copy-start(f32[71942]{0:T(1024)} %actor_t_hbm.1) | copy-start | bytes 863308
  90.3 5.6 %copy-start.10 = (f32[71942]{0:T(1024)S(1)}, f32[71942]{0:T(1024)}, u32[]{:S(2)}) copy-start(f32[71942]{0:T(1024)} %param.20) | copy-start | bytes 863308
  92.8 4.0 %copy-start = (f32[2,72193]{1,0:T(2,128)S(1)}, f32[2,72193]{1,0:T(2,128)}, u32[]{:S(2)}) copy-start(f32[2,72193]{1,0:T(2,128)} %critic_hbm.1) | copy-start | bytes 1732636
  92.8 4.0 %copy-start.6 = (f32[2,72193]{1,0:T(2,128)S(1)}, f32[2,72193]{1,0:T(2,128)}, u32[]{:S(2)}) copy-start(f32[2,72193]{1,0:T(2,128)} %param.19) | copy-start | bytes 1732636
  92.8 4.0 %copy-start.8 = (f32[2,72320]{1,0:T(2,128)S(1)}, f32[2,72320]{1,0:T(2,128)}, u32[]{:S(2)}) copy-start(f32[2,72320]{1,0:T(2,128)} %get-tuple-element.23) | copy-start | bytes 1735684
  95.9 2.8 %copy-start.5 = (f32[71942]{0:T(1024)}, f32[71942]{0:T(1024)S(1)}, u32[]{:S(2)}) copy-start(f32[71942]{0:T(1024)S(1)} %get-tuple-element.28) | copy-start | bytes 863308
  96.8 1.8 %copy-start.1 = (f32[2,72193]{1,0:T(2,128)S(1)}, f32[2,72193]{1,0:T(2,128)}, u32[]{:S(2)}) copy-start(f32[2,72193]{1,0:T(2,128)} %critic_t_hbm.1) | copy-start | bytes 1732636
  96.8 1.8 %copy-start.7 = (f32[2,72193]{1,0:T(2,128)S(1)}, f32[2,72193]{1,0:T(2,128)}, u32[]{:S(2)}) copy-start(f32[2,72193]{1,0:T(2,128)} %param.21) | copy-start | bytes 1732636
  98.6 1.9 %copy-start.2 = (f32[2,72193]{1,0:T(2,128)}, f32[2,72193]{1,0:T(2,128)S(1)}, u32[]{:S(2)}) copy-start(f32[2,72193]{1,0:T(2,128)S(1)} %get-tuple-element.25) | copy-start | bytes 1732636

commit v3 on v2

--- a/solution.py
+++ b/solution.py
@@ -31,15 +31,21 @@
 NEXT = 25
 
 TILES_C = 565
-ROWS_A = 568
+W2_ROW, W2_END = 96, 1120
+REST = 1024
+STAT = 1130
 AT_ACTOR = 1136
-STAT = AT_ACTOR + 564
+ROWS_A = 563
 CHIPS = DEVS // 2
 CHUNK = 8
-HALF = CHIPS * CHUNK
-PACK = 4 * HALF
+PACK = AT_ACTOR + 2 * CHIPS * CHUNK
+GROUPS = ((0, CHIPS, 1), (REST, 7, 9), (AT_ACTOR, CHIPS, 1))
 TURN = 512
 WIDTH = 1024
+
+
+def critic_row(r):
+    return r - W2_ROW if W2_ROW <= r < W2_END else r + REST if r < W2_ROW else r
 
 
 def dot(a, b):
@@ -100,19 +106,17 @@
     rows_ref[s, :] = jnp.transpose(v)
 
 
-def pick_rows(index_ref, rows_ref, picked_ref, x_ref):
+def pick_rows(block, width, index_ref, rows_ref, picked_ref, x_ref):
     ones = lax.broadcasted_iota(jnp.int32, (8, 128), 0) == (ONE - 40)
-
-    def body(c, carry):
+    tiles = width // 128
+    for t in range(tiles):
+        c = block * tiles + t
         for d in range(DEVS):
-            picked_ref[d : d + 1, :] = rows_ref[pl.ds(index_ref[c, d], 1), :]
-        turned = jnp.transpose(picked_ref[...])
+            picked_ref[t, d : d + 1, :] = rows_ref[pl.ds(index_ref[c, d], 1), :]
+        turned = jnp.transpose(picked_ref[t])
         s = pl.ds(pl.multiple_of(c * 128, 128), 128)
         x_ref[0:40, s] = turned[0:40]
         x_ref[40:48, s] = jnp.where(ones, 1.0, turned[40:48])
-        return carry
-
-    lax.fori_loop(0, CAP, body, 0)
 
 
 def put_square(net, w2, w2f_ref, w2b_ref):
@@ -378,18 +382,18 @@
         for half in range(2):
             s = slice(128 * half, 128 * (half + 1))
             at = c + 2 * half
-            pack_ref[pl.ds(at, OBS + ACT, stride=4), :] = g1[: OBS + ACT, s]
-            pack_ref[at + 92 : at + 93, :] = g1[ONE : ONE + 1, s]
-            pack_ref[pl.ds(at + 96, UNITS, stride=4), :] = g2_ref[c, :, s]
+            pack_ref[pl.ds(REST + at, OBS + ACT, stride=4), :] = g1[: OBS + ACT, s]
+            pack_ref[REST + at + 92 : REST + at + 93, :] = g1[ONE : ONE + 1, s]
+            pack_ref[pl.ds(at, UNITS, stride=4), :] = g2_ref[c, :, s]
             pack_ref[at + 1120 : at + 1121, :] = b2[:, s]
             pack_ref[at + 1124 : at + 1125, :] = w3[:, s]
         pack_ref[c + 1128 : c + 1129, :] = jnp.where(lane == 0, sums[2 + c : 3 + c], 0.0)
-    pack_ref[2 * TILES_C : AT_ACTOR, :] = jnp.zeros((AT_ACTOR - 2 * TILES_C, 128), f32)
+    pack_ref[STAT : STAT + 1, :] = jnp.where(lane == 0, sums[0:1], jnp.where(lane == 1, sums[1:2], 0.0))
+    pack_ref[STAT + 1 : AT_ACTOR, :] = jnp.zeros((AT_ACTOR - STAT - 1, 128), f32)
 
 
 def pack_actor(pack_ref, grads):
     g2_ref, g1_ref, g3a_ref, db2_ref, dw3_ref, st_ref = grads
-    lane = lax.broadcasted_iota(jnp.int32, (1, 128), 1)
     sums = jnp.sum(st_ref[...], 1, keepdims=True)
     g1 = g1_ref[A, :FEAT, :] + g1_ref[A, FEAT:, :]
     b2 = lane_sums(db2_ref[A])[0:1]
@@ -403,9 +407,7 @@
     pack_ref[o + 550 : o + 562, :] = head_back(g3a_ref[:8, :] + g3a_ref[8:, :])[:12]
     e = lax.broadcasted_iota(jnp.int32, (8, 128), 1) == lax.broadcasted_iota(jnp.int32, (8, 128), 0) - 1
     pack_ref[o + 562 : o + 563, :] = jnp.sum(jnp.where(e, sums[8:16], 0.0), 0, keepdims=True)
-    pack_ref[o + 563 : STAT, :] = jnp.zeros((STAT - o - 563, 128), f32)
-    pack_ref[STAT : STAT + 1, :] = jnp.where(lane == 0, sums[0:1], jnp.where(lane == 1, sums[1:2], 0.0))
-    pack_ref[STAT + 1 : PACK, :] = jnp.zeros((PACK - STAT - 1, 128), f32)
+    pack_ref[o + ROWS_A : PACK, :] = jnp.zeros((PACK - o - ROWS_A, 128), f32)
 
 
 WEIGHTS = [
@@ -436,15 +438,22 @@
 
 
 class Sum:
-    def __init__(self, g, shard_size, pack_ref, buffers, sems):
+    def __init__(self, g, shard_size, pack_ref, total_ref, buffers, sems):
         group, shard = lax.axis_index("group"), lax.axis_index("shard")
-        self.g, self.per = g, shard_size // 2
+        self.first, self.owners, self.apart = GROUPS[g]
+        self.rows = self.owners * CHUNK
+        self.per = shard_size // 2
         self.core = lax.rem(shard, 2)
         self.chip = group * self.per + shard // 2
         self.sibling = (group, shard + 1 - 2 * self.core)
-        self.pack_ref = pack_ref
-        self.other, self.half, self.parts, self.mine, self.whole = (b.at[g] for b in buffers)
+        self.pack_ref, self.total_ref = pack_ref, total_ref
+        self.other, self.half, self.parts, self.mine, self.whole = buffers
         self.sems = sems.at[g]
+        if self.owners == CHIPS:
+            self.own, self.owner = self.chip, None
+        else:
+            self.own = self.chip // self.apart
+            self.owner = (lax.rem(self.chip, self.apart) == 0) & (self.own < self.owners)
 
     def remote(self, src, dst, n, to):
         return pltpu.make_async_remote_copy(
@@ -456,37 +465,79 @@
             device_id_type=MESH,
         )
 
-    def to_all(self, src_of, dst, n):
-        def send(k, carry):
-            peer = lax.rem(self.chip + k, CHIPS)
-            to = (peer // self.per, lax.rem(peer, self.per) * 2 + self.core)
-            self.remote(src_of(peer), dst, n, to).start()
-            return carry
-
-        lax.fori_loop(1, CHIPS, send, 0)
+    def at(self, chip):
+        return (chip // self.per, lax.rem(chip, self.per) * 2 + self.core)
+
+    def if_owner(self, yes, no):
+        if self.owner is None:
+            yes()
+        else:
+            pl.when(self.owner)(yes)
+            pl.when(jnp.logical_not(self.owner))(no)
 
     def swap(self):
-        give = pl.multiple_of(self.g * 2 * HALF + (1 - self.core) * HALF, HALF)
-        return self.remote(self.pack_ref.at[pl.ds(give, HALF)], self.other, 0, self.sibling)
+        give = pl.multiple_of(self.first + (1 - self.core) * self.rows, 8)
+        return self.remote(self.pack_ref.at[pl.ds(give, self.rows)], self.other, 0, self.sibling)
 
     def scatter(self):
-        keep = pl.multiple_of(self.g * 2 * HALF + self.core * HALF, HALF)
-        total = self.pack_ref[pl.ds(keep, HALF), :] + self.other[...]
-        self.half[...] = total.reshape(CHIPS, CHUNK, 128)
-        self.to_all(lambda peer: self.half.at[peer], self.parts.at[self.chip], 1)
+        keep = pl.multiple_of(self.first + self.core * self.rows, 8)
+        total = self.pack_ref[pl.ds(keep, self.rows), :] + self.other[...]
+        self.half[...] = total.reshape(self.owners, CHUNK, 128)
+        if self.owner is None:
+
+            def send(k, carry):
+                peer = lax.rem(self.chip + k, CHIPS)
+                self.remote(self.half.at[peer], self.parts.at[self.chip], 1, self.at(peer)).start()
+                return carry
+
+            lax.fori_loop(1, CHIPS, send, 0)
+        else:
+            for k in range(self.owners):
+
+                @pl.when(self.chip != k * self.apart)
+                def _():
+                    self.remote(self.half.at[k], self.parts.at[self.chip], 1, self.at(k * self.apart)).start()
 
     def spread(self):
-        drain(self.half, self.sems.at[2], CHIPS - 1)
-        drain(self.parts, self.sems.at[3], CHIPS - 1)
-        self.parts[pl.ds(self.chip, 1)] = self.half[pl.ds(self.chip, 1)]
-        self.mine[...] = jnp.sum(self.parts[...], 0)
-        self.to_all(lambda peer: self.mine, self.whole.at[self.core, self.chip], 2)
+        def yes():
+            drain(self.half, self.sems.at[2], self.owners - 1)
+            drain(self.parts, self.sems.at[3], CHIPS - 1)
+            self.parts[pl.ds(self.chip, 1)] = self.half[pl.ds(self.own, 1)]
+            self.mine[...] = jnp.sum(self.parts[...], 0)
+
+            def send(k, carry):
+                peer = lax.rem(self.chip + k, CHIPS)
+                self.remote(self.mine, self.whole.at[self.core, self.own], 2, self.at(peer)).start()
+                return carry
+
+            lax.fori_loop(1, CHIPS, send, 0)
+
+        self.if_owner(yes, lambda: drain(self.half, self.sems.at[2], self.owners))
 
     def back(self):
-        drain(self.parts, self.sems.at[4], CHIPS - 1)
-        drain(self.whole.at[0], self.sems.at[5], CHIPS - 1)
-        self.whole[pl.ds(self.core, 1), pl.ds(self.chip, 1)] = self.mine[...][None, None]
+        def yes():
+            drain(self.parts, self.sems.at[4], CHIPS - 1)
+            drain(self.whole.at[0], self.sems.at[5], self.owners - 1)
+            self.whole[pl.ds(self.core, 1), pl.ds(self.own, 1)] = self.mine[...][None, None]
+
+        self.if_owner(yes, lambda: drain(self.whole.at[0], self.sems.at[5], self.owners))
         return self.remote(self.whole.at[self.core], self.whole.at[self.core], 3, self.sibling)
+
+    def store(self):
+        self.total_ref[self.first : self.first + 2 * self.rows, :] = self.whole[...].reshape(2 * self.rows, 128)
+
+
+def sum_buffers():
+    out = []
+    for _, owners, _ in GROUPS:
+        out += [
+            pltpu.VMEM((owners * CHUNK, 128), f32),
+            pltpu.VMEM((owners, CHUNK, 128), f32),
+            pltpu.VMEM((CHIPS, CHUNK, 128), f32),
+            pltpu.VMEM((CHUNK, 128), f32),
+            pltpu.VMEM((2, owners, CHUNK, 128), f32),
+        ]
+    return out
 
 
 def step_kernel(
@@ -523,16 +574,13 @@
     flat_ref,
     pad_ref,
     pack_ref,
-    other,
-    half,
-    parts,
-    mine,
-    whole,
     sems,
     *scratch,
 ):
-    weights, grads = scratch[: len(WEIGHTS)], scratch[len(WEIGHTS) :]
+    weights, grads = scratch[: len(WEIGHTS)], scratch[len(WEIGHTS) : len(WEIGHTS) + len(GRADS)]
+    buffers = scratch[len(WEIGHTS) + len(GRADS) :]
     w1_ref, w2f_ref, w2b_ref, b2_ref, w3_ref, b3_ref, w3t_ref, w3b_ref, b3a_ref, w1a_ref = weights
+    blocks = N // width
     me = lax.axis_index("group") * shard_size + lax.axis_index("shard")
 
     def device(k):
@@ -543,14 +591,14 @@
         pltpu.make_async_copy(src, dst, in_sems.at[n])
         for n, (src, dst) in enumerate(
             (
+                (table_hbm, table_ref),
+                (index_hbm, index_ref),
+                (critic_hbm, critic_ref),
+                (actor_hbm, actor_ref),
+                (count_hbm, count_ref),
                 (noise_hbm, noise_ref),
                 (critic_t_hbm, critic_t_ref),
                 (actor_t_hbm, actor_t_ref),
-                (critic_hbm, critic_ref),
-                (actor_hbm, actor_ref),
-                (count_hbm, count_ref),
-                (table_hbm, table_ref),
-                (index_hbm, index_ref),
             )
         )
     ]
@@ -567,21 +615,27 @@
     for ref in grads:
         ref[...] = jnp.zeros_like(ref)
     loads[0].wait()
+
+    def turn(i, carry):
+        turn_table(i, table_ref, rows_ref)
+        return carry
+
+    lax.fori_loop(0, R_DEV // TURN, turn, 0)
+    loads[1].wait()
+    pick_rows(0, width, index_ref, rows_ref, picked_ref, x_ref)
+    loads[2].wait()
+    prepare_critics(
+        critic_ref, flat_ref, pad_ref, C0, w1_ref, w2f_ref, w2b_ref, b2_ref, w3_ref, b3_ref, w1a_ref
+    )
+    loads[3].wait()
+    prepare_actor(
+        A, actor_ref, flat_ref, pad_ref, w1_ref, w2f_ref, w2b_ref, b2_ref, w3t_ref, w3b_ref, b3a_ref
+    )
+    loads[4].wait()
+    loads[5].wait()
     turn_noise(noise_ref, q_ref, nsend)
-    for n, first, ref in ((1, T0, critic_t_ref), (3, C0, critic_ref)):
-        loads[n].wait()
-        prepare_critics(
-            ref, flat_ref, pad_ref, first, w1_ref, w2f_ref, w2b_ref, b2_ref, w3_ref, b3_ref, w1a_ref
-        )
-    for n, net, ref in ((2, AT, actor_t_ref), (4, A, actor_ref)):
-        loads[n].wait()
-        prepare_actor(net, ref, flat_ref, pad_ref, w1_ref, w2f_ref, w2b_ref, b2_ref, w3t_ref, w3b_ref, b3a_ref)
-    for n in (5, 6, 7):
-        loads[n].wait()
-
-    pl.semaphore_wait(barrier, DEVS - 1)
-
-    def send(k):
+
+    def send(k, carry):
         peer, to = device(k)
         pltpu.make_async_remote_copy(
             src_ref=nsend.at[peer],
@@ -591,21 +645,34 @@
             device_id=to,
             device_id_type=MESH,
         ).start()
-
-    steps = R_DEV // TURN
-    each = DEVS // steps
-
-    def turn(i, carry):
-        turn_table(i, table_ref, rows_ref)
-        for j in range(each):
-            send(1 + i * each + j)
         return carry
 
-    lax.fori_loop(0, steps - 1, turn, 0)
-    turn_table(steps - 1, table_ref, rows_ref)
-    for j in range(each - 1):
-        send(1 + (steps - 1) * each + j)
-    pick_rows(index_ref, rows_ref, picked_ref, x_ref)
+    def actors(i, carry):
+        pick_rows(lax.rem(i + 1, blocks), width, index_ref, rows_ref, picked_ref, x_ref)
+        actor_block(i, width, x_ref, count_ref, weights, grads)
+
+        @pl.when(i == 0)
+        def _():
+            pl.semaphore_wait(barrier, DEVS - 1)
+            lax.fori_loop(1, DEVS, send, 0)
+
+        return carry
+
+    lax.fori_loop(0, blocks, actors, 0)
+    pack_actor(pack_ref, grads)
+    wide, rest, early = (
+        Sum(g, shard_size, pack_ref, sum_ref, buffers[5 * g : 5 * g + 5], sems) for g in range(3)
+    )
+    early.swap().start()
+
+    loads[6].wait()
+    prepare_critics(
+        critic_t_ref, flat_ref, pad_ref, T0, w1_ref, w2f_ref, w2b_ref, b2_ref, w3_ref, b3_ref, w1a_ref
+    )
+    loads[7].wait()
+    prepare_actor(
+        AT, actor_t_ref, flat_ref, pad_ref, w1_ref, w2f_ref, w2b_ref, b2_ref, w3t_ref, w3b_ref, b3a_ref
+    )
     drain(nsend, noise_sems.at[0], DEVS - 1)
     drain(nrecv, noise_sems.at[1], DEVS - 1)
     nrecv[pl.ds(me, 1)] = nsend[pl.ds(me, 1)]
@@ -613,40 +680,41 @@
 
     def critics(i, carry):
         critic_block(i, width, x_ref, nz_ref, count_ref, weights, prio_ref, grads)
+
+        @pl.when(i == 0)
+        def _():
+            early.swap().wait()
+            early.scatter()
+
+        @pl.when(i == 1)
+        def _():
+            early.spread()
+
+        @pl.when(i == 2)
+        def _():
+            early.back().start()
+
         return carry
 
-    blocks = N // width
     lax.fori_loop(0, blocks, critics, 0)
     pack_critics(pack_ref, grads)
-
-    buffers = (other, half, parts, mine, whole)
-    early = Sum(0, shard_size, pack_ref, buffers, sems)
-    late = Sum(1, shard_size, pack_ref, buffers, sems)
-    swap = early.swap()
-    swap.start()
-    back = early.back
-    for i in range(blocks):
-        actor_block(i, width, x_ref, count_ref, weights, grads)
-        if i == 0:
-            swap.wait()
-            early.scatter()
-        elif i == 1:
-            early.spread()
-        elif i == 2:
-            back = early.back()
-            back.start()
-    pack_actor(pack_ref, grads)
-    swap = late.swap()
-    swap.start()
-    back.wait()
-    swap.wait()
-    late.scatter()
-    sum_ref[: 2 * HALF, :] = whole[0].reshape(2 * HALF, 128)
-    late.spread()
-    back = late.back()
-    back.start()
-    back.wait()
-    sum_ref[2 * HALF :, :] = whole[1].reshape(2 * HALF, 128)
+    late = (wide, rest)
+    for part in late:
+        part.swap().start()
+    early.remote(early.whole.at[early.core], early.whole.at[early.core], 3, early.sibling).wait()
+    for part in late:
+        part.swap().wait()
+        part.scatter()
+    early.store()
+    for part in late:
+        part.spread()
+    backs = [part.back() for part in late]
+    for copy in backs:
+        copy.start()
+    for copy in backs:
+        copy.wait()
+    for part in late:
+        part.store()
 
 
 def update(weight, grad, momentum, average, target):
@@ -657,14 +725,42 @@
     return (weight_new, momentum_new, average_new, target_new, weight_new.astype(bf))
 
 
-def grads_kernel(sum_ref, prio_in, ga_ref, gc_ref, stat_ref, prio_ref):
+def update_kernel(sum_ref, prio_in, *refs):
+    ins, (stat_ref, prio_ref), outs, grad_ref = refs[:8], refs[8:10], refs[10:20], refs[20]
     stat = sum_ref[STAT : STAT + 1, :]
     factor = (1.0 / SCALE) / stat[:, 1:2]
     stat_ref[...] = stat
     prio_ref[...] = prio_in[...]
-    ga_ref[...] = sum_ref[AT_ACTOR : AT_ACTOR + ROWS_A, :] * factor
     for t in range(TILES_C):
-        gc_ref[:, 128 * t : 128 * (t + 1)] = sum_ref[2 * t : 2 * t + 2, :] * factor
+        r = critic_row(2 * t)
+        grad_ref[:, 128 * t : 128 * (t + 1)] = sum_ref[r : r + 2, :] * factor
+
+    def critics(s):
+        values = update(ins[1][:, s], grad_ref[:, s], ins[3][:, s], ins[5][:, s], ins[7][:, s])
+        for ref, value in zip(outs[1::2], values):
+            ref[:, s] = value
+
+    def actor(s, grad):
+        values = update(ins[0][s], grad, ins[2][s], ins[4][s], ins[6][s])
+        for ref, value in zip(outs[0::2], values):
+            ref[s] = value
+
+    step = 1024
+
+    def body(i, carry):
+        critics(pl.ds(pl.multiple_of(i * step, step), step))
+        r = pl.multiple_of(AT_ACTOR + 8 * i, 8)
+        actor(pl.ds(pl.multiple_of(i * step, step), step), (sum_ref[pl.ds(r, 8), :] * factor).reshape(step))
+        return carry
+
+    lax.fori_loop(0, PA // step, body, 0)
+    done = PA // step * step
+    critics(pl.ds(done, PC - done))
+    r = AT_ACTOR + done // 128
+    more = (PA - done) // 128
+    actor(pl.ds(done, 128 * more), (sum_ref[r : r + more, :] * factor).reshape(128 * more))
+    done += 128 * more
+    actor(pl.ds(done, ACT), (sum_ref[r + more : r + more + 1, :ACT] * factor).reshape(ACT))
 
 
 def local(
@@ -700,7 +796,7 @@
             pltpu.VMEM((2, PC), f32),
             pltpu.SemaphoreType.DMA((8,)),
             pltpu.VMEM((R_DEV, 128), f32),
-            pltpu.VMEM((128, 128), f32),
+            pltpu.VMEM((WIDTH // 128, 128, 128), f32),
             pltpu.VMEM((256, 128), f32),
             pltpu.VMEM((DEVS, 2, 128), f32),
             pltpu.VMEM((DEVS, 2, 128), f32),
@@ -710,15 +806,11 @@
             pltpu.VMEM((2 * TILES_C + 6, 128), f32),
             pltpu.VMEM((FEAT, 256), f32),
             pltpu.VMEM((PACK, 128), f32),
-            pltpu.VMEM((2, HALF, 128), f32),
-            pltpu.VMEM((2, CHIPS, CHUNK, 128), f32),
-            pltpu.VMEM((2, CHIPS, CHUNK, 128), f32),
-            pltpu.VMEM((2, CHUNK, 128), f32),
-            pltpu.VMEM((2, 2, CHIPS, CHUNK, 128), f32),
-            pltpu.SemaphoreType.DMA((2, 8)),
+            pltpu.SemaphoreType.DMA((3, 8)),
         ]
         + WEIGHTS
-        + GRADS,
+        + GRADS
+        + sum_buffers(),
         compiler_params=pltpu.CompilerParams(
             collective_id=0, has_side_effects=True, vmem_limit_bytes=56 << 20
         ),
@@ -733,24 +825,30 @@
         critic,
         critic_target,
     )
-    ga, gc, stat, prio = pl.pallas_call(
-        grads_kernel,
-        out_shape=(
-            SDS((ROWS_A, 128), f32),
-            SDS((2, TILES_C * 128), f32),
-            SDS((1, 128), f32),
-            SDS((CAP, DEVS), f32),
-        ),
-        in_specs=[VM, VM],
-        out_specs=(VM, VM, VM, VM),
-        name="unpack_grads",
-    )(total, prio)
-    actor_out = update(actor, ga.reshape(-1)[:PA], actor_momentum, actor_average, actor_target)
-    critic_out = update(critic, gc[:, :PC], critic_momentum, critic_average, critic_target)
-    outs = [stat[0, :2], prio.T[None]]
-    for one, two in zip(actor_out, critic_out):
-        outs += [one, two]
-    return tuple(outs)
+    shapes = [SDS((1, 128), f32), SDS((CAP, DEVS), f32)]
+    for kind in (f32, f32, f32, f32, bf):
+        shapes += [SDS((PA,), kind), SDS((2, PC), kind)]
+    stat, prio, *outs = pl.pallas_call(
+        update_kernel,
+        out_shape=tuple(shapes),
+        in_specs=[VM] * 10,
+        out_specs=(VM,) * 12,
+        scratch_shapes=[pltpu.VMEM((2, TILES_C * 128), f32)],
+        compiler_params=pltpu.CompilerParams(vmem_limit_bytes=24 << 20),
+        name="update",
+    )(
+        total,
+        prio,
+        actor,
+        critic,
+        actor_momentum,
+        critic_momentum,
+        actor_average,
+        critic_average,
+        actor_target,
+        critic_target,
+    )
+    return (stat[0, :2], prio.T[None], *outs)
 
 
 def solution(mesh):

time: 101 us -> 98.5 us (0.975)
  other arithmetic: 6.4 us -> 0 us
  local copies, waits for them, and re-layouts: 1.35 us -> 3.45 us
  Pallas kernels: 92.1 us -> 94 us
    convert_element_type x2 -> x0, other arithmetic: 3.59 us -> none  [update(): weight_new.astype(bf)]
    unnamed x22 -> x20, local copies, waits for them, and re-layouts: 0.05 us -> 2.94 us
    add x2 -> x0, other arithmetic: 2.81 us -> none  [update(): target_new = 0.005 * weight_new + 0.995 * target]
    pallas_call x1, Pallas kernels: 2.5 us -> 4 us  [local(): pl.pallas_call(update_kernel, out_shape=tuple(shapes), in_specs=[VM] * 10...]
where the time goes in v3:
time: 98.5 us; the launch traced here: 98.3 us
  Pallas kernels  94 us (95%)
  local copies, waits for them, and re-layouts  3.45 us (4%)
    pallas_call x1, Pallas kernels, local(): pl.pallas_call(functools.partial(step_kernel, group_size, shard_size, WID...  90 us
    pallas_call x1, Pallas kernels, local(): pl.pallas_call(update_kernel, out_shape=tuple(shapes), in_specs=[VM] * 10...  4 us
    unnamed x20, local copies, waits for them, and re-layouts  2.94 us

profile of v3, /device:TPU:1, one launch (start us, length us, event | category | flops | bytes accessed | tf_op | source)
XLA Modules:
  0.0 98.3 jit_solution(3134133386799861465)
XLA Ops:
  0.6 0.0 copy-start
  0.7 0.0 copy-start.1
  0.7 0.0 copy-start.2
  0.7 0.0 copy-start.3
  0.7 0.0 copy-start.5
  0.7 0.0 copy-start.6
  0.7 0.0 copy-start.7
  0.7 90.0 %td3_step.1 = (f32[32,128]{1,0:T(8,128)}, f32[2160,128]{1,0:T(8,128)}) custom-call(f32[42,8192]{1,0:T(8,128)} %bitcast.12, s32[32,128]{1,0:T(8,128)} %bitcast.14, f32[6,32,128]{2,1,0:T(8,128)} %bitcast.13, s32[1,128]{1,0:T(1,128)} %count_hbm.1, f32[71942]{0:T(1024)} %refs_0_.1, f32[71942]{0:T(1024)} %refs_6_.1, f32[2,72193]{1,0:T(2,128)} %refs_1_.1, ...), custom_call_target="tpu_custom_call" | custom-call | tf_op jit(solution)/shard_map/td3_step/pallas_call | solution.py:783
  90.8 0.0 copy-done
  90.8 0.0 copy-done.1
  90.8 0.0 copy-done.2
  90.8 0.0 copy-done.3
  90.8 0.0 copy-done.5
  90.8 0.0 copy-done.6
  90.8 0.0 copy-done.7
  90.8 0.0 copy-start.4
  90.9 1.2 %copy-done.4 = f32[2160,128]{1,0:T(8,128)S(1)} copy-done((f32[2160,128]{1,0:T(8,128)S(1)}, f32[2160,128]{1,0:T(8,128)}, u32[]{:S(2)}) %copy-start.4) | copy-done | bytes 1105944
  92.1 0.0 copy-start.8
  92.1 1.0 copy-done.8
  93.1 0.0 copy-start.9
  93.1 0.7 copy-done.9
  93.8 4.0 %update.1 = (f32[1,128]{1,0:T(1,128)S(1)}, f32[32,128]{1,0:T(8,128)}, f32[71942]{0:T(1024)}, f32[2,72193]{1,0:T(2,128)}, f32[71942]{0:T(1024)}, /*index=5*/f32[2...) custom-call(f32[2160,128]{1,0:T(8,128)S(1)} %copy-done.4, ...), custom_call_target="tpu_custom_call" | custom-call | tf_op jit(solution)/shard_map/update/pallas_call | solution.py:831
  97.8 0.5 slice_bitcast_fusion
Async XLA Ops:
  0.6 90.1 %copy-start = (f32[2,72193]{1,0:T(2,128)S(1)}, f32[2,72193]{1,0:T(2,128)}, u32[]{:S(2)}) copy-start(f32[2,72193]{1,0:T(2,128)} %refs_1_.1) | copy-start | bytes 1732636
  0.7 90.1 %copy-start.1 = (f32[2,72193]{1,0:T(2,128)S(1)}, f32[2,72193]{1,0:T(2,128)}, u32[]{:S(2)}) copy-start(f32[2,72193]{1,0:T(2,128)} %refs_7_.1) | copy-start | bytes 1732636
  0.7 90.1 %copy-start.2 = (f32[71942]{0:T(1024)S(1)}, f32[71942]{0:T(1024)}, u32[]{:S(2)}) copy-start(f32[71942]{0:T(1024)} %refs_0_.1) | copy-start | bytes 863308
  0.7 90.1 %copy-start.3 = (f32[71942]{0:T(1024)S(1)}, f32[71942]{0:T(1024)}, u32[]{:S(2)}) copy-start(f32[71942]{0:T(1024)} %refs_6_.1) | copy-start | bytes 863308
  0.7 90.1 %copy-start.5 = (f32[2,72193]{1,0:T(2,128)S(1)}, f32[2,72193]{1,0:T(2,128)}, u32[]{:S(2)}) copy-start(f32[2,72193]{1,0:T(2,128)} %refs_3_.1) | copy-start | bytes 1732636
  0.7 90.1 %copy-start.6 = (f32[2,72193]{1,0:T(2,128)S(1)}, f32[2,72193]{1,0:T(2,128)}, u32[]{:S(2)}) copy-start(f32[2,72193]{1,0:T(2,128)} %refs_5_.1) | copy-start | bytes 1732636
  0.7 90.1 %copy-start.7 = (f32[71942]{0:T(1024)S(1)}, f32[71942]{0:T(1024)}, u32[]{:S(2)}) copy-start(f32[71942]{0:T(1024)} %refs_2_.1) | copy-start | bytes 863308
  90.8 1.2 %copy-start.4 = (f32[2160,128]{1,0:T(8,128)S(1)}, f32[2160,128]{1,0:T(8,128)}, u32[]{:S(2)}) copy-start(f32[2160,128]{1,0:T(8,128)} %get-tuple-element.26.sum_ref) | copy-start | bytes 3317764
  92.1 1.0 copy-start.8
  93.1 0.7 copy-start.9

commit v4 on v3

--- a/solution.py
+++ b/solution.py
@@ -31,21 +31,18 @@
 NEXT = 25
 
 TILES_C = 565
-W2_ROW, W2_END = 96, 1120
-REST = 1024
 STAT = 1130
-AT_ACTOR = 1136
 ROWS_A = 563
 CHIPS = DEVS // 2
-CHUNK = 8
-PACK = AT_ACTOR + 2 * CHIPS * CHUNK
-GROUPS = ((0, CHIPS, 1), (REST, 7, 9), (AT_ACTOR, CHIPS, 1))
+CHUNKS = (9, 5)
+AT_ACTOR = 2 * CHIPS * CHUNKS[0]
+PACK = AT_ACTOR + 2 * CHIPS * CHUNKS[1]
 TURN = 512
 WIDTH = 1024
-
-
-def critic_row(r):
-    return r - W2_ROW if W2_ROW <= r < W2_END else r + REST if r < W2_ROW else r
+STEPS = sorted(
+    ((z, x, y) for z in range(4) for x in range(4) for y in range(4)),
+    key=lambda step: -sum(min(n, 4 - n) for n in step),
+)[:-1]
 
 
 def dot(a, b):
@@ -106,17 +103,18 @@
     rows_ref[s, :] = jnp.transpose(v)
 
 
-def pick_rows(block, width, index_ref, rows_ref, picked_ref, x_ref):
-    ones = lax.broadcasted_iota(jnp.int32, (8, 128), 0) == (ONE - 40)
+def pick_rows(block, width, index_ref, rows_ref, picked_ref):
     tiles = width // 128
     for t in range(tiles):
-        c = block * tiles + t
         for d in range(DEVS):
-            picked_ref[t, d : d + 1, :] = rows_ref[pl.ds(index_ref[c, d], 1), :]
-        turned = jnp.transpose(picked_ref[t])
-        s = pl.ds(pl.multiple_of(c * 128, 128), 128)
-        x_ref[0:40, s] = turned[0:40]
-        x_ref[40:48, s] = jnp.where(ones, 1.0, turned[40:48])
+            picked_ref[t, d : d + 1, :] = rows_ref[pl.ds(index_ref[block * tiles + t, d], 1), :]
+
+
+def turn_rows(width, picked_ref):
+    parts = [jnp.transpose(picked_ref[t])[:FEAT] for t in range(width // 128)]
+    x = jnp.concatenate(parts, 1)
+    ones = lax.broadcasted_iota(jnp.int32, (8, width), 0) == (ONE - 40)
+    return jnp.concatenate([x[:40], jnp.where(ones, 1.0, x[40:])], 0)
 
 
 def put_square(net, w2, w2f_ref, w2b_ref):
@@ -242,13 +240,13 @@
 
 
 class Step:
-    def __init__(self, i, width, x_ref, weights):
+    def __init__(self, i, width, x, weights):
         (
             self.w1, self.w2f, self.w2b, self.b2, self.w3, self.b3, self.w3t, self.w3b, self.b3a, self.w1a,
         ) = weights
         self.i, self.width = i, width
         self.lanes = pl.ds(pl.multiple_of(i * width, width), width)
-        self.x = x_ref[:, self.lanes]
+        self.x = x
         self.x3 = three(self.x)
         rows8 = lax.broadcasted_iota(jnp.int32, (8, width), 0)
         self.is_action = (rows8 >= 1) & (rows8 <= ACT)
@@ -288,10 +286,10 @@
         g1_ref[net] += dot_nt(left, jnp.concatenate([a, b], 1))
 
 
-def critic_block(i, width, x_ref, nz_ref, count_ref, weights, prio_ref, grads):
+def critic_block(i, width, x, nz_ref, count_ref, weights, prio_ref, grads):
     g2_ref, g1_ref, g3a_ref, db2_ref, dw3_ref, st_ref = grads
-    st = Step(i, width, x_ref, weights)
-    x, x3 = st.x, st.x3
+    st = Step(i, width, x, weights)
+    x3 = st.x3
 
     u, s = st.first(AT, x3)
     u, s = st.second(AT, three(s))
@@ -333,9 +331,9 @@
         st.weight_grads(net, h1, hi, lo, dh1 * d1, g2_ref, g1_ref)
 
 
-def actor_block(i, width, x_ref, count_ref, weights, grads):
+def actor_block(i, width, x, count_ref, weights, grads):
     g2_ref, g1_ref, g3a_ref, db2_ref, dw3_ref, st_ref = grads
-    st = Step(i, width, x_ref, weights)
+    st = Step(i, width, x, weights)
 
     u, s = st.first(A, st.x3)
     h1a, d1a = three(s), slope(u, s)
@@ -382,9 +380,9 @@
         for half in range(2):
             s = slice(128 * half, 128 * (half + 1))
             at = c + 2 * half
-            pack_ref[pl.ds(REST + at, OBS + ACT, stride=4), :] = g1[: OBS + ACT, s]
-            pack_ref[REST + at + 92 : REST + at + 93, :] = g1[ONE : ONE + 1, s]
-            pack_ref[pl.ds(at, UNITS, stride=4), :] = g2_ref[c, :, s]
+            pack_ref[pl.ds(at, OBS + ACT, stride=4), :] = g1[: OBS + ACT, s]
+            pack_ref[at + 92 : at + 93, :] = g1[ONE : ONE + 1, s]
+            pack_ref[pl.ds(at + 96, UNITS, stride=4), :] = g2_ref[c, :, s]
             pack_ref[at + 1120 : at + 1121, :] = b2[:, s]
             pack_ref[at + 1124 : at + 1125, :] = w3[:, s]
         pack_ref[c + 1128 : c + 1129, :] = jnp.where(lane == 0, sums[2 + c : 3 + c], 0.0)
@@ -437,23 +435,32 @@
     pltpu.make_async_copy(view, view, sem).wait()
 
 
+class Place:
+    def __init__(self):
+        group, shard = lax.axis_index("group"), lax.axis_index("shard")
+        self.core = lax.rem(shard, 2)
+        z, x, y = group // 4, lax.rem(group, 4), shard // 2
+        self.chip = group * 4 + y
+        self.sibling = (group, shard + 1 - 2 * self.core)
+        self.sibling_at = group * 8 + shard + 1 - 2 * self.core
+        self.me = group * 8 + shard
+        self.zs, self.xs, self.ys = ([lax.rem(v + n, 4) for n in range(4)] for v in (z, x, y))
+
+    def others(self, other_core=False):
+        core = 1 - self.core if other_core else self.core
+        for dz, dx, dy in STEPS:
+            group = self.zs[dz] * 4 + self.xs[dx]
+            yield group * 4 + self.ys[dy], (group, self.ys[dy] * 2 + core)
+
+
 class Sum:
-    def __init__(self, g, shard_size, pack_ref, total_ref, buffers, sems):
-        group, shard = lax.axis_index("group"), lax.axis_index("shard")
-        self.first, self.owners, self.apart = GROUPS[g]
-        self.rows = self.owners * CHUNK
-        self.per = shard_size // 2
-        self.core = lax.rem(shard, 2)
-        self.chip = group * self.per + shard // 2
-        self.sibling = (group, shard + 1 - 2 * self.core)
+    def __init__(self, place, g, pack_ref, total_ref, buffers, sems):
+        self.place, self.chunk = place, CHUNKS[g]
+        self.first = (0, AT_ACTOR)[g]
+        self.rows = CHIPS * self.chunk
         self.pack_ref, self.total_ref = pack_ref, total_ref
         self.other, self.half, self.parts, self.mine, self.whole = buffers
         self.sems = sems.at[g]
-        if self.owners == CHIPS:
-            self.own, self.owner = self.chip, None
-        else:
-            self.own = self.chip // self.apart
-            self.owner = (lax.rem(self.chip, self.apart) == 0) & (self.own < self.owners)
 
     def remote(self, src, dst, n, to):
         return pltpu.make_async_remote_copy(
@@ -465,84 +472,60 @@
             device_id_type=MESH,
         )
 
-    def at(self, chip):
-        return (chip // self.per, lax.rem(chip, self.per) * 2 + self.core)
-
-    def if_owner(self, yes, no):
-        if self.owner is None:
-            yes()
-        else:
-            pl.when(self.owner)(yes)
-            pl.when(jnp.logical_not(self.owner))(no)
-
     def swap(self):
-        give = pl.multiple_of(self.first + (1 - self.core) * self.rows, 8)
-        return self.remote(self.pack_ref.at[pl.ds(give, self.rows)], self.other, 0, self.sibling)
+        give = pl.multiple_of(self.first + (1 - self.place.core) * self.rows, 8)
+        return self.remote(self.pack_ref.at[pl.ds(give, self.rows)], self.other, 0, self.place.sibling)
 
     def scatter(self):
-        keep = pl.multiple_of(self.first + self.core * self.rows, 8)
+        keep = pl.multiple_of(self.first + self.place.core * self.rows, 8)
         total = self.pack_ref[pl.ds(keep, self.rows), :] + self.other[...]
-        self.half[...] = total.reshape(self.owners, CHUNK, 128)
-        if self.owner is None:
-
-            def send(k, carry):
-                peer = lax.rem(self.chip + k, CHIPS)
-                self.remote(self.half.at[peer], self.parts.at[self.chip], 1, self.at(peer)).start()
-                return carry
-
-            lax.fori_loop(1, CHIPS, send, 0)
-        else:
-            for k in range(self.owners):
-
-                @pl.when(self.chip != k * self.apart)
-                def _():
-                    self.remote(self.half.at[k], self.parts.at[self.chip], 1, self.at(k * self.apart)).start()
+        for j in range(self.chunk):
+            self.half[:, j, :] = total[CHIPS * j : CHIPS * (j + 1)]
+        chip = self.place.chip
+        for peer, device in self.place.others():
+            self.remote(self.half.at[peer], self.parts.at[chip], 1, device).start()
 
     def spread(self):
-        def yes():
-            drain(self.half, self.sems.at[2], self.owners - 1)
-            drain(self.parts, self.sems.at[3], CHIPS - 1)
-            self.parts[pl.ds(self.chip, 1)] = self.half[pl.ds(self.own, 1)]
-            self.mine[...] = jnp.sum(self.parts[...], 0)
-
-            def send(k, carry):
-                peer = lax.rem(self.chip + k, CHIPS)
-                self.remote(self.mine, self.whole.at[self.core, self.own], 2, self.at(peer)).start()
-                return carry
-
-            lax.fori_loop(1, CHIPS, send, 0)
-
-        self.if_owner(yes, lambda: drain(self.half, self.sems.at[2], self.owners))
+        chip = self.place.chip
+        drain(self.half, self.sems.at[2], CHIPS - 1)
+        drain(self.parts, self.sems.at[3], CHIPS - 1)
+        self.parts[pl.ds(chip, 1)] = self.half[pl.ds(chip, 1)]
+        self.mine[...] = jnp.sum(self.parts[...], 0)
+        for _, device in self.place.others():
+            self.remote(self.mine, self.whole.at[self.place.core, chip], 2, device).start()
+
+    def back_copy(self):
+        ref = self.whole.at[self.place.core]
+        return self.remote(ref, ref, 3, self.place.sibling)
 
     def back(self):
-        def yes():
-            drain(self.parts, self.sems.at[4], CHIPS - 1)
-            drain(self.whole.at[0], self.sems.at[5], self.owners - 1)
-            self.whole[pl.ds(self.core, 1), pl.ds(self.own, 1)] = self.mine[...][None, None]
-
-        self.if_owner(yes, lambda: drain(self.whole.at[0], self.sems.at[5], self.owners))
-        return self.remote(self.whole.at[self.core], self.whole.at[self.core], 3, self.sibling)
+        drain(self.parts, self.sems.at[4], CHIPS - 1)
+        drain(self.whole.at[0], self.sems.at[5], CHIPS - 1)
+        self.whole[pl.ds(self.place.core, 1), pl.ds(self.place.chip, 1)] = self.mine[...][None, None]
+        self.back_copy().start()
 
     def store(self):
-        self.total_ref[self.first : self.first + 2 * self.rows, :] = self.whole[...].reshape(2 * self.rows, 128)
+        self.back_copy().wait()
+        for core in range(2):
+            for j in range(self.chunk):
+                at = self.first + core * self.rows + CHIPS * j
+                self.total_ref[at : at + CHIPS, :] = self.whole[core, :, j, :]
 
 
 def sum_buffers():
     out = []
-    for _, owners, _ in GROUPS:
+    for chunk in CHUNKS:
         out += [
-            pltpu.VMEM((owners * CHUNK, 128), f32),
-            pltpu.VMEM((owners, CHUNK, 128), f32),
-            pltpu.VMEM((CHIPS, CHUNK, 128), f32),
-            pltpu.VMEM((CHUNK, 128), f32),
-            pltpu.VMEM((2, owners, CHUNK, 128), f32),
+            pltpu.VMEM((CHIPS * chunk, 128), f32),
+            pltpu.VMEM((CHIPS, chunk, 128), f32),
+            pltpu.VMEM((CHIPS, chunk, 128), f32),
+            pltpu.VMEM((chunk, 128), f32),
+            pltpu.VMEM((2, CHIPS, chunk, 128), f32),
         ]
     return out
 
 
 def step_kernel(
-    group_size,
-    shard_size,
     width,
     table_hbm,
     index_hbm,
@@ -581,11 +564,8 @@
     buffers = scratch[len(WEIGHTS) + len(GRADS) :]
     w1_ref, w2f_ref, w2b_ref, b2_ref, w3_ref, b3_ref, w3t_ref, w3b_ref, b3a_ref, w1a_ref = weights
     blocks = N // width
-    me = lax.axis_index("group") * shard_size + lax.axis_index("shard")
-
-    def device(k):
-        peer = lax.rem(me + k, DEVS)
-        return peer, (peer // shard_size, lax.rem(peer, shard_size))
+    place = Place()
+    me = place.me
 
     loads = [
         pltpu.make_async_copy(src, dst, in_sems.at[n])
@@ -607,11 +587,14 @@
 
     barrier = pltpu.get_barrier_semaphore()
 
-    def greet(k, carry):
-        pl.semaphore_signal(barrier, inc=1, device_id=device(k)[1], device_id_type=MESH)
-        return carry
-
-    lax.fori_loop(1, DEVS, greet, 0)
+    def all_others():
+        for other_core in (False, True):
+            for _, device in place.others(other_core):
+                yield device[0] * 8 + device[1], device
+        yield place.sibling_at, place.sibling
+
+    for _, device in all_others():
+        pl.semaphore_signal(barrier, inc=1, device_id=device, device_id_type=MESH)
     for ref in grads:
         ref[...] = jnp.zeros_like(ref)
     loads[0].wait()
@@ -622,7 +605,7 @@
 
     lax.fori_loop(0, R_DEV // TURN, turn, 0)
     loads[1].wait()
-    pick_rows(0, width, index_ref, rows_ref, picked_ref, x_ref)
+    pick_rows(0, width, index_ref, rows_ref, picked_ref)
     loads[2].wait()
     prepare_critics(
         critic_ref, flat_ref, pad_ref, C0, w1_ref, w2f_ref, w2b_ref, b2_ref, w3_ref, b3_ref, w1a_ref
@@ -635,34 +618,33 @@
     loads[5].wait()
     turn_noise(noise_ref, q_ref, nsend)
 
-    def send(k, carry):
-        peer, to = device(k)
-        pltpu.make_async_remote_copy(
-            src_ref=nsend.at[peer],
-            dst_ref=nrecv.at[me],
-            send_sem=noise_sems.at[0],
-            recv_sem=noise_sems.at[1],
-            device_id=to,
-            device_id_type=MESH,
-        ).start()
-        return carry
+    def send():
+        for peer, device in all_others():
+            pltpu.make_async_remote_copy(
+                src_ref=nsend.at[peer],
+                dst_ref=nrecv.at[me],
+                send_sem=noise_sems.at[0],
+                recv_sem=noise_sems.at[1],
+                device_id=device,
+                device_id_type=MESH,
+            ).start()
 
     def actors(i, carry):
-        pick_rows(lax.rem(i + 1, blocks), width, index_ref, rows_ref, picked_ref, x_ref)
-        actor_block(i, width, x_ref, count_ref, weights, grads)
+        x = turn_rows(width, picked_ref)
+        x_ref[:, pl.ds(pl.multiple_of(i * width, width), width)] = x
+        actor_block(i, width, x, count_ref, weights, grads)
+        pick_rows(lax.rem(i + 1, blocks), width, index_ref, rows_ref, picked_ref)
 
         @pl.when(i == 0)
         def _():
             pl.semaphore_wait(barrier, DEVS - 1)
-            lax.fori_loop(1, DEVS, send, 0)
+            send()
 
         return carry
 
     lax.fori_loop(0, blocks, actors, 0)
     pack_actor(pack_ref, grads)
-    wide, rest, early = (
-        Sum(g, shard_size, pack_ref, sum_ref, buffers[5 * g : 5 * g + 5], sems) for g in range(3)
-    )
+    late, early = (Sum(place, g, pack_ref, sum_ref, buffers[5 * g : 5 * g + 5], sems) for g in range(2))
     early.swap().start()
 
     loads[6].wait()
@@ -679,7 +661,8 @@
     noise_back(nrecv, nz_ref)
 
     def critics(i, carry):
-        critic_block(i, width, x_ref, nz_ref, count_ref, weights, prio_ref, grads)
+        x = x_ref[:, pl.ds(pl.multiple_of(i * width, width), width)]
+        critic_block(i, width, x, nz_ref, count_ref, weights, prio_ref, grads)
 
         @pl.when(i == 0)
         def _():
@@ -692,29 +675,19 @@
 
         @pl.when(i == 2)
         def _():
-            early.back().start()
+            early.back()
 
         return carry
 
     lax.fori_loop(0, blocks, critics, 0)
     pack_critics(pack_ref, grads)
-    late = (wide, rest)
-    for part in late:
-        part.swap().start()
-    early.remote(early.whole.at[early.core], early.whole.at[early.core], 3, early.sibling).wait()
-    for part in late:
-        part.swap().wait()
-        part.scatter()
+    late.swap().start()
     early.store()
-    for part in late:
-        part.spread()
-    backs = [part.back() for part in late]
-    for copy in backs:
-        copy.start()
-    for copy in backs:
-        copy.wait()
-    for part in late:
-        part.store()
+    late.swap().wait()
+    late.scatter()
+    late.spread()
+    late.back()
+    late.store()
 
 
 def update(weight, grad, momentum, average, target):
@@ -725,47 +698,70 @@
     return (weight_new, momentum_new, average_new, target_new, weight_new.astype(bf))
 
 
-def update_kernel(sum_ref, prio_in, *refs):
-    ins, (stat_ref, prio_ref), outs, grad_ref = refs[:8], refs[8:10], refs[10:20], refs[20]
+def update_kernel(sum_hbm, prio_hbm, *refs):
+    ins_hbm, stat_ref, prio_out, outs_hbm = refs[:8], refs[8], refs[9], refs[10:20]
+    sum_ref, ins, outs, grad_ref, in_sems, out_sems = refs[20], refs[21:29], refs[29:39], refs[39], refs[40], refs[41]
+    loads = [pltpu.make_async_copy(sum_hbm, sum_ref, in_sems.at[8])]
+    loads += [pltpu.make_async_copy(ins_hbm[n], ins[n], in_sems.at[n]) for n in range(8)]
+    for load in [loads[0]] + loads[1::2] + loads[2::2]:
+        load.start()
+    pass_on = pltpu.make_async_copy(prio_hbm, prio_out, in_sems.at[9])
+    pass_on.start()
+    loads[0].wait()
     stat = sum_ref[STAT : STAT + 1, :]
     factor = (1.0 / SCALE) / stat[:, 1:2]
     stat_ref[...] = stat
-    prio_ref[...] = prio_in[...]
-    for t in range(TILES_C):
-        r = critic_row(2 * t)
-        grad_ref[:, 128 * t : 128 * (t + 1)] = sum_ref[r : r + 2, :] * factor
-
-    def critics(s):
-        values = update(ins[1][:, s], grad_ref[:, s], ins[3][:, s], ins[5][:, s], ins[7][:, s])
-        for ref, value in zip(outs[1::2], values):
-            ref[:, s] = value
+    stores = [pltpu.make_async_copy(outs[n], outs_hbm[n], out_sems.at[n]) for n in range(10)]
+    step = 1024
 
     def actor(s, grad):
         values = update(ins[0][s], grad, ins[2][s], ins[4][s], ins[6][s])
         for ref, value in zip(outs[0::2], values):
             ref[s] = value
 
-    step = 1024
+    for load in loads[1::2]:
+        load.wait()
 
     def body(i, carry):
-        critics(pl.ds(pl.multiple_of(i * step, step), step))
         r = pl.multiple_of(AT_ACTOR + 8 * i, 8)
         actor(pl.ds(pl.multiple_of(i * step, step), step), (sum_ref[pl.ds(r, 8), :] * factor).reshape(step))
         return carry
 
-    lax.fori_loop(0, PA // step, body, 0)
+    lax.fori_loop(0, PA // step, body, 0, unroll=5)
     done = PA // step * step
-    critics(pl.ds(done, PC - done))
     r = AT_ACTOR + done // 128
     more = (PA - done) // 128
     actor(pl.ds(done, 128 * more), (sum_ref[r : r + more, :] * factor).reshape(128 * more))
     done += 128 * more
     actor(pl.ds(done, ACT), (sum_ref[r + more : r + more + 1, :ACT] * factor).reshape(ACT))
+    for store in stores[0::2]:
+        store.start()
+
+    def critics(s):
+        values = update(ins[1][:, s], grad_ref[:, s], ins[3][:, s], ins[5][:, s], ins[7][:, s])
+        for ref, value in zip(outs[1::2], values):
+            ref[:, s] = value
+
+    for t in range(TILES_C):
+        grad_ref[:, 128 * t : 128 * (t + 1)] = sum_ref[2 * t : 2 * t + 2, :] * factor
+    for load in loads[2::2]:
+        load.wait()
+
+    def body(i, carry):
+        critics(pl.ds(pl.multiple_of(i * step, step), step))
+        return carry
+
+    lax.fori_loop(0, PC // step, body, 0, unroll=5)
+    done = PC // step * step
+    critics(pl.ds(done, PC - done))
+    for store in stores[1::2]:
+        store.start()
+    for store in stores:
+        store.wait()
+    pass_on.wait()
 
 
 def local(
-    group_size,
-    shard_size,
     replay,
     sample_index,
     pair_count,
@@ -781,7 +777,7 @@
 ):
     any_ = pl.BlockSpec(memory_space=pl.ANY)
     prio, total = pl.pallas_call(
-        functools.partial(step_kernel, group_size, shard_size, WIDTH),
+        functools.partial(step_kernel, WIDTH),
         out_shape=(SDS((CAP, DEVS), f32), SDS((PACK, 128), f32)),
         in_specs=[any_] * 8,
         out_specs=(VM, VM),
@@ -806,7 +802,7 @@
             pltpu.VMEM((2 * TILES_C + 6, 128), f32),
             pltpu.VMEM((FEAT, 256), f32),
             pltpu.VMEM((PACK, 128), f32),
-            pltpu.SemaphoreType.DMA((3, 8)),
+            pltpu.SemaphoreType.DMA((2, 8)),
         ]
         + WEIGHTS
         + GRADS
@@ -826,14 +822,15 @@
         critic_target,
     )
     shapes = [SDS((1, 128), f32), SDS((CAP, DEVS), f32)]
-    for kind in (f32, f32, f32, f32, bf):
-        shapes += [SDS((PA,), kind), SDS((2, PC), kind)]
+    places = [SDS((PA,), f32), SDS((2, PC), f32)] * 4 + [SDS((PA,), bf), SDS((2, PC), bf)]
     stat, prio, *outs = pl.pallas_call(
         update_kernel,
-        out_shape=tuple(shapes),
-        in_specs=[VM] * 10,
-        out_specs=(VM,) * 12,
-        scratch_shapes=[pltpu.VMEM((2, TILES_C * 128), f32)],
+        out_shape=tuple(shapes + places),
+        in_specs=[any_] * 10,
+        out_specs=(VM,) + (any_,) * 11,
+        scratch_shapes=[pltpu.VMEM((PACK, 128), f32)]
+        + [pltpu.VMEM(p.shape, p.dtype) for p in places[:8] + places]
+        + [pltpu.VMEM((2, TILES_C * 128), f32), pltpu.SemaphoreType.DMA((10,)), pltpu.SemaphoreType.DMA((10,))],
         compiler_params=pltpu.CompilerParams(vmem_limit_bytes=24 << 20),
         name="update",
     )(
@@ -855,5 +852,4 @@
     rows = ("group", "shard")
     in_specs = (P(rows, None), P(rows, None, None), P(rows, None), P(rows, None, None, None)) + (P(),) * 8
     out_specs = (P(), P(rows, None, None)) + (P(),) * 10
-    body = functools.partial(local, mesh.shape["group"], mesh.shape["shard"])
-    return jax.shard_map(body, mesh=mesh, in_specs=in_specs, out_specs=out_specs, check_vma=False)
+    return jax.shard_map(local, mesh=mesh, in_specs=in_specs, out_specs=out_specs, check_vma=False)

time: 98.5 us -> 88.9 us (0.903)
  Pallas kernels: 94 us -> 84.5 us
    pallas_call x2, Pallas kernels: 94 us -> 84.5 us  [the longest x1 79.1 us: local(): pl.pallas_call(functools.partial(step_kernel, WIDTH), out_shape=(SDS((CAP...]
where the time goes in v4:
time: 88.9 us; the launch traced here: 88.6 us
  Pallas kernels  84.5 us (95%)
  local copies, waits for them, and re-layouts  3.39 us (4%)
    pallas_call x1, Pallas kernels, local(): pl.pallas_call(functools.partial(step_kernel, WIDTH), out_shape=(SDS((CAP...  79.1 us
    pallas_call x1, Pallas kernels, local(): pl.pallas_call(update_kernel, out_shape=tuple(shapes + places), in_specs=...  5.32 us
    unnamed x20, local copies, waits for them, and re-layouts  2.88 us

profile of v4, /device:TPU:1, one launch (start us, length us, event | category | flops | bytes accessed | tf_op | source)
XLA Modules:
  0.0 88.6 jit_solution(12068237142888087631)
XLA Ops:
  0.6 0.0 copy-start
  0.7 0.0 copy-start.1
  0.7 0.0 copy-start.2
  0.7 0.0 copy-start.3
  0.7 0.0 copy-start.5
  0.7 0.0 copy-start.6
  0.7 0.0 copy-start.7
  0.7 79.1 %td3_step.1 = (f32[32,128]{1,0:T(8,128)}, f32[1792,128]{1,0:T(8,128)}) custom-call(f32[42,8192]{1,0:T(8,128)} %bitcast.12, s32[32,128]{1,0:T(8,128)} %bitcast.14, f32[6,32,128]{2,1,0:T(8,128)} %bitcast.13, s32[1,128]{1,0:T(1,128)} %count_hbm.1, f32[71942]{0:T(1024)} %refs_0_.1, f32[71942]{0:T(1024)} %refs_6_.1, f32[2,72193]{1,0:T(2,128)} %refs_1_.1, ...), custom_call_target="tpu_custom_call" | custom-call | tf_op jit(solution)/shard_map/td3_step/pallas_call | solution.py:779
  79.9 0.0 copy-done
  79.9 0.0 copy-done.1
  79.9 0.0 copy-done.2
  79.9 0.0 copy-done.3
  79.9 0.0 copy-done.5
  79.9 0.0 copy-done.6
  79.9 0.0 copy-done.7
  79.9 0.0 copy-start.4
  80.0 1.2 %copy-done.4 = f32[1792,128]{1,0:T(8,128)S(1)} copy-done((f32[1792,128]{1,0:T(8,128)S(1)}, f32[1792,128]{1,0:T(8,128)}, u32[]{:S(2)}) %copy-start.4) | copy-done | bytes 917528
  81.1 0.0 copy-start.8
  81.1 1.0 %copy-done.8 = f32[71942]{0:T(1024)S(1)} copy-done((f32[71942]{0:T(1024)S(1)}, f32[71942]{0:T(1024)}, u32[]{:S(2)}) %copy-start.8) | copy-done | bytes 287792
  82.1 0.0 copy-start.9
  82.1 0.7 copy-done.9
  82.8 5.3 %update.1 = (f32[1,128]{1,0:T(1,128)S(1)}, f32[32,128]{1,0:T(8,128)}, f32[71942]{0:T(1024)}, f32[2,72193]{1,0:T(2,128)}, f32[71942]{0:T(1024)}, /*index=5*/f32[2...) custom-call(f32[1792,128]{1,0:T(8,128)S(1)} %copy-done.4, ...), custom_call_target="tpu_custom_call" | custom-call | tf_op jit(solution)/shard_map/update/pallas_call | solution.py:826
  88.1 0.5 slice_bitcast_fusion
Async XLA Ops:
  0.6 79.2 %copy-start = (f32[2,72193]{1,0:T(2,128)S(1)}, f32[2,72193]{1,0:T(2,128)}, u32[]{:S(2)}) copy-start(f32[2,72193]{1,0:T(2,128)} %refs_1_.1) | copy-start | bytes 1732636
  0.7 79.2 %copy-start.1 = (f32[2,72193]{1,0:T(2,128)S(1)}, f32[2,72193]{1,0:T(2,128)}, u32[]{:S(2)}) copy-start(f32[2,72193]{1,0:T(2,128)} %refs_7_.1) | copy-start | bytes 1732636
  0.7 79.2 %copy-start.2 = (f32[71942]{0:T(1024)S(1)}, f32[71942]{0:T(1024)}, u32[]{:S(2)}) copy-start(f32[71942]{0:T(1024)} %refs_0_.1) | copy-start | bytes 863308
  0.7 79.2 %copy-start.3 = (f32[71942]{0:T(1024)S(1)}, f32[71942]{0:T(1024)}, u32[]{:S(2)}) copy-start(f32[71942]{0:T(1024)} %refs_6_.1) | copy-start | bytes 863308
  0.7 79.2 %copy-start.5 = (f32[2,72193]{1,0:T(2,128)S(1)}, f32[2,72193]{1,0:T(2,128)}, u32[]{:S(2)}) copy-start(f32[2,72193]{1,0:T(2,128)} %refs_3_.1) | copy-start | bytes 1732636
  0.7 79.2 %copy-start.6 = (f32[2,72193]{1,0:T(2,128)S(1)}, f32[2,72193]{1,0:T(2,128)}, u32[]{:S(2)}) copy-start(f32[2,72193]{1,0:T(2,128)} %refs_5_.1) | copy-start | bytes 1732636
  0.7 79.2 %copy-start.7 = (f32[71942]{0:T(1024)S(1)}, f32[71942]{0:T(1024)}, u32[]{:S(2)}) copy-start(f32[71942]{0:T(1024)} %refs_2_.1) | copy-start | bytes 863308
  79.9 1.2 %copy-start.4 = (f32[1792,128]{1,0:T(8,128)S(1)}, f32[1792,128]{1,0:T(8,128)}, u32[]{:S(2)}) copy-start(f32[1792,128]{1,0:T(8,128)} %get-tuple-element.26.sum_hbm) | copy-start | bytes 2752516
  81.1 1.0 %copy-start.8 = (f32[71942]{0:T(1024)S(1)}, f32[71942]{0:T(1024)}, u32[]{:S(2)}) copy-start(f32[71942]{0:T(1024)} %refs_4_.1) | copy-start | bytes 863308
  82.1 0.7 copy-start.9

commit v5 on v4

--- a/solution.py
+++ b/solution.py
@@ -169,10 +169,10 @@
 def head_maps(j):
     k = lax.broadcasted_iota(jnp.int32, (UNITS, 16), 0)
     r = lax.broadcasted_iota(jnp.int32, (UNITS, 16), 1)
-    row = ((k * ACT + j) // 128) == r
+    row = ((k * ACT + j) >> 7) == r
     k = lax.broadcasted_iota(jnp.int32, (UNITS, 128), 0)
     l = lax.broadcasted_iota(jnp.int32, (UNITS, 128), 1)
-    lane = ((k * ACT + j) % 128) == l
+    lane = ((k * ACT + j) & 127) == l
     return row.astype(f32), lane
 
 
@@ -187,7 +187,7 @@
             spread.append(jnp.where(lane, dot(row.astype(bf), part), 0.0).astype(bf))
         r = lax.broadcasted_iota(jnp.int32, (16, 128 * ACT), 0)
         l = lax.broadcasted_iota(jnp.int32, (16, 128 * ACT), 1)
-        take = ((l // 128) == (r - 1)).astype(f32).astype(bf)
+        take = ((l >> 7) == (r - 1)).astype(f32).astype(bf)
         out.append(dot_nt(take, jnp.concatenate(spread, 1))[:8])
     return out
 
@@ -271,13 +271,12 @@
         tiles = self.width // 128
         return jnp.concatenate([((self.i * tiles + t) < count_ref[...]).astype(f32) for t in range(tiles)], 1)
 
-    def back(self, net, dz2):
-        hi, lo = split(dz2)
-        return hi, lo, dot(self.w2b[net], jnp.concatenate([hi, lo, hi], 0))
-
-    def weight_grads(self, net, h1, hi, lo, dz1, g2_ref, g1_ref):
-        left = jnp.concatenate([h1[:UNITS], h1[UNITS : 2 * UNITS], h1[:UNITS]], 1)
-        g2_ref[net] += dot_nt(left, jnp.concatenate([hi, hi, lo], 1))
+    def grads2(self, net, h1, dz2, g2_ref):
+        u = UNITS
+        left = jnp.concatenate([h1[:u], h1[u : 2 * u], h1[:u]], 1)
+        g2_ref[net] += dot_nt(left, jnp.concatenate([dz2[:u], dz2[:u], dz2[u : 2 * u]], 1))
+
+    def grads1(self, net, dz1, g1_ref):
         xhi, xlo = self.x3[:FEAT], self.x3[FEAT : 2 * FEAT]
         left = jnp.concatenate(
             [jnp.concatenate([xhi, xlo], 0), jnp.concatenate([xhi, jnp.zeros_like(xlo)], 0)], 1
@@ -294,41 +293,46 @@
     u, s = st.first(AT, x3)
     u, s = st.second(AT, three(s))
     next_action = jnp.tanh(st.head(AT, three(s)) + nz_ref[:, st.lanes])
-
-    kept = []
-    for net in (C0, C1):
-        u, s = st.first(net, x3)
-        h1, d1 = three(s), slope(u, s)
-        u, s = st.second(net, h1)
-        kept.append((h1, d1, s, slope(u, s), st.value(net, s)))
-
     xt = st.with_action(next_action)
     targets = []
     for net in (T0, T1):
         u, s = st.first(net, xt)
         u, s = st.second(net, three(s))
         targets.append(st.value(net, s))
-
     y = x[23:24] + 0.99 * x[24:25] * jnp.minimum(targets[0], targets[1])
     valid = st.valid(count_ref)
-    delta = [k[4] - y for k in kept]
-    prio = valid * jnp.sqrt(delta[0] * delta[0] + 1.0)
-    tiles = width // 128
-    for t in range(tiles):
-        prio_ref[pl.ds(i * tiles + t, 1), :] = prio[:, 128 * t : 128 * (t + 1)]
-    st_ref[0:1, :] += fold(valid * (delta[0] * delta[0] + delta[1] * delta[1]))
+    scaled = valid * SCALE
     st_ref[1:2, :] += fold(valid)
-    scaled = valid * SCALE
-
-    for net in (C0, C1):
-        h1, d1, s2, d2, _ = kept[net]
-        dq = (2.0 * scaled) * delta[net]
+
+    def top(net, s, d2):
+        delta = st.value(net, s) - y
+        if net == C0:
+            prio = valid * jnp.sqrt(delta * delta + 1.0)
+            tiles = width // 128
+            for t in range(tiles):
+                prio_ref[pl.ds(i * tiles + t, 1), :] = prio[:, 128 * t : 128 * (t + 1)]
+        st_ref[0:1, :] += fold(valid * (delta * delta))
+        dq = (2.0 * scaled) * delta
         st_ref[2 + net : 3 + net, :] += fold(dq)
-        dw3_ref[net] += fold(s2 * dq)
+        dw3_ref[net] += fold(s * dq)
         dz2 = lanes(st.w3[net], width) * (0.5 * dq) * d2
         db2_ref[net] += fold(dz2)
-        hi, lo, dh1 = st.back(net, dz2)
-        st.weight_grads(net, h1, hi, lo, dh1 * d1, g2_ref, g1_ref)
+        return three(dz2)
+
+    u, s = st.first(C0, x3)
+    h1, d1 = three(s), slope(u, s)
+    u, s = st.second(C0, h1)
+    dz2 = top(C0, s, slope(u, s))
+    dz1 = dot(st.w2b[C0], dz2) * d1
+    u, s = st.first(C1, x3)
+    h1b, d1b = three(s), slope(u, s)
+    st.grads2(C0, h1, dz2, g2_ref)
+    u, s = st.second(C1, h1b)
+    st.grads1(C0, dz1, g1_ref)
+    dz2 = top(C1, s, slope(u, s))
+    dz1 = dot(st.w2b[C1], dz2) * d1b
+    st.grads2(C1, h1b, dz2, g2_ref)
+    st.grads1(C1, dz1, g1_ref)
 
 
 def actor_block(i, width, x, count_ref, weights, grads):
@@ -348,9 +352,9 @@
     valid = st.valid(count_ref)
     st_ref[0:1, :] -= fold(valid * q_policy)
 
-    dz2 = lanes(st.w3[C0], width) * (-0.5 * SCALE * valid) * d2f
-    hi, lo, dh1 = st.back(C0, dz2)
-    da = dot(st.w1a[...], three(dh1 * d1f))[:8]
+    dz2 = three(lanes(st.w3[C0], width) * (-0.5 * SCALE * valid) * d2f)
+    dz1 = three(dot(st.w2b[C0], dz2) * d1f)
+    da = dot(st.w1a[...], dz1)[:8]
     dp = jnp.where(st.is_action, da * (1.0 - policy * policy), 0.0)
     st_ref[8:16, :] += fold(dp)
     hi = dp.astype(bf).astype(f32)
@@ -361,8 +365,10 @@
     g3a_ref[...] += dot_nt(left, jnp.concatenate([h2a[:UNITS], h2a[UNITS : 2 * UNITS]], 1))
     dz2 = dot(st.w3b[:, :32], stacked) * d2a
     db2_ref[A] += fold(dz2)
-    hi, lo, dh1 = st.back(A, dz2)
-    st.weight_grads(A, h1a, hi, lo, dh1 * d1a, g2_ref, g1_ref)
+    dz2 = three(dz2)
+    dz1 = dot(st.w2b[A], dz2) * d1a
+    st.grads2(A, h1a, dz2, g2_ref)
+    st.grads1(A, dz1, g1_ref)
 
 
 def lane_sums(tile):
@@ -698,66 +704,82 @@
     return (weight_new, momentum_new, average_new, target_new, weight_new.astype(bf))
 
 
+STEP = 1024
+CUTS = (0, 35 * STEP, PC)
+
+
 def update_kernel(sum_hbm, prio_hbm, *refs):
     ins_hbm, stat_ref, prio_out, outs_hbm = refs[:8], refs[8], refs[9], refs[10:20]
     sum_ref, ins, outs, grad_ref, in_sems, out_sems = refs[20], refs[21:29], refs[29:39], refs[39], refs[40], refs[41]
-    loads = [pltpu.make_async_copy(sum_hbm, sum_ref, in_sems.at[8])]
-    loads += [pltpu.make_async_copy(ins_hbm[n], ins[n], in_sems.at[n]) for n in range(8)]
-    for load in [loads[0]] + loads[1::2] + loads[2::2]:
-        load.start()
-    pass_on = pltpu.make_async_copy(prio_hbm, prio_out, in_sems.at[9])
+
+    def copies(srcs, dsts, sems, piece):
+        out = []
+        for n, (src, dst) in enumerate(zip(srcs, dsts)):
+            if piece:
+                s = pl.ds(CUTS[piece - 1], CUTS[piece] - CUTS[piece - 1])
+                src, dst = src.at[:, s], dst.at[:, s]
+            out.append(pltpu.make_async_copy(src, dst, sems.at[piece, n]))
+        return out
+
+    first = pltpu.make_async_copy(sum_hbm, sum_ref, in_sems.at[3, 0])
+    first.start()
+    loads = [copies(ins_hbm[min(p, 1) :: 2], ins[min(p, 1) :: 2], in_sems, p) for p in range(3)]
+    for piece in loads:
+        for load in piece:
+            load.start()
+    pass_on = pltpu.make_async_copy(prio_hbm, prio_out, in_sems.at[3, 1])
     pass_on.start()
-    loads[0].wait()
+    stores = [copies(outs[min(p, 1) :: 2], outs_hbm[min(p, 1) :: 2], out_sems, p) for p in range(3)]
+    first.wait()
     stat = sum_ref[STAT : STAT + 1, :]
     factor = (1.0 / SCALE) / stat[:, 1:2]
-    stat_ref[...] = stat
-    stores = [pltpu.make_async_copy(outs[n], outs_hbm[n], out_sems.at[n]) for n in range(10)]
-    step = 1024
+    stat_ref[...] = stat[:, :2].reshape(2)
 
     def actor(s, grad):
         values = update(ins[0][s], grad, ins[2][s], ins[4][s], ins[6][s])
         for ref, value in zip(outs[0::2], values):
             ref[s] = value
 
-    for load in loads[1::2]:
+    def actors(i, carry):
+        r = pl.multiple_of(AT_ACTOR + 8 * i, 8)
+        actor(pl.ds(pl.multiple_of(i * STEP, STEP), STEP), (sum_ref[pl.ds(r, 8), :] * factor).reshape(STEP))
+        return carry
+
+    for load in loads[0]:
         load.wait()
-
-    def body(i, carry):
-        r = pl.multiple_of(AT_ACTOR + 8 * i, 8)
-        actor(pl.ds(pl.multiple_of(i * step, step), step), (sum_ref[pl.ds(r, 8), :] * factor).reshape(step))
-        return carry
-
-    lax.fori_loop(0, PA // step, body, 0, unroll=5)
-    done = PA // step * step
+    lax.fori_loop(0, PA // STEP, actors, 0, unroll=5)
+    done = PA // STEP * STEP
     r = AT_ACTOR + done // 128
     more = (PA - done) // 128
     actor(pl.ds(done, 128 * more), (sum_ref[r : r + more, :] * factor).reshape(128 * more))
     done += 128 * more
     actor(pl.ds(done, ACT), (sum_ref[r + more : r + more + 1, :ACT] * factor).reshape(ACT))
-    for store in stores[0::2]:
+    for store in stores[0]:
         store.start()
 
-    def critics(s):
+    def critic(s):
         values = update(ins[1][:, s], grad_ref[:, s], ins[3][:, s], ins[5][:, s], ins[7][:, s])
         for ref, value in zip(outs[1::2], values):
             ref[:, s] = value
 
+    def critics(i, carry):
+        critic(pl.ds(pl.multiple_of(i * STEP, STEP), STEP))
+        return carry
+
     for t in range(TILES_C):
         grad_ref[:, 128 * t : 128 * (t + 1)] = sum_ref[2 * t : 2 * t + 2, :] * factor
-    for load in loads[2::2]:
-        load.wait()
-
-    def body(i, carry):
-        critics(pl.ds(pl.multiple_of(i * step, step), step))
-        return carry
-
-    lax.fori_loop(0, PC // step, body, 0, unroll=5)
-    done = PC // step * step
-    critics(pl.ds(done, PC - done))
-    for store in stores[1::2]:
-        store.start()
-    for store in stores:
-        store.wait()
+    for piece in (1, 2):
+        for load in loads[piece]:
+            load.wait()
+        lax.fori_loop(CUTS[piece - 1] // STEP, CUTS[piece] // STEP, critics, 0, unroll=5)
+        if piece == 2:
+            done = PC // STEP * STEP
+            critic(pl.ds(done, PC - done))
+        for store in stores[piece]:
+            store.start()
+    for piece in stores:
+        for store in piece:
+            store.wait()
     pass_on.wait()
 
 
@@ -821,7 +843,7 @@
         critic,
         critic_target,
     )
-    shapes = [SDS((1, 128), f32), SDS((CAP, DEVS), f32)]
+    shapes = [SDS((2,), f32), SDS((CAP, DEVS), f32)]
     places = [SDS((PA,), f32), SDS((2, PC), f32)] * 4 + [SDS((PA,), bf), SDS((2, PC), bf)]
     stat, prio, *outs = pl.pallas_call(
         update_kernel,
@@ -830,8 +852,8 @@
         out_specs=(VM,) + (any_,) * 11,
         scratch_shapes=[pltpu.VMEM((PACK, 128), f32)]
         + [pltpu.VMEM(p.shape, p.dtype) for p in places[:8] + places]
-        + [pltpu.VMEM((2, TILES_C * 128), f32), pltpu.SemaphoreType.DMA((10,)), pltpu.SemaphoreType.DMA((10,))],
-        compiler_params=pltpu.CompilerParams(vmem_limit_bytes=24 << 20),
+        + [pltpu.VMEM((2, TILES_C * 128), f32), pltpu.SemaphoreType.DMA((4, 5)), pltpu.SemaphoreType.DMA((3, 5))],
+        compiler_params=pltpu.CompilerParams(vmem_limit_bytes=60 << 20),
         name="update",
     )(
         total,
@@ -845,7 +867,7 @@
         actor_target,
         critic_target,
     )
-    return (stat[0, :2], prio.T[None], *outs)
+    return (stat, prio.T[None], *outs)
 
 
 def solution(mesh):

time: 88.9 us -> 85.3 us (0.960)
  local copies, waits for them, and re-layouts: 3.39 us -> 0 us
    unnamed x20 -> x0, local copies, waits for them, and re-layouts: 2.88 us -> none
    pallas_call x1, Pallas kernels: 79.1 us -> 78.1 us  [local(): pl.pallas_call(functools.partial(step_kernel, WIDTH), out_shape=(SDS((CAP...]
where the time goes in v5:
time: 85.3 us; the launch traced here: 85.2 us
  Pallas kernels  84.3 us (99%)
    pallas_call x1, Pallas kernels, local(): pl.pallas_call(functools.partial(step_kernel, WIDTH), out_shape=(SDS((CAP...  78.1 us
    pallas_call x1, Pallas kernels, local(): pl.pallas_call(update_kernel, out_shape=tuple(shapes + places), in_specs=...  6.21 us

profile of v5, /device:TPU:1, one launch (start us, length us, event | category | flops | bytes accessed | tf_op | source)
XLA Modules:
  0.0 85.2 jit_solution(3884350878532046217)
XLA Ops:
  0.6 78.1 %td3_step.1 = (f32[32,128]{1,0:T(8,128)}, f32[1792,128]{1,0:T(8,128)}) custom-call(f32[42,8192]{1,0:T(8,128)} %bitcast.10, s32[32,128]{1,0:T(8,128)} %bitcast.12, f32[6,32,128]{2,1,0:T(8,128)} %bitcast.11, s32[1,128]{1,0:T(1,128)} %count_hbm.1, f32[71942]{0:T(1024)} %refs_0_.1, f32[71942]{0:T(1024)} %refs_6_.1, f32[2,72193]{1,0:T(2,128)} %refs_1_.1, ...), custom_call_target="tpu_custom_call" | custom-call | tf_op jit(solution)/shard_map/td3_step/pallas_call | solution.py:801
  78.8 6.2 %update.1 = (f32[2]{0:T(128)}, f32[32,128]{1,0:T(8,128)}, f32[71942]{0:T(1024)}, f32[2,72193]{1,0:T(2,128)}, f32[71942]{0:T(1024)}, /*index=5*/f32[2,72193]{1,0:...) custom-call(f32[1792,128]{1,0:T(8,128)} %get-tuple-element.26.sum_hb, ...), custom_call_target="tpu_custom_call" | custom-call | tf_op jit(solution)/shard_map/update/pallas_call | solution.py:848

commit v6 on v5

--- a/solution.py
+++ b/solution.py
@@ -37,6 +37,8 @@
 CHUNKS = (9, 5)
 AT_ACTOR = 2 * CHIPS * CHUNKS[0]
 PACK = AT_ACTOR + 2 * CHIPS * CHUNKS[1]
+PLACES = (0, 16)
+SUMS = (DEVS + 2, 24, 128)
 TURN = 512
 WIDTH = 1024
 STEPS = sorted(
@@ -294,11 +296,17 @@
     u, s = st.second(AT, three(s))
     next_action = jnp.tanh(st.head(AT, three(s)) + nz_ref[:, st.lanes])
     xt = st.with_action(next_action)
-    targets = []
-    for net in (T0, T1):
-        u, s = st.first(net, xt)
-        u, s = st.second(net, three(s))
-        targets.append(st.value(net, s))
+    u, s = st.first(T0, xt)
+    h0 = three(s)
+    u, s = st.first(T1, xt)
+    h1t = three(s)
+    u, s = st.second(T0, h0)
+    targets = [st.value(T0, s)]
+    u0, s0 = st.first(C0, x3)
+    h1, d1 = three(s0), slope(u0, s0)
+    u, s = st.second(T1, h1t)
+    targets.append(st.value(T1, s))
+    u0, s0 = st.second(C0, h1)
     y = x[23:24] + 0.99 * x[24:25] * jnp.minimum(targets[0], targets[1])
     valid = st.valid(count_ref)
     scaled = valid * SCALE
@@ -319,13 +327,10 @@
         db2_ref[net] += fold(dz2)
         return three(dz2)
 
-    u, s = st.first(C0, x3)
-    h1, d1 = three(s), slope(u, s)
-    u, s = st.second(C0, h1)
-    dz2 = top(C0, s, slope(u, s))
-    dz1 = dot(st.w2b[C0], dz2) * d1
     u, s = st.first(C1, x3)
     h1b, d1b = three(s), slope(u, s)
+    dz2 = top(C0, s0, slope(u0, s0))
+    dz1 = dot(st.w2b[C0], dz2) * d1
     st.grads2(C0, h1, dz2, g2_ref)
     u, s = st.second(C1, h1b)
     st.grads1(C0, dz1, g1_ref)
@@ -362,11 +367,11 @@
     zero = jnp.zeros_like(hi)
     stacked = jnp.concatenate([hi, lo, hi, zero], 0).astype(bf)
     left = jnp.concatenate([jnp.concatenate([hi, lo], 0), jnp.concatenate([hi, zero], 0)], 1).astype(bf)
-    g3a_ref[...] += dot_nt(left, jnp.concatenate([h2a[:UNITS], h2a[UNITS : 2 * UNITS]], 1))
     dz2 = dot(st.w3b[:, :32], stacked) * d2a
     db2_ref[A] += fold(dz2)
     dz2 = three(dz2)
     dz1 = dot(st.w2b[A], dz2) * d1a
+    g3a_ref[...] += dot_nt(left, jnp.concatenate([h2a[:UNITS], h2a[UNITS : 2 * UNITS]], 1))
     st.grads2(A, h1a, dz2, g2_ref)
     st.grads1(A, dz1, g1_ref)
 
@@ -460,11 +465,12 @@
 
 
 class Sum:
-    def __init__(self, place, g, pack_ref, total_ref, buffers, sems):
+    def __init__(self, place, g, pack_ref, out, buffers, sems):
         self.place, self.chunk = place, CHUNKS[g]
+        self.out = out.at[pl.ds(place.core * CHIPS, CHIPS), pl.ds(PLACES[g], self.chunk)]
         self.first = (0, AT_ACTOR)[g]
         self.rows = CHIPS * self.chunk
-        self.pack_ref, self.total_ref = pack_ref, total_ref
+        self.pack_ref = pack_ref
         self.other, self.half, self.parts, self.mine, self.whole = buffers
         self.sems = sems.at[g]
 
@@ -498,24 +504,24 @@
         self.parts[pl.ds(chip, 1)] = self.half[pl.ds(chip, 1)]
         self.mine[...] = jnp.sum(self.parts[...], 0)
         for _, device in self.place.others():
-            self.remote(self.mine, self.whole.at[self.place.core, chip], 2, device).start()
-
-    def back_copy(self):
-        ref = self.whole.at[self.place.core]
-        return self.remote(ref, ref, 3, self.place.sibling)
+            self.remote(self.mine, self.whole.at[chip], 2, device).start()
+
+    def back_copies(self):
+        return (
+            pltpu.make_async_copy(self.whole, self.out, self.sems.at[8]),
+            self.remote(self.whole, self.out, 3, self.place.sibling),
+        )
 
     def back(self):
         drain(self.parts, self.sems.at[4], CHIPS - 1)
-        drain(self.whole.at[0], self.sems.at[5], CHIPS - 1)
-        self.whole[pl.ds(self.place.core, 1), pl.ds(self.place.chip, 1)] = self.mine[...][None, None]
-        self.back_copy().start()
-
-    def store(self):
-        self.back_copy().wait()
-        for core in range(2):
-            for j in range(self.chunk):
-                at = self.first + core * self.rows + CHIPS * j
-                self.total_ref[at : at + CHIPS, :] = self.whole[core, :, j, :]
+        drain(self.whole, self.sems.at[5], CHIPS - 1)
+        self.whole[pl.ds(self.place.chip, 1)] = self.mine[...][None]
+        for copy in self.back_copies():
+            copy.start()
+
+    def finish(self):
+        for copy in self.back_copies():
+            copy.wait()
 
 
 def sum_buffers():
@@ -526,7 +532,7 @@
             pltpu.VMEM((CHIPS, chunk, 128), f32),
             pltpu.VMEM((CHIPS, chunk, 128), f32),
             pltpu.VMEM((chunk, 128), f32),
-            pltpu.VMEM((2, CHIPS, chunk, 128), f32),
+            pltpu.VMEM((CHIPS, chunk, 128), f32),
         ]
     return out
 
@@ -541,8 +547,8 @@
     actor_t_hbm,
     critic_hbm,
     critic_t_hbm,
+    out_hbm,
     prio_ref,
-    sum_ref,
     table_ref,
     index_ref,
     noise_ref,
@@ -577,10 +583,10 @@
         pltpu.make_async_copy(src, dst, in_sems.at[n])
         for n, (src, dst) in enumerate(
             (
+                (critic_hbm, critic_ref),
+                (actor_hbm, actor_ref),
                 (table_hbm, table_ref),
                 (index_hbm, index_ref),
-                (critic_hbm, critic_ref),
-                (actor_hbm, actor_ref),
                 (count_hbm, count_ref),
                 (noise_hbm, noise_ref),
                 (critic_t_hbm, critic_t_ref),
@@ -604,22 +610,22 @@
     for ref in grads:
         ref[...] = jnp.zeros_like(ref)
     loads[0].wait()
+    prepare_critics(
+        critic_ref, flat_ref, pad_ref, C0, w1_ref, w2f_ref, w2b_ref, b2_ref, w3_ref, b3_ref, w1a_ref
+    )
+    loads[1].wait()
+    prepare_actor(
+        A, actor_ref, flat_ref, pad_ref, w1_ref, w2f_ref, w2b_ref, b2_ref, w3t_ref, w3b_ref, b3a_ref
+    )
+    loads[2].wait()
 
     def turn(i, carry):
         turn_table(i, table_ref, rows_ref)
         return carry
 
     lax.fori_loop(0, R_DEV // TURN, turn, 0)
-    loads[1].wait()
+    loads[3].wait()
     pick_rows(0, width, index_ref, rows_ref, picked_ref)
-    loads[2].wait()
-    prepare_critics(
-        critic_ref, flat_ref, pad_ref, C0, w1_ref, w2f_ref, w2b_ref, b2_ref, w3_ref, b3_ref, w1a_ref
-    )
-    loads[3].wait()
-    prepare_actor(
-        A, actor_ref, flat_ref, pad_ref, w1_ref, w2f_ref, w2b_ref, b2_ref, w3t_ref, w3b_ref, b3a_ref
-    )
     loads[4].wait()
     loads[5].wait()
     turn_noise(noise_ref, q_ref, nsend)
@@ -650,7 +656,7 @@
 
     lax.fori_loop(0, blocks, actors, 0)
     pack_actor(pack_ref, grads)
-    late, early = (Sum(place, g, pack_ref, sum_ref, buffers[5 * g : 5 * g + 5], sems) for g in range(2))
+    late, early = (Sum(place, g, pack_ref, out_hbm, buffers[5 * g : 5 * g + 5], sems) for g in range(2))
     early.swap().start()
 
     loads[6].wait()
@@ -688,12 +694,22 @@
     lax.fori_loop(0, blocks, critics, 0)
     pack_critics(pack_ref, grads)
     late.swap().start()
-    early.store()
+    prios = [
+        pltpu.make_async_copy(
+            prio_ref.at[pl.ds(16 * n, 16)], out_hbm.at[DEVS + n, pl.ds(0, 16)], in_sems.at[n]
+        )
+        for n in range(2)
+    ]
+    for copy in prios:
+        copy.start()
     late.swap().wait()
     late.scatter()
+    early.finish()
+    for copy in prios:
+        copy.wait()
     late.spread()
     late.back()
-    late.store()
+    late.finish()
 
 
 def update(weight, grad, momentum, average, target):
@@ -708,30 +724,39 @@
 CUTS = (0, 35 * STEP, PC)
 
 
-def update_kernel(sum_hbm, prio_hbm, *refs):
-    ins_hbm, stat_ref, prio_out, outs_hbm = refs[:8], refs[8], refs[9], refs[10:20]
-    sum_ref, ins, outs, grad_ref, in_sems, out_sems = refs[20], refs[21:29], refs[29:39], refs[39], refs[40], refs[41]
-
-    def copies(srcs, dsts, sems, piece):
+def update_kernel(sum_hbm, *refs):
+    ins, stat_ref, prio_out, outs_hbm, outs = refs[:8], refs[8], refs[9], refs[10:20], refs[20:30]
+    late_ref, early_ref, grad_ref, in_sems, out_sems = refs[30:]
+    loads = [
+        pltpu.make_async_copy(
+            sum_hbm.at[pl.ds(0, DEVS), pl.ds(PLACES[g], CHUNKS[g])], (late_ref, early_ref)[g], in_sems.at[g]
+        )
+        for g in range(2)
+    ]
+    for load in loads:
+        load.start()
+    pass_on = pltpu.make_async_copy(sum_hbm.at[pl.ds(DEVS, 2), pl.ds(0, 16)], prio_out, in_sems.at[2])
+    pass_on.start()
+
+    def stores(piece):
         out = []
-        for n, (src, dst) in enumerate(zip(srcs, dsts)):
+        for n in range(5):
+            src, dst = outs[2 * n + min(piece, 1)], outs_hbm[2 * n + min(piece, 1)]
             if piece:
                 s = pl.ds(CUTS[piece - 1], CUTS[piece] - CUTS[piece - 1])
                 src, dst = src.at[:, s], dst.at[:, s]
-            out.append(pltpu.make_async_copy(src, dst, sems.at[piece, n]))
+            out.append(pltpu.make_async_copy(src, dst, out_sems.at[piece, n]))
         return out
 
-    first = pltpu.make_async_copy(sum_hbm, sum_ref, in_sems.at[3, 0])
-    first.start()
-    loads = [copies(ins_hbm[min(p, 1) :: 2], ins[min(p, 1) :: 2], in_sems, p) for p in range(3)]
-    for piece in loads:
-        for load in piece:
-            load.start()
-    pass_on = pltpu.make_async_copy(prio_hbm, prio_out, in_sems.at[3, 1])
-    pass_on.start()
-    stores = [copies(outs[min(p, 1) :: 2], outs_hbm[min(p, 1) :: 2], out_sems, p) for p in range(3)]
-    first.wait()
-    stat = sum_ref[STAT : STAT + 1, :]
+    for load in loads:
+        load.wait()
+
+    def rows(g, r, n):
+        core, r = divmod(r, CHIPS * CHUNKS[g])
+        j, k = divmod(r, CHIPS)
+        return (late_ref, early_ref)[g][core * CHIPS + k : core * CHIPS + k + n, j, :]
+
+    stat = rows(0, STAT, 1)
     factor = (1.0 / SCALE) / stat[:, 1:2]
     stat_ref[...] = stat[:, :2].reshape(2)
 
@@ -740,21 +765,15 @@
         for ref, value in zip(outs[0::2], values):
             ref[s] = value
 
-    def actors(i, carry):
-        r = pl.multiple_of(AT_ACTOR + 8 * i, 8)
-        actor(pl.ds(pl.multiple_of(i * STEP, STEP), STEP), (sum_ref[pl.ds(r, 8), :] * factor).reshape(STEP))
-        return carry
-
-    for load in loads[0]:
-        load.wait()
-    lax.fori_loop(0, PA // STEP, actors, 0, unroll=5)
+    for i in range(PA // STEP):
+        actor(slice(STEP * i, STEP * (i + 1)), (rows(1, 8 * i, 8) * factor).reshape(STEP))
     done = PA // STEP * STEP
-    r = AT_ACTOR + done // 128
+    r = done // 128
     more = (PA - done) // 128
-    actor(pl.ds(done, 128 * more), (sum_ref[r : r + more, :] * factor).reshape(128 * more))
+    actor(slice(done, done + 128 * more), (rows(1, r, more) * factor).reshape(128 * more))
     done += 128 * more
-    actor(pl.ds(done, ACT), (sum_ref[r + more : r + more + 1, :ACT] * factor).reshape(ACT))
-    for store in stores[0]:
+    actor(slice(done, PA), (rows(1, r + more, 1)[:, :ACT] * factor).reshape(ACT))
+    for store in stores(0):
         store.start()
 
     def critic(s):
@@ -767,18 +786,16 @@
         return carry
 
     for t in range(TILES_C):
-        grad_ref[:, 128 * t : 128 * (t + 1)] = sum_ref[2 * t : 2 * t + 2, :] * factor
+        grad_ref[:, 128 * t : 128 * (t + 1)] = rows(0, 2 * t, 2) * factor
     for piece in (1, 2):
-        for load in loads[piece]:
-            load.wait()
         lax.fori_loop(CUTS[piece - 1] // STEP, CUTS[piece] // STEP, critics, 0, unroll=5)
         if piece == 2:
             done = PC // STEP * STEP
             critic(pl.ds(done, PC - done))
-        for store in stores[piece]:
+        for store in stores(piece):
             store.start()
-    for piece in stores:
-        for store in piece:
+    for piece in range(3):
+        for store in stores(piece):
             store.wait()
     pass_on.wait()
 
@@ -798,12 +815,13 @@
     critic_target,
 ):
     any_ = pl.BlockSpec(memory_space=pl.ANY)
-    prio, total = pl.pallas_call(
+    total = pl.pallas_call(
         functools.partial(step_kernel, WIDTH),
-        out_shape=(SDS((CAP, DEVS), f32), SDS((PACK, 128), f32)),
+        out_shape=SDS(SUMS, f32),
         in_specs=[any_] * 8,
-        out_specs=(VM, VM),
+        out_specs=any_,
         scratch_shapes=[
+            pltpu.VMEM((CAP, DEVS), f32),
             pltpu.VMEM((ROW, R_DEV), f32),
             pltpu.SMEM((CAP, DEVS), jnp.int32),
             pltpu.VMEM((ACT, CAP, DEVS), f32),
@@ -824,7 +842,7 @@
             pltpu.VMEM((2 * TILES_C + 6, 128), f32),
             pltpu.VMEM((FEAT, 256), f32),
             pltpu.VMEM((PACK, 128), f32),
-            pltpu.SemaphoreType.DMA((2, 8)),
+            pltpu.SemaphoreType.DMA((2, 9)),
         ]
         + WEIGHTS
         + GRADS
@@ -843,21 +861,25 @@
         critic,
         critic_target,
     )
-    shapes = [SDS((2,), f32), SDS((CAP, DEVS), f32)]
+    shapes = [SDS((2,), f32), SDS((2, CAP // 2, DEVS), f32)]
     places = [SDS((PA,), f32), SDS((2, PC), f32)] * 4 + [SDS((PA,), bf), SDS((2, PC), bf)]
     stat, prio, *outs = pl.pallas_call(
         update_kernel,
         out_shape=tuple(shapes + places),
-        in_specs=[any_] * 10,
+        in_specs=[any_] + [VM] * 8,
         out_specs=(VM,) + (any_,) * 11,
-        scratch_shapes=[pltpu.VMEM((PACK, 128), f32)]
-        + [pltpu.VMEM(p.shape, p.dtype) for p in places[:8] + places]
-        + [pltpu.VMEM((2, TILES_C * 128), f32), pltpu.SemaphoreType.DMA((4, 5)), pltpu.SemaphoreType.DMA((3, 5))],
+        scratch_shapes=[pltpu.VMEM(p.shape, p.dtype) for p in places]
+        + [
+            pltpu.VMEM((DEVS, CHUNKS[0], 128), f32),
+            pltpu.VMEM((DEVS, CHUNKS[1], 128), f32),
+            pltpu.VMEM((2, TILES_C * 128), f32),
+            pltpu.SemaphoreType.DMA((3,)),
+            pltpu.SemaphoreType.DMA((3, 5)),
+        ],
         compiler_params=pltpu.CompilerParams(vmem_limit_bytes=60 << 20),
         name="update",
     )(
         total,
-        prio,
         actor,
         critic,
         actor_momentum,
@@ -867,7 +889,7 @@
         actor_target,
         critic_target,
     )
-    return (stat, prio.T[None], *outs)
+    return (stat, prio.reshape(CAP, DEVS).T[None], *outs)
 
 
 def solution(mesh):

time: 85.3 us -> 83 us (0.973)
  Pallas kernels: 84.3 us -> 82.1 us
    pallas_call x1, Pallas kernels: 78.1 us -> 75.5 us  [local(): pl.pallas_call(functools.partial(step_kernel, WIDTH), out_shape=SDS(SUMS,...]
where the time goes in v6:
time: 83 us; the launch traced here: 82.9 us
  Pallas kernels  82.1 us (99%)
    pallas_call x1, Pallas kernels, local(): pl.pallas_call(functools.partial(step_kernel, WIDTH), out_shape=SDS(SUMS,...  75.5 us
    pallas_call x1, Pallas kernels, local(): pl.pallas_call(update_kernel, out_shape=tuple(shapes + places), in_specs=...  6.62 us

profile of v6, /device:TPU:1, one launch (start us, length us, event | category | flops | bytes accessed | tf_op | source)
XLA Modules:
  0.0 82.9 jit_solution(15216223604917870876)
XLA Ops:
  0.6 75.5 %td3_step.1.sum_hbm = f32[130,24,128]{2,1,0:T(8,128)} custom-call(f32[42,8192]{1,0:T(8,128)} %bitcast.12, s32[32,128]{1,0:T(8,128)} %bitcast.14, f32[6,32,128]{2,1,0:T(8,128)} %bitcast.13, s32[1,128]{1,0:T(1,128)} %count_hbm.1, f32[71942]{0:T(1024)} %refs_0_.1, f32[71942]{0:T(1024)} %refs_6_.1, f32[2,72193]{1,0:T(2,128)} %refs_1_.1, f32[2,72193]{1,0:T(2,128)} %refs_7_.1), custom_call_target="tpu_custom_call" | custom-call | tf_op jit(solution)/shard_map/td3_step/pallas_call | solution.py:818
  76.1 6.6 %update.1 = (f32[2]{0:T(128)}, f32[2,16,128]{2,1,0:T(8,128)}, f32[71942]{0:T(1024)}, f32[2,72193]{1,0:T(2,128)}, f32[71942]{0:T(1024)}, /*index=5*/f32[2,72193]{...) custom-call(f32[130,24,128]{2,1,0:T(8,128)} %td3_step.1.sum_hbm, ...), custom_call_target="tpu_custom_call" | custom-call | tf_op jit(solution)/shard_map/update/pallas_call | solution.py:866

commit v7 on v6

--- a/solution.py
+++ b/solution.py
@@ -37,8 +37,9 @@
 CHUNKS = (9, 5)
 AT_ACTOR = 2 * CHIPS * CHUNKS[0]
 PACK = AT_ACTOR + 2 * CHIPS * CHUNKS[1]
-PLACES = (0, 16)
-SUMS = (DEVS + 2, 24, 128)
+AT_PRIO = DEVS
+AT_SUM = DEVS + 2
+RESULT = (3700, 16, 128)
 TURN = 512
 WIDTH = 1024
 STEPS = sorted(
@@ -318,7 +319,7 @@
             prio = valid * jnp.sqrt(delta * delta + 1.0)
             tiles = width // 128
             for t in range(tiles):
-                prio_ref[pl.ds(i * tiles + t, 1), :] = prio[:, 128 * t : 128 * (t + 1)]
+                prio_ref[(i * tiles) // 16, pl.ds(lax.rem(i * tiles, 16) + t, 1), :] = prio[:, 128 * t : 128 * (t + 1)]
         st_ref[0:1, :] += fold(valid * (delta * delta))
         dq = (2.0 * scaled) * delta
         st_ref[2 + net : 3 + net, :] += fold(dq)
@@ -467,11 +468,16 @@
 class Sum:
     def __init__(self, place, g, pack_ref, out, buffers, sems):
         self.place, self.chunk = place, CHUNKS[g]
-        self.out = out.at[pl.ds(place.core * CHIPS, CHIPS), pl.ds(PLACES[g], self.chunk)]
+        self.late = g == 0
         self.first = (0, AT_ACTOR)[g]
         self.rows = CHIPS * self.chunk
         self.pack_ref = pack_ref
-        self.other, self.half, self.parts, self.mine, self.whole = buffers
+        self.other, self.half, self.parts, self.mine, self.both = buffers
+        self.whole = self.both.at[place.core]
+        if self.late:
+            self.out = out.at[pl.ds(place.core * CHIPS, CHIPS), pl.ds(0, self.chunk)]
+        else:
+            self.out = self.whole
         self.sems = sems.at[g]
 
     def remote(self, src, dst, n, to):
@@ -507,10 +513,10 @@
             self.remote(self.mine, self.whole.at[chip], 2, device).start()
 
     def back_copies(self):
-        return (
-            pltpu.make_async_copy(self.whole, self.out, self.sems.at[8]),
-            self.remote(self.whole, self.out, 3, self.place.sibling),
-        )
+        copies = [self.remote(self.whole, self.out, 3, self.place.sibling)]
+        if self.late:
+            copies.append(pltpu.make_async_copy(self.whole, self.out, self.sems.at[8]))
+        return copies
 
     def back(self):
         drain(self.parts, self.sems.at[4], CHIPS - 1)
@@ -522,6 +528,12 @@
     def finish(self):
         for copy in self.back_copies():
             copy.wait()
+
+    def in_order(self, flat_ref):
+        for core in range(2):
+            for j in range(self.chunk):
+                at = (core * self.chunk + j) * CHIPS
+                flat_ref[at // 16 : (at + CHIPS) // 16] = self.both[core, :, j, :].reshape(CHIPS // 16, 16, 128)
 
 
 def sum_buffers():
@@ -532,7 +544,7 @@
             pltpu.VMEM((CHIPS, chunk, 128), f32),
             pltpu.VMEM((CHIPS, chunk, 128), f32),
             pltpu.VMEM((chunk, 128), f32),
-            pltpu.VMEM((CHIPS, chunk, 128), f32),
+            pltpu.VMEM((2, CHIPS, chunk, 128), f32),
         ]
     return out
 
@@ -549,6 +561,7 @@
     critic_t_hbm,
     out_hbm,
     prio_ref,
+    order_ref,
     table_ref,
     index_ref,
     noise_ref,
@@ -605,15 +618,15 @@
                 yield device[0] * 8 + device[1], device
         yield place.sibling_at, place.sibling
 
-    for _, device in all_others():
-        pl.semaphore_signal(barrier, inc=1, device_id=device, device_id_type=MESH)
     for ref in grads:
         ref[...] = jnp.zeros_like(ref)
     loads[0].wait()
+    loads[1].wait()
+    for _, device in all_others():
+        pl.semaphore_signal(barrier, inc=1, device_id=device, device_id_type=MESH)
     prepare_critics(
         critic_ref, flat_ref, pad_ref, C0, w1_ref, w2f_ref, w2b_ref, b2_ref, w3_ref, b3_ref, w1a_ref
     )
-    loads[1].wait()
     prepare_actor(
         A, actor_ref, flat_ref, pad_ref, w1_ref, w2f_ref, w2b_ref, b2_ref, w3t_ref, w3b_ref, b3a_ref
     )
@@ -649,8 +662,16 @@
 
         @pl.when(i == 0)
         def _():
+            loads[6].wait()
+            loads[7].wait()
             pl.semaphore_wait(barrier, DEVS - 1)
             send()
+            prepare_critics(
+                critic_t_ref, flat_ref, pad_ref, T0, w1_ref, w2f_ref, w2b_ref, b2_ref, w3_ref, b3_ref, w1a_ref
+            )
+            prepare_actor(
+                AT, actor_t_ref, flat_ref, pad_ref, w1_ref, w2f_ref, w2b_ref, b2_ref, w3t_ref, w3b_ref, b3a_ref
+            )
 
         return carry
 
@@ -659,14 +680,6 @@
     late, early = (Sum(place, g, pack_ref, out_hbm, buffers[5 * g : 5 * g + 5], sems) for g in range(2))
     early.swap().start()
 
-    loads[6].wait()
-    prepare_critics(
-        critic_t_ref, flat_ref, pad_ref, T0, w1_ref, w2f_ref, w2b_ref, b2_ref, w3_ref, b3_ref, w1a_ref
-    )
-    loads[7].wait()
-    prepare_actor(
-        AT, actor_t_ref, flat_ref, pad_ref, w1_ref, w2f_ref, w2b_ref, b2_ref, w3t_ref, w3b_ref, b3a_ref
-    )
     drain(nsend, noise_sems.at[0], DEVS - 1)
     drain(nrecv, noise_sems.at[1], DEVS - 1)
     nrecv[pl.ds(me, 1)] = nsend[pl.ds(me, 1)]
@@ -694,20 +707,17 @@
     lax.fori_loop(0, blocks, critics, 0)
     pack_critics(pack_ref, grads)
     late.swap().start()
-    prios = [
-        pltpu.make_async_copy(
-            prio_ref.at[pl.ds(16 * n, 16)], out_hbm.at[DEVS + n, pl.ds(0, 16)], in_sems.at[n]
-        )
-        for n in range(2)
-    ]
-    for copy in prios:
-        copy.start()
+    prios = pltpu.make_async_copy(prio_ref, out_hbm.at[pl.ds(AT_PRIO, 2)], in_sems.at[0])
+    prios.start()
+    early.finish()
     late.swap().wait()
     late.scatter()
-    early.finish()
-    for copy in prios:
-        copy.wait()
+    early.in_order(order_ref)
+    order = pltpu.make_async_copy(order_ref, out_hbm.at[pl.ds(AT_SUM, order_ref.shape[0])], in_sems.at[1])
+    order.start()
+    prios.wait()
     late.spread()
+    order.wait()
     late.back()
     late.finish()
 
@@ -726,16 +736,15 @@
 
 def update_kernel(sum_hbm, *refs):
     ins, stat_ref, prio_out, outs_hbm, outs = refs[:8], refs[8], refs[9], refs[10:20], refs[20:30]
-    late_ref, early_ref, grad_ref, in_sems, out_sems = refs[30:]
-    loads = [
-        pltpu.make_async_copy(
-            sum_hbm.at[pl.ds(0, DEVS), pl.ds(PLACES[g], CHUNKS[g])], (late_ref, early_ref)[g], in_sems.at[g]
-        )
-        for g in range(2)
-    ]
-    for load in loads:
+    late_ref, early_ref, count_ref, grad_ref, in_sems, out_sems = refs[30:]
+    early = pltpu.make_async_copy(sum_hbm.at[pl.ds(AT_SUM, early_ref.shape[0])], early_ref, in_sems.at[0])
+    late = pltpu.make_async_copy(sum_hbm.at[pl.ds(0, DEVS), pl.ds(0, CHUNKS[0])], late_ref, in_sems.at[1])
+    stat_core, stat_row = divmod(STAT, CHIPS * CHUNKS[0])
+    stat_at = stat_core * CHIPS + stat_row % CHIPS
+    count = pltpu.make_async_copy(sum_hbm.at[pl.ds(stat_at, 1), pl.ds(0, CHUNKS[0])], count_ref, in_sems.at[3])
+    for load in (count, early, late):
         load.start()
-    pass_on = pltpu.make_async_copy(sum_hbm.at[pl.ds(DEVS, 2), pl.ds(0, 16)], prio_out, in_sems.at[2])
+    pass_on = pltpu.make_async_copy(sum_hbm.at[pl.ds(AT_PRIO, 2)], prio_out, in_sems.at[2])
     pass_on.start()
 
     def stores(piece):
@@ -748,17 +757,11 @@
             out.append(pltpu.make_async_copy(src, dst, out_sems.at[piece, n]))
         return out
 
-    for load in loads:
-        load.wait()
-
-    def rows(g, r, n):
-        core, r = divmod(r, CHIPS * CHUNKS[g])
-        j, k = divmod(r, CHIPS)
-        return (late_ref, early_ref)[g][core * CHIPS + k : core * CHIPS + k + n, j, :]
-
-    stat = rows(0, STAT, 1)
+    count.wait()
+    stat = count_ref[0, stat_row // CHIPS : stat_row // CHIPS + 1, :]
     factor = (1.0 / SCALE) / stat[:, 1:2]
     stat_ref[...] = stat[:, :2].reshape(2)
+    early.wait()
 
     def actor(s, grad):
         values = update(ins[0][s], grad, ins[2][s], ins[4][s], ins[6][s])
@@ -766,18 +769,18 @@
             ref[s] = value
 
     for i in range(PA // STEP):
-        actor(slice(STEP * i, STEP * (i + 1)), (rows(1, 8 * i, 8) * factor).reshape(STEP))
+        actor(slice(STEP * i, STEP * (i + 1)), (early_ref[i // 2, 8 * (i % 2) : 8 * (i % 2) + 8, :] * factor).reshape(STEP))
     done = PA // STEP * STEP
-    r = done // 128
+    last = early_ref[done // 2048, done // 128 % 16 : done // 128 % 16 + 8, :] * factor
     more = (PA - done) // 128
-    actor(slice(done, done + 128 * more), (rows(1, r, more) * factor).reshape(128 * more))
+    actor(slice(done, done + 128 * more), last[:more].reshape(128 * more))
     done += 128 * more
-    actor(slice(done, PA), (rows(1, r + more, 1)[:, :ACT] * factor).reshape(ACT))
+    actor(slice(done, PA), last[more : more + 1, :ACT].reshape(ACT))
     for store in stores(0):
         store.start()
 
     def critic(s):
-        values = update(ins[1][:, s], grad_ref[:, s], ins[3][:, s], ins[5][:, s], ins[7][:, s])
+        values = update(ins[1][:, s], grad_ref[:, s] * factor, ins[3][:, s], ins[5][:, s], ins[7][:, s])
         for ref, value in zip(outs[1::2], values):
             ref[:, s] = value
 
@@ -785,8 +788,12 @@
         critic(pl.ds(pl.multiple_of(i * STEP, STEP), STEP))
         return carry
 
+    late.wait()
     for t in range(TILES_C):
-        grad_ref[:, 128 * t : 128 * (t + 1)] = rows(0, 2 * t, 2) * factor
+        core, r = divmod(2 * t, CHIPS * CHUNKS[0])
+        j, k = divmod(r, CHIPS)
+        k += core * CHIPS
+        grad_ref[:, 128 * t : 128 * (t + 1)] = late_ref[k : k + 2, j, :]
     for piece in (1, 2):
         lax.fori_loop(CUTS[piece - 1] // STEP, CUTS[piece] // STEP, critics, 0, unroll=5)
         if piece == 2:
@@ -817,11 +824,12 @@
     any_ = pl.BlockSpec(memory_space=pl.ANY)
     total = pl.pallas_call(
         functools.partial(step_kernel, WIDTH),
-        out_shape=SDS(SUMS, f32),
+        out_shape=SDS(RESULT, f32),
         in_specs=[any_] * 8,
         out_specs=any_,
         scratch_shapes=[
-            pltpu.VMEM((CAP, DEVS), f32),
+            pltpu.VMEM((2, 16, DEVS), f32),
+            pltpu.VMEM((2 * CHIPS * CHUNKS[1] // 16, 16, 128), f32),
             pltpu.VMEM((ROW, R_DEV), f32),
             pltpu.SMEM((CAP, DEVS), jnp.int32),
             pltpu.VMEM((ACT, CAP, DEVS), f32),
@@ -871,12 +879,13 @@
         scratch_shapes=[pltpu.VMEM(p.shape, p.dtype) for p in places]
         + [
             pltpu.VMEM((DEVS, CHUNKS[0], 128), f32),
-            pltpu.VMEM((DEVS, CHUNKS[1], 128), f32),
+            pltpu.VMEM((2 * CHIPS * CHUNKS[1] // 16, 16, 128), f32),
+            pltpu.VMEM((1, CHUNKS[0], 128), f32),
             pltpu.VMEM((2, TILES_C * 128), f32),
-            pltpu.SemaphoreType.DMA((3,)),
+            pltpu.SemaphoreType.DMA((4,)),
             pltpu.SemaphoreType.DMA((3, 5)),
         ],
-        compiler_params=pltpu.CompilerParams(vmem_limit_bytes=60 << 20),
+        compiler_params=pltpu.CompilerParams(vmem_limit_bytes=24 << 20),
         name="update",
     )(
         total,

time: 83 us -> 81.3 us (0.980)
  Pallas kernels: 82.1 us -> 80.2 us
    pallas_call x1, Pallas kernels: 6.62 us -> 4.43 us  [local(): pl.pallas_call(update_kernel, out_shape=tuple(shapes + places), in_specs=...]
where the time goes in v7:
time: 81.3 us; the launch traced here: 81.1 us
  Pallas kernels  80.2 us (99%)
  between operations  0.94 us (1%)
    pallas_call x1, Pallas kernels, local(): pl.pallas_call(functools.partial(step_kernel, WIDTH), out_shape=SDS(RESUL...  75.7 us
    pallas_call x1, Pallas kernels, local(): pl.pallas_call(update_kernel, out_shape=tuple(shapes + places), in_specs=...  4.43 us

profile of v7, /device:TPU:1, one launch (start us, length us, event | category | flops | bytes accessed | tf_op | source)
XLA Modules:
  0.0 81.1 jit_solution(14037216209874475215)
XLA Ops:
  0.6 0.0 copy-start.1
  0.7 0.0 copy-start.3
  0.7 0.0 copy-start
  0.7 0.0 copy-start.2
  0.7 0.0 copy-start.5
  0.7 0.0 copy-start.7
  0.7 0.0 copy-start.4
  0.7 0.0 copy-start.6
  0.7 75.7 %td3_step.1.sum_hbm = f32[3700,16,128]{2,1,0:T(8,128)} custom-call(f32[42,8192]{1,0:T(8,128)} %bitcast.12, s32[32,128]{1,0:T(8,128)} %bitcast.14, f32[6,32,128]{2,1,0:T(8,128)} %bitcast.13, s32[1,128]{1,0:T(1,128)} %count_hbm.1, f32[71942]{0:T(1024)} %refs_0_.1, f32[71942]{0:T(1024)} %refs_6_.1, f32[2,72193]{1,0:T(2,128)} %refs_1_.1, f32[2,72193]{1,0:T(2,128)} %refs_7_.1), custom_call_target="tpu_custom_call" | custom-call | tf_op jit(solution)/shard_map/td3_step/pallas_call | solution.py:825
  76.5 0.0 copy-done.1
  76.5 0.0 copy-done.3
  76.5 0.0 copy-done
  76.5 0.0 copy-done.2
  76.5 0.0 copy-done.5
  76.5 0.0 copy-done.7
  76.5 0.0 copy-done.4
  76.5 0.0 copy-done.6
  76.5 4.4 %update.1 = (f32[2]{0:T(128)}, f32[2,16,128]{2,1,0:T(8,128)}, f32[71942]{0:T(1024)}, f32[2,72193]{1,0:T(2,128)}, f32[71942]{0:T(1024)}, /*index=5*/f32[2,72193]{...) custom-call(f32[3700,16,128]{2,1,0:T(8,128)} %td3_step.1.sum_hbm, ...), custom_call_target="tpu_custom_call" | custom-call | tf_op jit(solution)/shard_map/update/pallas_call | solution.py:874
Async XLA Ops:
  0.6 75.8 %copy-start.1 = (f32[2,72193]{1,0:T(2,128)S(1)}, f32[2,72193]{1,0:T(2,128)}, u32[]{:S(2)}) copy-start(f32[2,72193]{1,0:T(2,128)} %refs_7_.1) | copy-start | bytes 1732636
  0.7 75.8 %copy-start.3 = (f32[71942]{0:T(1024)S(1)}, f32[71942]{0:T(1024)}, u32[]{:S(2)}) copy-start(f32[71942]{0:T(1024)} %refs_6_.1) | copy-start | bytes 863308
  0.7 75.8 %copy-start = (f32[2,72193]{1,0:T(2,128)S(1)}, f32[2,72193]{1,0:T(2,128)}, u32[]{:S(2)}) copy-start(f32[2,72193]{1,0:T(2,128)} %refs_1_.1) | copy-start | bytes 1732636
  0.7 75.8 %copy-start.2 = (f32[71942]{0:T(1024)S(1)}, f32[71942]{0:T(1024)}, u32[]{:S(2)}) copy-start(f32[71942]{0:T(1024)} %refs_0_.1) | copy-start | bytes 863308
  0.7 75.8 %copy-start.5 = (f32[2,72193]{1,0:T(2,128)S(1)}, f32[2,72193]{1,0:T(2,128)}, u32[]{:S(2)}) copy-start(f32[2,72193]{1,0:T(2,128)} %refs_5_.1) | copy-start | bytes 1732636
  0.7 75.8 %copy-start.7 = (f32[71942]{0:T(1024)S(1)}, f32[71942]{0:T(1024)}, u32[]{:S(2)}) copy-start(f32[71942]{0:T(1024)} %refs_4_.1) | copy-start | bytes 863308
  0.7 75.8 %copy-start.4 = (f32[2,72193]{1,0:T(2,128)S(1)}, f32[2,72193]{1,0:T(2,128)}, u32[]{:S(2)}) copy-start(f32[2,72193]{1,0:T(2,128)} %refs_3_.1) | copy-start | bytes 1732636
  0.7 75.8 %copy-start.6 = (f32[71942]{0:T(1024)S(1)}, f32[71942]{0:T(1024)}, u32[]{:S(2)}) copy-start(f32[71942]{0:T(1024)} %refs_2_.1) | copy-start | bytes 863308

commit v8 on v7

--- a/solution.py
+++ b/solution.py
@@ -276,8 +276,14 @@
 
     def grads2(self, net, h1, dz2, g2_ref):
         u = UNITS
-        left = jnp.concatenate([h1[:u], h1[u : 2 * u], h1[:u]], 1)
-        g2_ref[net] += dot_nt(left, jnp.concatenate([dz2[:u], dz2[:u], dz2[u : 2 * u]], 1))
+        right = jnp.concatenate([dz2[:u], dz2[:u], dz2[u : 2 * u]], 1)
+        hi, lo = h1[:u], h1[u : 2 * u]
+        if net == A:
+            g2_ref[net, :u, :] += dot_nt(jnp.concatenate([hi, lo, hi], 1), right)
+        else:
+            hi = jnp.concatenate([hi, jnp.ones((16, self.width), bf)], 0)
+            lo = jnp.concatenate([lo, jnp.zeros((16, self.width), bf)], 0)
+            g2_ref[net] += dot_nt(jnp.concatenate([hi, lo, hi], 1), right)
 
     def grads1(self, net, dz1, g1_ref):
         xhi, xlo = self.x3[:FEAT], self.x3[FEAT : 2 * FEAT]
@@ -325,7 +331,6 @@
         st_ref[2 + net : 3 + net, :] += fold(dq)
         dw3_ref[net] += fold(s * dq)
         dz2 = lanes(st.w3[net], width) * (0.5 * dq) * d2
-        db2_ref[net] += fold(dz2)
         return three(dz2)
 
     u, s = st.first(C1, x3)
@@ -369,7 +374,7 @@
     stacked = jnp.concatenate([hi, lo, hi, zero], 0).astype(bf)
     left = jnp.concatenate([jnp.concatenate([hi, lo], 0), jnp.concatenate([hi, zero], 0)], 1).astype(bf)
     dz2 = dot(st.w3b[:, :32], stacked) * d2a
-    db2_ref[A] += fold(dz2)
+    db2_ref[...] += fold(dz2)
     dz2 = three(dz2)
     dz1 = dot(st.w2b[A], dz2) * d1a
     g3a_ref[...] += dot_nt(left, jnp.concatenate([h2a[:UNITS], h2a[UNITS : 2 * UNITS]], 1))
@@ -387,14 +392,14 @@
     sums = jnp.sum(st_ref[...], 1, keepdims=True)
     for c in range(2):
         g1 = g1_ref[c, :FEAT, :] + g1_ref[c, FEAT:, :]
-        b2 = lane_sums(db2_ref[c])[0:1]
+        b2 = g2_ref[c, UNITS : UNITS + 1, :]
         w3 = lane_sums(dw3_ref[c])[0:1]
         for half in range(2):
             s = slice(128 * half, 128 * (half + 1))
             at = c + 2 * half
             pack_ref[pl.ds(at, OBS + ACT, stride=4), :] = g1[: OBS + ACT, s]
             pack_ref[at + 92 : at + 93, :] = g1[ONE : ONE + 1, s]
-            pack_ref[pl.ds(at + 96, UNITS, stride=4), :] = g2_ref[c, :, s]
+            pack_ref[pl.ds(at + 96, UNITS, stride=4), :] = g2_ref[c, :UNITS, s]
             pack_ref[at + 1120 : at + 1121, :] = b2[:, s]
             pack_ref[at + 1124 : at + 1125, :] = w3[:, s]
         pack_ref[c + 1128 : c + 1129, :] = jnp.where(lane == 0, sums[2 + c : 3 + c], 0.0)
@@ -406,13 +411,13 @@
     g2_ref, g1_ref, g3a_ref, db2_ref, dw3_ref, st_ref = grads
     sums = jnp.sum(st_ref[...], 1, keepdims=True)
     g1 = g1_ref[A, :FEAT, :] + g1_ref[A, FEAT:, :]
-    b2 = lane_sums(db2_ref[A])[0:1]
+    b2 = lane_sums(db2_ref[...])[0:1]
     o = AT_ACTOR
     for half in range(2):
         s = slice(128 * half, 128 * (half + 1))
         pack_ref[pl.ds(o + half, OBS, stride=2), :] = g1[:OBS, s]
         pack_ref[o + 34 + half : o + 35 + half, :] = g1[ONE : ONE + 1, s]
-        pack_ref[pl.ds(o + 36 + half, UNITS, stride=2), :] = g2_ref[A, :, s]
+        pack_ref[pl.ds(o + 36 + half, UNITS, stride=2), :] = g2_ref[A, :UNITS, s]
         pack_ref[o + 548 + half : o + 549 + half, :] = b2[:, s]
     pack_ref[o + 550 : o + 562, :] = head_back(g3a_ref[:8, :] + g3a_ref[8:, :])[:12]
     e = lax.broadcasted_iota(jnp.int32, (8, 128), 1) == lax.broadcasted_iota(jnp.int32, (8, 128), 0) - 1
@@ -433,10 +438,10 @@
     pltpu.VMEM((16, 3 * UNITS), bf),
 ]
 GRADS = [
-    pltpu.VMEM((3, UNITS, UNITS), f32),
+    pltpu.VMEM((3, UNITS + 16, UNITS), f32),
     pltpu.VMEM((3, 2 * FEAT, UNITS), f32),
     pltpu.VMEM((16, UNITS), f32),
-    pltpu.VMEM((3, UNITS, 128), f32),
+    pltpu.VMEM((UNITS, 128), f32),
     pltpu.VMEM((2, UNITS, 128), f32),
     pltpu.VMEM((16, 128), f32),
 ]
@@ -618,12 +623,17 @@
                 yield device[0] * 8 + device[1], device
         yield place.sibling_at, place.sibling
 
+    def greet(devices):
+        for _, device in devices:
+            pl.semaphore_signal(barrier, inc=1, device_id=device, device_id_type=MESH)
+
+    names = list(all_others())
+    greet(names[:80])
     for ref in grads:
         ref[...] = jnp.zeros_like(ref)
     loads[0].wait()
     loads[1].wait()
-    for _, device in all_others():
-        pl.semaphore_signal(barrier, inc=1, device_id=device, device_id_type=MESH)
+    greet(names[80:])
     prepare_critics(
         critic_ref, flat_ref, pad_ref, C0, w1_ref, w2f_ref, w2b_ref, b2_ref, w3_ref, b3_ref, w1a_ref
     )
@@ -644,7 +654,7 @@
     turn_noise(noise_ref, q_ref, nsend)
 
     def send():
-        for peer, device in all_others():
+        for peer, device in names:
             pltpu.make_async_remote_copy(
                 src_ref=nsend.at[peer],
                 dst_ref=nrecv.at[me],
@@ -731,7 +741,8 @@
 
 
 STEP = 1024
-CUTS = (0, 35 * STEP, PC)
+CUTS = (0, 24 * STEP, 44 * STEP, 60 * STEP, PC)
+LAST = len(CUTS) - 1
 
 
 def update_kernel(sum_hbm, *refs):
@@ -789,19 +800,19 @@
         return carry
 
     late.wait()
-    for t in range(TILES_C):
-        core, r = divmod(2 * t, CHIPS * CHUNKS[0])
-        j, k = divmod(r, CHIPS)
-        k += core * CHIPS
-        grad_ref[:, 128 * t : 128 * (t + 1)] = late_ref[k : k + 2, j, :]
-    for piece in (1, 2):
-        lax.fori_loop(CUTS[piece - 1] // STEP, CUTS[piece] // STEP, critics, 0, unroll=5)
-        if piece == 2:
+    for piece in range(1, LAST + 1):
+        for t in range(CUTS[piece - 1] // 128, -(-CUTS[piece] // 128)):
+            core, r = divmod(2 * t, CHIPS * CHUNKS[0])
+            j, k = divmod(r, CHIPS)
+            k += core * CHIPS
+            grad_ref[:, 128 * t : 128 * (t + 1)] = late_ref[k : k + 2, j, :]
+        lax.fori_loop(CUTS[piece - 1] // STEP, CUTS[piece] // STEP, critics, 0, unroll=4)
+        if piece == LAST:
             done = PC // STEP * STEP
             critic(pl.ds(done, PC - done))
         for store in stores(piece):
             store.start()
-    for piece in range(3):
+    for piece in range(LAST + 1):
         for store in stores(piece):
             store.wait()
     pass_on.wait()
@@ -883,7 +894,7 @@
             pltpu.VMEM((1, CHUNKS[0], 128), f32),
             pltpu.VMEM((2, TILES_C * 128), f32),
             pltpu.SemaphoreType.DMA((4,)),
-            pltpu.SemaphoreType.DMA((3, 5)),
+            pltpu.SemaphoreType.DMA((LAST + 1, 5)),
         ],
         compiler_params=pltpu.CompilerParams(vmem_limit_bytes=24 << 20),
         name="update",

time: 81.3 us -> 80.2 us (0.986)
  Pallas kernels: 80.2 us -> 79.1 us
where the time goes in v8:
time: 80.2 us; the launch traced here: 80.1 us
  Pallas kernels  79.1 us (99%)
  between operations  0.94 us (1%)
    pallas_call x1, Pallas kernels, local(): pl.pallas_call(functools.partial(step_kernel, WIDTH), out_shape=SDS(RESUL...  75 us
    pallas_call x1, Pallas kernels, local(): pl.pallas_call(update_kernel, out_shape=tuple(shapes + places), in_specs=...  4.14 us

profile of v8, /device:TPU:1, one launch (start us, length us, event | category | flops | bytes accessed | tf_op | source)
XLA Modules:
  0.0 80.1 jit_solution(1301029665556601560)
XLA Ops:
  0.6 0.0 copy-start.1
  0.7 0.0 copy-start.3
  0.7 0.0 copy-start
  0.7 0.0 copy-start.2
  0.7 0.0 copy-start.5
  0.7 0.0 copy-start.7
  0.7 0.0 copy-start.4
  0.7 0.0 copy-start.6
  0.7 75.0 %td3_step.1.sum_hbm = f32[3700,16,128]{2,1,0:T(8,128)} custom-call(f32[42,8192]{1,0:T(8,128)} %bitcast.12, s32[32,128]{1,0:T(8,128)} %bitcast.14, f32[6,32,128]{2,1,0:T(8,128)} %bitcast.13, s32[1,128]{1,0:T(1,128)} %count_hbm.1, f32[71942]{0:T(1024)} %refs_0_.1, f32[71942]{0:T(1024)} %refs_6_.1, f32[2,72193]{1,0:T(2,128)} %refs_1_.1, f32[2,72193]{1,0:T(2,128)} %refs_7_.1), custom_call_target="tpu_custom_call" | custom-call | tf_op jit(solution)/shard_map/td3_step/pallas_call | solution.py:836
  75.7 0.0 copy-done.1
  75.7 0.0 copy-done.3
  75.7 0.0 copy-done
  75.7 0.0 copy-done.2
  75.8 0.0 copy-done.5
  75.8 0.0 copy-done.7
  75.8 0.0 copy-done.4
  75.8 0.0 copy-done.6
  75.8 4.1 %update.1 = (f32[2]{0:T(128)}, f32[2,16,128]{2,1,0:T(8,128)}, f32[71942]{0:T(1024)}, f32[2,72193]{1,0:T(2,128)}, f32[71942]{0:T(1024)}, /*index=5*/f32[2,72193]{...) custom-call(f32[3700,16,128]{2,1,0:T(8,128)} %td3_step.1.sum_hbm, ...), custom_call_target="tpu_custom_call" | custom-call | tf_op jit(solution)/shard_map/update/pallas_call | solution.py:885
Async XLA Ops:
  0.6 75.1 %copy-start.1 = (f32[2,72193]{1,0:T(2,128)S(1)}, f32[2,72193]{1,0:T(2,128)}, u32[]{:S(2)}) copy-start(f32[2,72193]{1,0:T(2,128)} %refs_7_.1) | copy-start | bytes 1732636
  0.7 75.1 %copy-start.3 = (f32[71942]{0:T(1024)S(1)}, f32[71942]{0:T(1024)}, u32[]{:S(2)}) copy-start(f32[71942]{0:T(1024)} %refs_6_.1) | copy-start | bytes 863308
  0.7 75.1 %copy-start = (f32[2,72193]{1,0:T(2,128)S(1)}, f32[2,72193]{1,0:T(2,128)}, u32[]{:S(2)}) copy-start(f32[2,72193]{1,0:T(2,128)} %refs_1_.1) | copy-start | bytes 1732636
  0.7 75.1 %copy-start.2 = (f32[71942]{0:T(1024)S(1)}, f32[71942]{0:T(1024)}, u32[]{:S(2)}) copy-start(f32[71942]{0:T(1024)} %refs_0_.1) | copy-start | bytes 863308
  0.7 75.1 %copy-start.5 = (f32[2,72193]{1,0:T(2,128)S(1)}, f32[2,72193]{1,0:T(2,128)}, u32[]{:S(2)}) copy-start(f32[2,72193]{1,0:T(2,128)} %refs_5_.1) | copy-start | bytes 1732636
  0.7 75.1 %copy-start.7 = (f32[71942]{0:T(1024)S(1)}, f32[71942]{0:T(1024)}, u32[]{:S(2)}) copy-start(f32[71942]{0:T(1024)} %refs_4_.1) | copy-start | bytes 863308
  0.7 75.1 %copy-start.4 = (f32[2,72193]{1,0:T(2,128)S(1)}, f32[2,72193]{1,0:T(2,128)}, u32[]{:S(2)}) copy-start(f32[2,72193]{1,0:T(2,128)} %refs_3_.1) | copy-start | bytes 1732636
  0.7 75.1 %copy-start.6 = (f32[71942]{0:T(1024)S(1)}, f32[71942]{0:T(1024)}, u32[]{:S(2)}) copy-start(f32[71942]{0:T(1024)} %refs_2_.1) | copy-start | bytes 863308

commit v9 on v8

--- a/solution.py
+++ b/solution.py
@@ -34,9 +34,11 @@
 STAT = 1130
 ROWS_A = 563
 CHIPS = DEVS // 2
-CHUNKS = (9, 5)
-AT_ACTOR = 2 * CHIPS * CHUNKS[0]
-PACK = AT_ACTOR + 2 * CHIPS * CHUNKS[1]
+PLANE = 16
+CHUNK = 9
+CHUNK_A = 20
+AT_ACTOR = 2 * CHIPS * CHUNK
+PACK = AT_ACTOR + 2 * PLANE * CHUNK_A
 AT_PRIO = DEVS
 AT_SUM = DEVS + 2
 RESULT = (3700, 16, 128)
@@ -90,14 +92,56 @@
     for j in range(ACT):
         q_ref[pl.ds(j + 1, CAP, stride=8), :] = 0.5 * jnp.tanh(0.4 * noise_ref[j])
     turned = jnp.transpose(q_ref[...])
-    nsend[:, 0, :] = turned[:, :128]
-    nsend[:, 1, :] = turned[:, 128:]
-
-
-def noise_back(nrecv, nz_ref):
-    back = jnp.transpose(jnp.concatenate([nrecv[:, 0, :], nrecv[:, 1, :]], 1))
+    nsend[:, :, :, :, 0, :] = turned[:, :128].reshape(4, 4, 4, 2, 128)
+    nsend[:, :, :, :, 1, :] = turned[:, 128:].reshape(4, 4, 4, 2, 128)
+
+
+def noise_back(nrecv, turned_ref, nz_ref):
+    for d in range(DEVS):
+        core, y, x, z = d % 2, d // 2 % 4, d // 8 % 4, d // 32
+        for half in range(2):
+            turned_ref[d : d + 1, 128 * half : 128 * (half + 1)] = nrecv[core, y, x, z, half : half + 1, :]
+    back = jnp.transpose(turned_ref[...])
     for c in range(CAP):
         nz_ref[:, 128 * c : 128 * (c + 1)] = back[8 * c : 8 * (c + 1), :]
+
+
+class Exchange:
+    def __init__(self, place, buffers, sems):
+        self.place, self.sems = place, sems
+        self.buffers = buffers
+
+    def slab(self, stage, n):
+        p, (send, by_z, by_x, by_y, by_core) = self.place, self.buffers
+        if stage == 0:
+            return send.at[p.zs[n]], by_z.at[p.zs[0]], (p.zs[n] * 4 + p.xs[0], p.shard)
+        if stage == 1:
+            return by_z.at[:, p.xs[n]], by_x.at[p.xs[0]], (p.zs[0] * 4 + p.xs[n], p.shard)
+        if stage == 2:
+            return by_x.at[:, :, p.ys[n]], by_y.at[p.ys[0]], (p.group, p.ys[n] * 2 + p.core)
+        return by_y.at[:, :, :, (1 - p.core) if n else p.core], by_core.at[p.core], p.sibling
+
+    def start(self, stage):
+        for n in range(1, 2 if stage == 3 else 4):
+            src, dst, device = self.slab(stage, n)
+            pltpu.make_async_remote_copy(
+                src_ref=src,
+                dst_ref=dst,
+                send_sem=self.sems.at[2 * stage],
+                recv_sem=self.sems.at[2 * stage + 1],
+                device_id=device,
+                device_id_type=MESH,
+            ).start()
+        src, dst, _ = self.slab(stage, 0)
+        dst[...] = src[...]
+
+    def wait(self, stage):
+        if stage == 3:
+            view = self.buffers[4].at[0]
+        else:
+            view = self.buffers[stage + 1].at[pl.ds(0, 3)]
+        for n in range(2):
+            pltpu.make_async_copy(view, view, self.sems.at[2 * stage + n]).wait()
 
 
 def turn_table(i, table_ref, rows_ref):
@@ -455,58 +499,61 @@
 class Place:
     def __init__(self):
         group, shard = lax.axis_index("group"), lax.axis_index("shard")
+        self.group, self.shard = group, shard
         self.core = lax.rem(shard, 2)
         z, x, y = group // 4, lax.rem(group, 4), shard // 2
         self.chip = group * 4 + y
         self.sibling = (group, shard + 1 - 2 * self.core)
-        self.sibling_at = group * 8 + shard + 1 - 2 * self.core
-        self.me = group * 8 + shard
         self.zs, self.xs, self.ys = ([lax.rem(v + n, 4) for n in range(4)] for v in (z, x, y))
 
-    def others(self, other_core=False):
-        core = 1 - self.core if other_core else self.core
+    def others(self):
         for dz, dx, dy in STEPS:
             group = self.zs[dz] * 4 + self.xs[dx]
-            yield group * 4 + self.ys[dy], (group, self.ys[dy] * 2 + core)
-
-
-class Sum:
-    def __init__(self, place, g, pack_ref, out, buffers, sems):
-        self.place, self.chunk = place, CHUNKS[g]
-        self.late = g == 0
-        self.first = (0, AT_ACTOR)[g]
-        self.rows = CHIPS * self.chunk
-        self.pack_ref = pack_ref
-        self.other, self.half, self.parts, self.mine, self.both = buffers
-        self.whole = self.both.at[place.core]
-        if self.late:
-            self.out = out.at[pl.ds(place.core * CHIPS, CHIPS), pl.ds(0, self.chunk)]
-        else:
-            self.out = self.whole
-        self.sems = sems.at[g]
-
-    def remote(self, src, dst, n, to):
-        return pltpu.make_async_remote_copy(
-            src_ref=src,
-            dst_ref=dst,
-            send_sem=self.sems.at[2 * n],
-            recv_sem=self.sems.at[2 * n + 1],
-            device_id=to,
-            device_id_type=MESH,
-        )
+            yield group * 4 + self.ys[dy], (group, self.ys[dy] * 2 + self.core)
+
+    def plane(self):
+        for dz, dx, dy in STEPS:
+            if not dy:
+                group = self.zs[dz] * 4 + self.xs[dx]
+                yield group, (group, self.shard)
+
+    def column(self):
+        for y in (self.ys[2], self.ys[1], self.ys[3]):
+            yield (self.group, y * 2 + self.core)
+
+
+def remote(src, dst, sems, n, device):
+    return pltpu.make_async_remote_copy(
+        src_ref=src,
+        dst_ref=dst,
+        send_sem=sems.at[2 * n],
+        recv_sem=sems.at[2 * n + 1],
+        device_id=device,
+        device_id_type=MESH,
+    )
+
+
+def halves(place, first, rows):
+    return tuple(pl.multiple_of(first + core * rows, 8) for core in (place.core, 1 - place.core))
+
+
+class CriticSum:
+    def __init__(self, place, pack_ref, out, buffers, sems):
+        self.place, self.pack_ref, self.sems = place, pack_ref, sems
+        self.rows = CHIPS * CHUNK
+        self.keep, self.give = halves(place, 0, self.rows)
+        self.other, self.half, self.parts, self.mine, self.whole = buffers
+        self.out = out.at[pl.ds(place.core * CHIPS, CHIPS), pl.ds(0, CHUNK)]
 
     def swap(self):
-        give = pl.multiple_of(self.first + (1 - self.place.core) * self.rows, 8)
-        return self.remote(self.pack_ref.at[pl.ds(give, self.rows)], self.other, 0, self.place.sibling)
+        return remote(self.pack_ref.at[pl.ds(self.give, self.rows)], self.other, self.sems, 0, self.place.sibling)
 
     def scatter(self):
-        keep = pl.multiple_of(self.first + self.place.core * self.rows, 8)
-        total = self.pack_ref[pl.ds(keep, self.rows), :] + self.other[...]
-        for j in range(self.chunk):
+        total = self.pack_ref[pl.ds(self.keep, self.rows), :] + self.other[...]
+        for j in range(CHUNK):
             self.half[:, j, :] = total[CHIPS * j : CHIPS * (j + 1)]
-        chip = self.place.chip
         for peer, device in self.place.others():
-            self.remote(self.half.at[peer], self.parts.at[chip], 1, device).start()
+            remote(self.half.at[peer], self.parts.at[self.place.chip], self.sems, 1, device).start()
 
     def spread(self):
         chip = self.place.chip
@@ -515,43 +562,92 @@
         self.parts[pl.ds(chip, 1)] = self.half[pl.ds(chip, 1)]
         self.mine[...] = jnp.sum(self.parts[...], 0)
         for _, device in self.place.others():
-            self.remote(self.mine, self.whole.at[chip], 2, device).start()
-
-    def back_copies(self):
-        copies = [self.remote(self.whole, self.out, 3, self.place.sibling)]
-        if self.late:
-            copies.append(pltpu.make_async_copy(self.whole, self.out, self.sems.at[8]))
-        return copies
+            remote(self.mine, self.whole.at[chip], self.sems, 2, device).start()
 
     def back(self):
         drain(self.parts, self.sems.at[4], CHIPS - 1)
         drain(self.whole, self.sems.at[5], CHIPS - 1)
         self.whole[pl.ds(self.place.chip, 1)] = self.mine[...][None]
-        for copy in self.back_copies():
+        copies = (
+            remote(self.whole, self.out, self.sems, 3, self.place.sibling),
+            pltpu.make_async_copy(self.whole, self.out, self.sems.at[8]),
+        )
+        for copy in copies:
             copy.start()
-
-    def finish(self):
-        for copy in self.back_copies():
+        for copy in copies:
             copy.wait()
+
+
+class ActorSum:
+    def __init__(self, place, pack_ref, buffers, sems):
+        self.place, self.pack_ref, self.sems = place, pack_ref, sems
+        self.rows = PLANE * CHUNK_A
+        self.keep, self.give = halves(place, AT_ACTOR, self.rows)
+        self.other, self.half, self.parts, self.columns, self.mine, self.both = buffers
+        self.whole = self.both.at[place.core]
+
+    def swap(self):
+        return remote(self.pack_ref.at[pl.ds(self.give, self.rows)], self.other, self.sems, 0, self.place.sibling)
+
+    def scatter(self):
+        total = self.pack_ref[pl.ds(self.keep, self.rows), :] + self.other[...]
+        for j in range(CHUNK_A):
+            self.half[:, j, :] = total[PLANE * j : PLANE * (j + 1)]
+        for peer, device in self.place.plane():
+            remote(self.half.at[peer], self.parts.at[self.place.group], self.sems, 1, device).start()
+
+    def along(self):
+        group, y = self.place.group, self.place.ys[0]
+        drain(self.half, self.sems.at[2], PLANE - 1)
+        drain(self.parts, self.sems.at[3], PLANE - 1)
+        self.parts[pl.ds(group, 1)] = self.half[pl.ds(group, 1)]
+        self.mine[0] = jnp.sum(self.parts[...], 0)
+        self.columns[pl.ds(y, 1)] = self.mine[0:1]
+        for device in self.place.column():
+            remote(self.mine.at[0], self.columns.at[y], self.sems, 2, device).start()
+
+    def spread(self):
+        drain(self.columns, self.sems.at[4], 3)
+        drain(self.columns, self.sems.at[5], 3)
+        self.mine[1] = jnp.sum(self.columns[...], 0)
+        for _, device in self.place.plane():
+            remote(self.mine.at[1], self.whole.at[self.place.group], self.sems, 3, device).start()
+
+    def back_copy(self):
+        return remote(self.whole, self.whole, self.sems, 4, self.place.sibling)
+
+    def back(self):
+        drain(self.parts, self.sems.at[6], PLANE - 1)
+        drain(self.whole, self.sems.at[7], PLANE - 1)
+        self.whole[pl.ds(self.place.group, 1)] = self.mine[1:2]
+        self.back_copy().start()
 
     def in_order(self, flat_ref):
         for core in range(2):
-            for j in range(self.chunk):
-                at = (core * self.chunk + j) * CHIPS
-                flat_ref[at // 16 : (at + CHIPS) // 16] = self.both[core, :, j, :].reshape(CHIPS // 16, 16, 128)
-
-
-def sum_buffers():
-    out = []
-    for chunk in CHUNKS:
-        out += [
-            pltpu.VMEM((CHIPS * chunk, 128), f32),
-            pltpu.VMEM((CHIPS, chunk, 128), f32),
-            pltpu.VMEM((CHIPS, chunk, 128), f32),
-            pltpu.VMEM((chunk, 128), f32),
-            pltpu.VMEM((2, CHIPS, chunk, 128), f32),
-        ]
-    return out
+            for j in range(CHUNK_A):
+                flat_ref[core * CHUNK_A + j] = self.both[core, :, j, :]
+
+
+SUM_BUFFERS = [
+    pltpu.VMEM((CHIPS * CHUNK, 128), f32),
+    pltpu.VMEM((CHIPS, CHUNK, 128), f32),
+    pltpu.VMEM((CHIPS, CHUNK, 128), f32),
+    pltpu.VMEM((CHUNK, 128), f32),
+    pltpu.VMEM((CHIPS, CHUNK, 128), f32),
+    pltpu.VMEM((PLANE * CHUNK_A, 128), f32),
+    pltpu.VMEM((PLANE, CHUNK_A, 128), f32),
+    pltpu.VMEM((PLANE, CHUNK_A, 128), f32),
+    pltpu.VMEM((4, CHUNK_A, 128), f32),
+    pltpu.VMEM((2, CHUNK_A, 128), f32),
+    pltpu.VMEM((2, PLANE, CHUNK_A, 128), f32),
+]
+NOISE_BUFFERS = [
+    pltpu.VMEM((4, 4, 4, 2, 2, 128), f32),
+    pltpu.VMEM((4, 4, 4, 2, 2, 128), f32),
+    pltpu.VMEM((4, 4, 4, 2, 2, 128), f32),
+    pltpu.VMEM((4, 4, 4, 2, 2, 128), f32),
+    pltpu.VMEM((2, 4, 4, 4, 2, 128), f32),
+]
 
 
 def step_kernel(
@@ -579,8 +675,7 @@
     rows_ref,
     picked_ref,
     q_ref,
-    nsend,
-    nrecv,
+    turned_ref,
     noise_sems,
     x_ref,
     nz_ref,
@@ -592,11 +687,9 @@
 ):
     weights, grads = scratch[: len(WEIGHTS)], scratch[len(WEIGHTS) : len(WEIGHTS) + len(GRADS)]
     buffers = scratch[len(WEIGHTS) + len(GRADS) :]
+    noise = Exchange(place := Place(), buffers[len(SUM_BUFFERS) :], noise_sems)
     w1_ref, w2f_ref, w2b_ref, b2_ref, w3_ref, b3_ref, w3t_ref, w3b_ref, b3a_ref, w1a_ref = weights
     blocks = N // width
-    place = Place()
-    me = place.me
-
     loads = [
         pltpu.make_async_copy(src, dst, in_sems.at[n])
         for n, (src, dst) in enumerate(
@@ -617,23 +710,12 @@
 
     barrier = pltpu.get_barrier_semaphore()
 
-    def all_others():
-        for other_core in (False, True):
-            for _, device in place.others(other_core):
-                yield device[0] * 8 + device[1], device
-        yield place.sibling_at, place.sibling
-
-    def greet(devices):
-        for _, device in devices:
-            pl.semaphore_signal(barrier, inc=1, device_id=device, device_id_type=MESH)
-
-    names = list(all_others())
-    greet(names[:80])
+    for device in [place.sibling] + [device for _, device in place.others()]:
+        pl.semaphore_signal(barrier, inc=1, device_id=device, device_id_type=MESH)
     for ref in grads:
         ref[...] = jnp.zeros_like(ref)
     loads[0].wait()
     loads[1].wait()
-    greet(names[80:])
     prepare_critics(
         critic_ref, flat_ref, pad_ref, C0, w1_ref, w2f_ref, w2b_ref, b2_ref, w3_ref, b3_ref, w1a_ref
     )
@@ -651,18 +733,7 @@
     pick_rows(0, width, index_ref, rows_ref, picked_ref)
     loads[4].wait()
     loads[5].wait()
-    turn_noise(noise_ref, q_ref, nsend)
-
-    def send():
-        for peer, device in names:
-            pltpu.make_async_remote_copy(
-                src_ref=nsend.at[peer],
-                dst_ref=nrecv.at[me],
-                send_sem=noise_sems.at[0],
-                recv_sem=noise_sems.at[1],
-                device_id=device,
-                device_id_type=MESH,
-            ).start()
+    turn_noise(noise_ref, q_ref, noise.buffers[0])
 
     def actors(i, carry):
         x = turn_rows(width, picked_ref)
@@ -674,8 +745,8 @@
         def _():
             loads[6].wait()
             loads[7].wait()
-            pl.semaphore_wait(barrier, DEVS - 1)
-            send()
+            pl.semaphore_wait(barrier, CHIPS)
+            noise.start(0)
             prepare_critics(
                 critic_t_ref, flat_ref, pad_ref, T0, w1_ref, w2f_ref, w2b_ref, b2_ref, w3_ref, b3_ref, w1a_ref
             )
@@ -683,17 +754,23 @@
                 AT, actor_t_ref, flat_ref, pad_ref, w1_ref, w2f_ref, w2b_ref, b2_ref, w3t_ref, w3b_ref, b3a_ref
             )
 
+        for stage in range(1, 4):
+
+            @pl.when(i == stage)
+            def _():
+                noise.wait(stage - 1)
+                noise.start(stage)
+
         return carry
 
     lax.fori_loop(0, blocks, actors, 0)
     pack_actor(pack_ref, grads)
-    late, early = (Sum(place, g, pack_ref, out_hbm, buffers[5 * g : 5 * g + 5], sems) for g in range(2))
+    late = CriticSum(place, pack_ref, out_hbm, buffers[:5], sems.at[0])
+    early = ActorSum(place, pack_ref, buffers[5 : len(SUM_BUFFERS)], sems.at[1])
     early.swap().start()
 
-    drain(nsend, noise_sems.at[0], DEVS - 1)
-    drain(nrecv, noise_sems.at[1], DEVS - 1)
-    nrecv[pl.ds(me, 1)] = nsend[pl.ds(me, 1)]
-    noise_back(nrecv, nz_ref)
+    noise.wait(3)
+    noise_back(noise.buffers[4], turned_ref, nz_ref)
 
     def critics(i, carry):
         x = x_ref[:, pl.ds(pl.multiple_of(i * width, width), width)]
@@ -706,9 +783,13 @@
 
         @pl.when(i == 1)
         def _():
+            early.along()
+
+        @pl.when(i == 2)
+        def _():
             early.spread()
 
-        @pl.when(i == 2)
+        @pl.when(i == 3)
         def _():
             early.back()
 
@@ -719,9 +800,9 @@
     late.swap().start()
     prios = pltpu.make_async_copy(prio_ref, out_hbm.at[pl.ds(AT_PRIO, 2)], in_sems.at[0])
     prios.start()
-    early.finish()
     late.swap().wait()
     late.scatter()
+    early.back_copy().wait()
     early.in_order(order_ref)
     order = pltpu.make_async_copy(order_ref, out_hbm.at[pl.ds(AT_SUM, order_ref.shape[0])], in_sems.at[1])
     order.start()
@@ -729,7 +810,6 @@
     late.spread()
     order.wait()
     late.back()
-    late.finish()
 
 
 def update(weight, grad, momentum, average, target):
@@ -749,10 +829,10 @@
     ins, stat_ref, prio_out, outs_hbm, outs = refs[:8], refs[8], refs[9], refs[10:20], refs[20:30]
     late_ref, early_ref, count_ref, grad_ref, in_sems, out_sems = refs[30:]
     early = pltpu.make_async_copy(sum_hbm.at[pl.ds(AT_SUM, early_ref.shape[0])], early_ref, in_sems.at[0])
-    late = pltpu.make_async_copy(sum_hbm.at[pl.ds(0, DEVS), pl.ds(0, CHUNKS[0])], late_ref, in_sems.at[1])
-    stat_core, stat_row = divmod(STAT, CHIPS * CHUNKS[0])
+    late = pltpu.make_async_copy(sum_hbm.at[pl.ds(0, DEVS), pl.ds(0, CHUNK)], late_ref, in_sems.at[1])
+    stat_core, stat_row = divmod(STAT, CHIPS * CHUNK)
     stat_at = stat_core * CHIPS + stat_row % CHIPS
-    count = pltpu.make_async_copy(sum_hbm.at[pl.ds(stat_at, 1), pl.ds(0, CHUNKS[0])], count_ref, in_sems.at[3])
+    count = pltpu.make_async_copy(sum_hbm.at[pl.ds(stat_at, 1), pl.ds(0, CHUNK)], count_ref, in_sems.at[3])
     for load in (count, early, late):
         load.start()
     pass_on = pltpu.make_async_copy(sum_hbm.at[pl.ds(AT_PRIO, 2)], prio_out, in_sems.at[2])
@@ -802,7 +882,7 @@
     late.wait()
     for piece in range(1, LAST + 1):
         for t in range(CUTS[piece - 1] // 128, -(-CUTS[piece] // 128)):
-            core, r = divmod(2 * t, CHIPS * CHUNKS[0])
+            core, r = divmod(2 * t, CHIPS * CHUNK)
             j, k = divmod(r, CHIPS)
             k += core * CHIPS
             grad_ref[:, 128 * t : 128 * (t + 1)] = late_ref[k : k + 2, j, :]
@@ -840,7 +920,7 @@
         out_specs=any_,
         scratch_shapes=[
             pltpu.VMEM((2, 16, DEVS), f32),
-            pltpu.VMEM((2 * CHIPS * CHUNKS[1] // 16, 16, 128), f32),
+            pltpu.VMEM((2 * CHUNK_A, PLANE, 128), f32),
             pltpu.VMEM((ROW, R_DEV), f32),
             pltpu.SMEM((CAP, DEVS), jnp.int32),
             pltpu.VMEM((ACT, CAP, DEVS), f32),
@@ -853,19 +933,19 @@
             pltpu.VMEM((R_DEV, 128), f32),
             pltpu.VMEM((WIDTH // 128, 128, 128), f32),
             pltpu.VMEM((256, 128), f32),
-            pltpu.VMEM((DEVS, 2, 128), f32),
-            pltpu.VMEM((DEVS, 2, 128), f32),
-            pltpu.SemaphoreType.DMA((2,)),
+            pltpu.VMEM((DEVS, 256), f32),
+            pltpu.SemaphoreType.DMA((8,)),
             pltpu.VMEM((FEAT, N), f32),
             pltpu.VMEM((8, N), f32),
             pltpu.VMEM((2 * TILES_C + 6, 128), f32),
             pltpu.VMEM((FEAT, 256), f32),
             pltpu.VMEM((PACK, 128), f32),
-            pltpu.SemaphoreType.DMA((2, 9)),
+            pltpu.SemaphoreType.DMA((2, 10)),
         ]
         + WEIGHTS
         + GRADS
-        + sum_buffers(),
+        + SUM_BUFFERS
+        + NOISE_BUFFERS,
         compiler_params=pltpu.CompilerParams(
             collective_id=0, has_side_effects=True, vmem_limit_bytes=56 << 20
         ),
@@ -889,9 +969,9 @@
         out_specs=(VM,) + (any_,) * 11,
         scratch_shapes=[pltpu.VMEM(p.shape, p.dtype) for p in places]
         + [
-            pltpu.VMEM((DEVS, CHUNKS[0], 128), f32),
-            pltpu.VMEM((2 * CHIPS * CHUNKS[1] // 16, 16, 128), f32),
-            pltpu.VMEM((1, CHUNKS[0], 128), f32),
+            pltpu.VMEM((DEVS, CHUNK, 128), f32),
+            pltpu.VMEM((2 * CHUNK_A, PLANE, 128), f32),
+            pltpu.VMEM((1, CHUNK, 128), f32),
             pltpu.VMEM((2, TILES_C * 128), f32),
             pltpu.SemaphoreType.DMA((4,)),
             pltpu.SemaphoreType.DMA((LAST + 1, 5)),

time: 80.2 us -> 78.7 us (0.981)
  Pallas kernels: 79.1 us -> 77.6 us
    pallas_call x1, Pallas kernels: 75 us -> 73.5 us  [local(): pl.pallas_call(functools.partial(step_kernel, WIDTH), out_shape=SDS(RESUL...]
where the time goes in v9:
time: 78.7 us; the launch traced here: 78.6 us
  Pallas kernels  77.6 us (99%)
  between operations  0.94 us (1%)
    pallas_call x1, Pallas kernels, local(): pl.pallas_call(functools.partial(step_kernel, WIDTH), out_shape=SDS(RESUL...  73.5 us
    pallas_call x1, Pallas kernels, local(): pl.pallas_call(update_kernel, out_shape=tuple(shapes + places), in_specs=...  4.14 us

profile of v9, /device:TPU:1, one launch (start us, length us, event | category | flops | bytes accessed | tf_op | source)
XLA Modules:
  0.0 78.6 jit_solution(11366414905723231273)
XLA Ops:
  0.6 0.0 copy-start.1
  0.7 0.0 copy-start.3
  0.7 0.0 copy-start
  0.7 0.0 copy-start.2
  0.7 0.0 copy-start.5
  0.7 0.0 copy-start.7
  0.7 0.0 copy-start.4
  0.7 0.0 copy-start.6
  0.7 73.5 %td3_step.1.sum_hbm = f32[3700,16,128]{2,1,0:T(8,128)} custom-call(f32[42,8192]{1,0:T(8,128)} %bitcast.12, s32[32,128]{1,0:T(8,128)} %bitcast.14, f32[6,32,128]{2,1,0:T(8,128)} %bitcast.13, s32[1,128]{1,0:T(1,128)} %count_hbm.1, f32[71942]{0:T(1024)} %refs_0_.1, f32[71942]{0:T(1024)} %refs_6_.1, f32[2,72193]{1,0:T(2,128)} %refs_1_.1, f32[2,72193]{1,0:T(2,128)} %refs_7_.1), custom_call_target="tpu_custom_call" | custom-call | tf_op jit(solution)/shard_map/td3_step/pallas_call | solution.py:916
  74.2 0.0 copy-done.1
  74.2 0.0 copy-done.3
  74.2 0.0 copy-done
  74.3 0.0 copy-done.2
  74.3 0.0 copy-done.5
  74.3 0.0 copy-done.7
  74.3 0.0 copy-done.4
  74.3 0.0 copy-done.6
  74.3 4.1 %update.1 = (f32[2]{0:T(128)}, f32[2,16,128]{2,1,0:T(8,128)}, f32[71942]{0:T(1024)}, f32[2,72193]{1,0:T(2,128)}, f32[71942]{0:T(1024)}, /*index=5*/f32[2,72193]{...) custom-call(f32[3700,16,128]{2,1,0:T(8,128)} %td3_step.1.sum_hbm, ...), custom_call_target="tpu_custom_call" | custom-call | tf_op jit(solution)/shard_map/update/pallas_call | solution.py:965
Async XLA Ops:
  0.6 73.6 %copy-start.1 = (f32[2,72193]{1,0:T(2,128)S(1)}, f32[2,72193]{1,0:T(2,128)}, u32[]{:S(2)}) copy-start(f32[2,72193]{1,0:T(2,128)} %refs_7_.1) | copy-start | bytes 1732636
  0.7 73.6 %copy-start.3 = (f32[71942]{0:T(1024)S(1)}, f32[71942]{0:T(1024)}, u32[]{:S(2)}) copy-start(f32[71942]{0:T(1024)} %refs_6_.1) | copy-start | bytes 863308
  0.7 73.6 %copy-start = (f32[2,72193]{1,0:T(2,128)S(1)}, f32[2,72193]{1,0:T(2,128)}, u32[]{:S(2)}) copy-start(f32[2,72193]{1,0:T(2,128)} %refs_1_.1) | copy-start | bytes 1732636
  0.7 73.6 %copy-start.2 = (f32[71942]{0:T(1024)S(1)}, f32[71942]{0:T(1024)}, u32[]{:S(2)}) copy-start(f32[71942]{0:T(1024)} %refs_0_.1) | copy-start | bytes 863308
  0.7 73.6 %copy-start.5 = (f32[2,72193]{1,0:T(2,128)S(1)}, f32[2,72193]{1,0:T(2,128)}, u32[]{:S(2)}) copy-start(f32[2,72193]{1,0:T(2,128)} %refs_5_.1) | copy-start | bytes 1732636
  0.7 73.6 %copy-start.7 = (f32[71942]{0:T(1024)S(1)}, f32[71942]{0:T(1024)}, u32[]{:S(2)}) copy-start(f32[71942]{0:T(1024)} %refs_4_.1) | copy-start | bytes 863308
  0.7 73.6 %copy-start.4 = (f32[2,72193]{1,0:T(2,128)S(1)}, f32[2,72193]{1,0:T(2,128)}, u32[]{:S(2)}) copy-start(f32[2,72193]{1,0:T(2,128)} %refs_3_.1) | copy-start | bytes 1732636
  0.7 73.6 %copy-start.6 = (f32[71942]{0:T(1024)S(1)}, f32[71942]{0:T(1024)}, u32[]{:S(2)}) copy-start(f32[71942]{0:T(1024)} %refs_2_.1) | copy-start | bytes 863308

commit v10 on v9

--- a/solution.py
+++ b/solution.py
@@ -31,6 +31,8 @@
 NEXT = 25
 
 TILES_C = 565
+W2_ROW, W2_END = 96, 1120
+REST = 1024
 STAT = 1130
 ROWS_A = 563
 CHIPS = DEVS // 2
@@ -58,10 +60,6 @@
     return lax.dot_general(a, b, (((1,), (1,)), ((), ())), preferred_element_type=f32)
 
 
-def dot_exact(a, b, dims):
-    return lax.dot_general(a, b, (dims, ((), ())), precision=lax.Precision.HIGHEST, preferred_element_type=f32)
-
-
 def split(v):
     hi = v.astype(bf)
     return hi, (v - hi.astype(f32)).astype(bf)
@@ -146,8 +144,8 @@
 
 def turn_table(i, table_ref, rows_ref):
     s = pl.ds(pl.multiple_of(i * TURN, TURN), TURN)
-    v = jnp.concatenate([table_ref[:, s], jnp.zeros((128 - ROW, TURN), f32)], 0)
-    rows_ref[s, :] = jnp.transpose(v)
+    v = jnp.concatenate([table_ref[:, s], jnp.zeros((FEAT - ROW, TURN), f32)], 0)
+    rows_ref[s, :FEAT] = jnp.transpose(v)
 
 
 def pick_rows(block, width, index_ref, rows_ref, picked_ref):
@@ -158,7 +156,7 @@
 
 
 def turn_rows(width, picked_ref):
-    parts = [jnp.transpose(picked_ref[t])[:FEAT] for t in range(width // 128)]
+    parts = [jnp.transpose(picked_ref[t, :, :FEAT]) for t in range(width // 128)]
     x = jnp.concatenate(parts, 1)
     ones = lax.broadcasted_iota(jnp.int32, (8, width), 0) == (ONE - 40)
     return jnp.concatenate([x[:40], jnp.where(ones, 1.0, x[40:])], 0)
@@ -244,7 +242,9 @@
     for j in range(ACT):
         row, lane = head_maps(j)
         picked = jnp.transpose(row) * turned[j + 1 : j + 2, :]
-        out = out + dot_exact(picked, lane.astype(f32), ((1,), (0,)))
+        hi, lo = split(picked)
+        lane = lane.astype(f32).astype(bf)
+        out = out + dot(hi, lane) + dot(lo, lane)
     return out
 
 
@@ -427,7 +427,9 @@
 
 
 def lane_sums(tile):
-    return dot_exact(jnp.ones((8, 128), f32), tile, ((1,), (1,)))
+    hi, lo = split(tile)
+    ones = jnp.ones((16, 128), bf)
+    return (dot_nt(ones, hi) + dot_nt(ones, lo))[:8]
 
 
 def pack_critics(pack_ref, grads):
@@ -441,9 +443,9 @@
         for half in range(2):
             s = slice(128 * half, 128 * (half + 1))
             at = c + 2 * half
-            pack_ref[pl.ds(at, OBS + ACT, stride=4), :] = g1[: OBS + ACT, s]
-            pack_ref[at + 92 : at + 93, :] = g1[ONE : ONE + 1, s]
-            pack_ref[pl.ds(at + 96, UNITS, stride=4), :] = g2_ref[c, :UNITS, s]
+            pack_ref[pl.ds(REST + at, OBS + ACT, stride=4), :] = g1[: OBS + ACT, s]
+            pack_ref[REST + at + 92 : REST + at + 93, :] = g1[ONE : ONE + 1, s]
+            pack_ref[pl.ds(at, UNITS, stride=4), :] = g2_ref[c, :UNITS, s]
             pack_ref[at + 1120 : at + 1121, :] = b2[:, s]
             pack_ref[at + 1124 : at + 1125, :] = w3[:, s]
         pack_ref[c + 1128 : c + 1129, :] = jnp.where(lane == 0, sums[2 + c : 3 + c], 0.0)
@@ -540,18 +542,25 @@
 class CriticSum:
     def __init__(self, place, pack_ref, out, buffers, sems):
         self.place, self.pack_ref, self.sems = place, pack_ref, sems
-        self.rows = CHIPS * CHUNK
-        self.keep, self.give = halves(place, 0, self.rows)
+        self.wide = CHIPS * (CHUNK - 1)
+        self.pieces = (halves(place, 0, self.wide), halves(place, REST, CHIPS))
         self.other, self.half, self.parts, self.mine, self.whole = buffers
         self.out = out.at[pl.ds(place.core * CHIPS, CHIPS), pl.ds(0, CHUNK)]
 
     def swap(self):
-        return remote(self.pack_ref.at[pl.ds(self.give, self.rows)], self.other, self.sems, 0, self.place.sibling)
+        at = 0
+        for (_, give), rows in zip(self.pieces, (self.wide, CHIPS)):
+            src, dst = self.pack_ref.at[pl.ds(give, rows)], self.other.at[pl.ds(at, rows)]
+            remote(src, dst, self.sems, 0, self.place.sibling).start()
+            at += rows
 
     def scatter(self):
-        total = self.pack_ref[pl.ds(self.keep, self.rows), :] + self.other[...]
-        for j in range(CHUNK):
-            self.half[:, j, :] = total[CHIPS * j : CHIPS * (j + 1)]
+        drain(self.other, self.sems.at[0], CHIPS * CHUNK)
+        drain(self.other, self.sems.at[1], CHIPS * CHUNK)
+        (wide, _), (more, _) = self.pieces
+        total = self.pack_ref[pl.ds(wide, self.wide), :] + self.other[: self.wide, :]
+        self.half[:, : CHUNK - 1, :] = total.reshape(CHIPS, CHUNK - 1, 128)
+        self.half[:, CHUNK - 1, :] = self.pack_ref[pl.ds(more, CHIPS), :] + self.other[self.wide :, :]
         for peer, device in self.place.others():
             remote(self.half.at[peer], self.parts.at[self.place.chip], self.sems, 1, device).start()
 
@@ -797,10 +806,9 @@
 
     lax.fori_loop(0, blocks, critics, 0)
     pack_critics(pack_ref, grads)
-    late.swap().start()
+    late.swap()
     prios = pltpu.make_async_copy(prio_ref, out_hbm.at[pl.ds(AT_PRIO, 2)], in_sems.at[0])
     prios.start()
-    late.swap().wait()
     late.scatter()
     early.back_copy().wait()
     early.in_order(order_ref)
@@ -830,8 +838,7 @@
     late_ref, early_ref, count_ref, grad_ref, in_sems, out_sems = refs[30:]
     early = pltpu.make_async_copy(sum_hbm.at[pl.ds(AT_SUM, early_ref.shape[0])], early_ref, in_sems.at[0])
     late = pltpu.make_async_copy(sum_hbm.at[pl.ds(0, DEVS), pl.ds(0, CHUNK)], late_ref, in_sems.at[1])
-    stat_core, stat_row = divmod(STAT, CHIPS * CHUNK)
-    stat_at = stat_core * CHIPS + stat_row % CHIPS
+    stat_at = STAT - REST
     count = pltpu.make_async_copy(sum_hbm.at[pl.ds(stat_at, 1), pl.ds(0, CHUNK)], count_ref, in_sems.at[3])
     for load in (count, early, late):
         load.start()
@@ -849,7 +856,7 @@
         return out
 
     count.wait()
-    stat = count_ref[0, stat_row // CHIPS : stat_row // CHIPS + 1, :]
+    stat = count_ref[0, CHUNK - 1 : CHUNK, :]
     factor = (1.0 / SCALE) / stat[:, 1:2]
     stat_ref[...] = stat[:, :2].reshape(2)
     early.wait()
@@ -882,10 +889,14 @@
     late.wait()
     for piece in range(1, LAST + 1):
         for t in range(CUTS[piece - 1] // 128, -(-CUTS[piece] // 128)):
-            core, r = divmod(2 * t, CHIPS * CHUNK)
-            j, k = divmod(r, CHIPS)
-            k += core * CHIPS
-            grad_ref[:, 128 * t : 128 * (t + 1)] = late_ref[k : k + 2, j, :]
+            r = 2 * t
+            if W2_ROW <= r < W2_END:
+                k, j = divmod(r - W2_ROW, CHUNK - 1)
+                pair = late_ref[k, j : j + 2, :]
+            else:
+                k = r % REST
+                pair = late_ref[k : k + 2, CHUNK - 1, :]
+            grad_ref[:, 128 * t : 128 * (t + 1)] = pair
         lax.fori_loop(CUTS[piece - 1] // STEP, CUTS[piece] // STEP, critics, 0, unroll=4)
         if piece == LAST:
             done = PC // STEP * STEP

time: 78.7 us -> 78.5 us (level)
  no operation moved by 1% of the time
where the time goes in v10:
time: 78.5 us; the launch traced here: 78.3 us
  Pallas kernels  77.3 us (98%)
  between operations  0.94 us (1%)
    pallas_call x1, Pallas kernels, local(): pl.pallas_call(functools.partial(step_kernel, WIDTH), out_shape=SDS(RESUL...  73.2 us
    pallas_call x1, Pallas kernels, local(): pl.pallas_call(update_kernel, out_shape=tuple(shapes + places), in_specs=...  4.11 us

profile of v10, /device:TPU:1, one launch (start us, length us, event | category | flops | bytes accessed | tf_op | source)
XLA Modules:
  0.0 78.3 jit_solution(17639276981424993720)
XLA Ops:
  0.6 0.0 copy-start.1
  0.7 0.0 copy-start.3
  0.7 0.0 copy-start
  0.7 0.0 copy-start.2
  0.7 0.0 copy-start.5
  0.7 0.0 copy-start.7
  0.7 0.0 copy-start.4
  0.7 0.0 copy-start.6
  0.7 73.2 %td3_step.1.sum_hbm = f32[3700,16,128]{2,1,0:T(8,128)} custom-call(f32[42,8192]{1,0:T(8,128)} %bitcast.12, s32[32,128]{1,0:T(8,128)} %bitcast.14, f32[6,32,128]{2,1,0:T(8,128)} %bitcast.13, s32[1,128]{1,0:T(1,128)} %count_hbm.1, f32[71942]{0:T(1024)} %refs_0_.1, f32[71942]{0:T(1024)} %refs_6_.1, f32[2,72193]{1,0:T(2,128)} %refs_1_.1, f32[2,72193]{1,0:T(2,128)} %refs_7_.1), custom_call_target="tpu_custom_call" | custom-call | tf_op jit(solution)/shard_map/td3_step/pallas_call | solution.py:927
  74.0 0.0 copy-done.1
  74.0 0.0 copy-done.3
  74.0 0.0 copy-done
  74.0 0.0 copy-done.2
  74.0 0.0 copy-done.5
  74.0 0.0 copy-done.7
  74.0 0.0 copy-done.4
  74.0 0.0 copy-done.6
  74.1 4.1 %update.1 = (f32[2]{0:T(128)}, f32[2,16,128]{2,1,0:T(8,128)}, f32[71942]{0:T(1024)}, f32[2,72193]{1,0:T(2,128)}, f32[71942]{0:T(1024)}, /*index=5*/f32[2,72193]{...) custom-call(f32[3700,16,128]{2,1,0:T(8,128)} %td3_step.1.sum_hbm, ...), custom_call_target="tpu_custom_call" | custom-call | tf_op jit(solution)/shard_map/update/pallas_call | solution.py:976
Async XLA Ops:
  0.6 73.3 %copy-start.1 = (f32[2,72193]{1,0:T(2,128)S(1)}, f32[2,72193]{1,0:T(2,128)}, u32[]{:S(2)}) copy-start(f32[2,72193]{1,0:T(2,128)} %refs_7_.1) | copy-start | bytes 1732636
  0.7 73.3 %copy-start.3 = (f32[71942]{0:T(1024)S(1)}, f32[71942]{0:T(1024)}, u32[]{:S(2)}) copy-start(f32[71942]{0:T(1024)} %refs_6_.1) | copy-start | bytes 863308
  0.7 73.3 %copy-start = (f32[2,72193]{1,0:T(2,128)S(1)}, f32[2,72193]{1,0:T(2,128)}, u32[]{:S(2)}) copy-start(f32[2,72193]{1,0:T(2,128)} %refs_1_.1) | copy-start | bytes 1732636
  0.7 73.3 %copy-start.2 = (f32[71942]{0:T(1024)S(1)}, f32[71942]{0:T(1024)}, u32[]{:S(2)}) copy-start(f32[71942]{0:T(1024)} %refs_0_.1) | copy-start | bytes 863308
  0.7 73.3 %copy-start.5 = (f32[2,72193]{1,0:T(2,128)S(1)}, f32[2,72193]{1,0:T(2,128)}, u32[]{:S(2)}) copy-start(f32[2,72193]{1,0:T(2,128)} %refs_5_.1) | copy-start | bytes 1732636
  0.7 73.3 %copy-start.7 = (f32[71942]{0:T(1024)S(1)}, f32[71942]{0:T(1024)}, u32[]{:S(2)}) copy-start(f32[71942]{0:T(1024)} %refs_4_.1) | copy-start | bytes 863308
  0.7 73.3 %copy-start.4 = (f32[2,72193]{1,0:T(2,128)S(1)}, f32[2,72193]{1,0:T(2,128)}, u32[]{:S(2)}) copy-start(f32[2,72193]{1,0:T(2,128)} %refs_3_.1) | copy-start | bytes 1732636
  0.7 73.3 %copy-start.6 = (f32[71942]{0:T(1024)S(1)}, f32[71942]{0:T(1024)}, u32[]{:S(2)}) copy-start(f32[71942]{0:T(1024)} %refs_2_.1) | copy-start | bytes 863308

commit v11 on v10

--- a/solution.py
+++ b/solution.py
@@ -211,44 +211,43 @@
         b3_ref[net] = jnp.broadcast_to(critic_ref[c : c + 1, PC - 1 : PC], (1, 128))
 
 
-def head_maps(j):
-    k = lax.broadcasted_iota(jnp.int32, (UNITS, 16), 0)
-    r = lax.broadcasted_iota(jnp.int32, (UNITS, 16), 1)
-    row = ((k * ACT + j) >> 7) == r
-    k = lax.broadcasted_iota(jnp.int32, (UNITS, 128), 0)
-    l = lax.broadcasted_iota(jnp.int32, (UNITS, 128), 1)
-    lane = ((k * ACT + j) & 127) == l
-    return row.astype(f32), lane
-
-
-def head_of(flat):
+def make_maps(row_ref, turned_ref, lane_ref):
+    def entry(shape, axis, j):
+        return lax.broadcasted_iota(jnp.int32, shape, axis) * ACT + j
+
+    for j in range(ACT):
+        r = lax.broadcasted_iota(jnp.int32, (UNITS, 16), 1)
+        row_ref[j] = ((entry((UNITS, 16), 0, j) >> 7) == r).astype(f32).astype(bf)
+        r = lax.broadcasted_iota(jnp.int32, (16, UNITS), 0)
+        turned_ref[j] = ((entry((16, UNITS), 1, j) >> 7) == r).astype(f32)
+        l = lax.broadcasted_iota(jnp.int32, (UNITS, 128), 1)
+        lane_ref[j] = ((entry((UNITS, 128), 0, j) & 127) == l).astype(f32).astype(bf)
+
+
+def head_of(flat, maps):
+    row_ref, _, lane_ref = maps
     hi = flat.astype(bf).astype(f32)
+    r = lax.broadcasted_iota(jnp.int32, (16, 128 * ACT), 0)
+    l = lax.broadcasted_iota(jnp.int32, (16, 128 * ACT), 1)
+    take = ((l >> 7) == (r - 1)).astype(f32).astype(bf)
     out = []
     for part in (hi, flat - hi):
         part = part.astype(bf)
-        spread = []
-        for j in range(ACT):
-            row, lane = head_maps(j)
-            spread.append(jnp.where(lane, dot(row.astype(bf), part), 0.0).astype(bf))
-        r = lax.broadcasted_iota(jnp.int32, (16, 128 * ACT), 0)
-        l = lax.broadcasted_iota(jnp.int32, (16, 128 * ACT), 1)
-        take = ((l >> 7) == (r - 1)).astype(f32).astype(bf)
+        spread = [dot(row_ref[j], part).astype(bf) * lane_ref[j] for j in range(ACT)]
         out.append(dot_nt(take, jnp.concatenate(spread, 1))[:8])
     return out
 
 
-def head_back(turned):
+def head_back(turned, maps):
+    _, turned_ref, lane_ref = maps
     out = jnp.zeros((16, 128), f32)
     for j in range(ACT):
-        row, lane = head_maps(j)
-        picked = jnp.transpose(row) * turned[j + 1 : j + 2, :]
-        hi, lo = split(picked)
-        lane = lane.astype(f32).astype(bf)
-        out = out + dot(hi, lane) + dot(lo, lane)
+        hi, lo = split(turned_ref[j] * turned[j + 1 : j + 2, :])
+        out = out + dot(hi, lane_ref[j]) + dot(lo, lane_ref[j])
     return out
 
 
-def prepare_actor(net, actor_ref, rows_ref, pad_ref, w1_ref, w2f_ref, w2b_ref, b2_ref, w3t_ref, w3b_ref, b3a_ref):
+def prepare_actor(net, maps, actor_ref, rows_ref, pad_ref, w1_ref, w2f_ref, w2b_ref, b2_ref, w3t_ref, w3b_ref, b3a_ref):
     whole = PA // 1024
     for t in range(whole):
         rows_ref[8 * t : 8 * t + 8, :] = actor_ref[pl.ds(1024 * t, 1024)].reshape(8, 128)
@@ -266,7 +265,7 @@
     put_square(net, w2, w2f_ref, w2b_ref)
     put_column(b2_ref, net, rows_ref[548:549, :], rows_ref[549:550, :], 0.5)
     flat = jnp.concatenate([rows_ref[550:562, :], jnp.zeros((4, 128), f32)], 0)
-    hi, lo = head_of(flat)
+    hi, lo = head_of(flat, maps)
     block = jnp.concatenate([hi, hi, lo], 1)
     w3t_ref[net - A] = jnp.concatenate([block, jnp.zeros_like(block)], 0).astype(bf)
     if net == A:
@@ -432,7 +431,14 @@
     return (dot_nt(ones, hi) + dot_nt(ones, lo))[:8]
 
 
-def pack_critics(pack_ref, grads):
+def pack_w2(pack_ref, grads):
+    for c in range(2):
+        for half in range(2):
+            s = slice(128 * half, 128 * (half + 1))
+            pack_ref[pl.ds(c + 2 * half, UNITS, stride=4), :] = grads[0][c, :UNITS, s]
+
+
+def pack_rest(pack_ref, grads):
     g2_ref, g1_ref, g3a_ref, db2_ref, dw3_ref, st_ref = grads
     lane = lax.broadcasted_iota(jnp.int32, (1, 128), 1)
     sums = jnp.sum(st_ref[...], 1, keepdims=True)
@@ -445,7 +451,6 @@
             at = c + 2 * half
             pack_ref[pl.ds(REST + at, OBS + ACT, stride=4), :] = g1[: OBS + ACT, s]
             pack_ref[REST + at + 92 : REST + at + 93, :] = g1[ONE : ONE + 1, s]
-            pack_ref[pl.ds(at, UNITS, stride=4), :] = g2_ref[c, :UNITS, s]
             pack_ref[at + 1120 : at + 1121, :] = b2[:, s]
             pack_ref[at + 1124 : at + 1125, :] = w3[:, s]
         pack_ref[c + 1128 : c + 1129, :] = jnp.where(lane == 0, sums[2 + c : 3 + c], 0.0)
@@ -453,7 +458,7 @@
     pack_ref[STAT + 1 : AT_ACTOR, :] = jnp.zeros((AT_ACTOR - STAT - 1, 128), f32)
 
 
-def pack_actor(pack_ref, grads):
+def pack_actor(pack_ref, maps, grads):
     g2_ref, g1_ref, g3a_ref, db2_ref, dw3_ref, st_ref = grads
     sums = jnp.sum(st_ref[...], 1, keepdims=True)
     g1 = g1_ref[A, :FEAT, :] + g1_ref[A, FEAT:, :]
@@ -465,7 +470,7 @@
         pack_ref[o + 34 + half : o + 35 + half, :] = g1[ONE : ONE + 1, s]
         pack_ref[pl.ds(o + 36 + half, UNITS, stride=2), :] = g2_ref[A, :UNITS, s]
         pack_ref[o + 548 + half : o + 549 + half, :] = b2[:, s]
-    pack_ref[o + 550 : o + 562, :] = head_back(g3a_ref[:8, :] + g3a_ref[8:, :])[:12]
+    pack_ref[o + 550 : o + 562, :] = head_back(g3a_ref[:8, :] + g3a_ref[8:, :], maps)[:12]
     e = lax.broadcasted_iota(jnp.int32, (8, 128), 1) == lax.broadcasted_iota(jnp.int32, (8, 128), 0) - 1
     pack_ref[o + 562 : o + 563, :] = jnp.sum(jnp.where(e, sums[8:16], 0.0), 0, keepdims=True)
     pack_ref[o + ROWS_A : PACK, :] = jnp.zeros((PACK - o - ROWS_A, 128), f32)
@@ -547,12 +552,10 @@
         self.other, self.half, self.parts, self.mine, self.whole = buffers
         self.out = out.at[pl.ds(place.core * CHIPS, CHIPS), pl.ds(0, CHUNK)]
 
-    def swap(self):
-        at = 0
-        for (_, give), rows in zip(self.pieces, (self.wide, CHIPS)):
-            src, dst = self.pack_ref.at[pl.ds(give, rows)], self.other.at[pl.ds(at, rows)]
-            remote(src, dst, self.sems, 0, self.place.sibling).start()
-            at += rows
+    def swap(self, piece):
+        at, rows = ((0, self.wide), (self.wide, CHIPS))[piece]
+        src = self.pack_ref.at[pl.ds(self.pieces[piece][1], rows)]
+        remote(src, self.other.at[pl.ds(at, rows)], self.sems, 0, self.place.sibling).start()
 
     def scatter(self):
         drain(self.other, self.sems.at[0], CHIPS * CHUNK)
@@ -637,6 +640,11 @@
                 flat_ref[core * CHUNK_A + j] = self.both[core, :, j, :]
 
 
+MAPS = [
+    pltpu.VMEM((ACT, UNITS, 16), bf),
+    pltpu.VMEM((ACT, 16, UNITS), f32),
+    pltpu.VMEM((ACT, UNITS, 128), bf),
+]
 SUM_BUFFERS = [
     pltpu.VMEM((CHIPS * CHUNK, 128), f32),
     pltpu.VMEM((CHIPS, CHUNK, 128), f32),
@@ -695,7 +703,8 @@
     *scratch,
 ):
     weights, grads = scratch[: len(WEIGHTS)], scratch[len(WEIGHTS) : len(WEIGHTS) + len(GRADS)]
-    buffers = scratch[len(WEIGHTS) + len(GRADS) :]
+    buffers = scratch[len(WEIGHTS) + len(GRADS) : -len(MAPS)]
+    maps = scratch[-len(MAPS) :]
     noise = Exchange(place := Place(), buffers[len(SUM_BUFFERS) :], noise_sems)
     w1_ref, w2f_ref, w2b_ref, b2_ref, w3_ref, b3_ref, w3t_ref, w3b_ref, b3a_ref, w1a_ref = weights
     blocks = N // width
@@ -723,13 +732,14 @@
         pl.semaphore_signal(barrier, inc=1, device_id=device, device_id_type=MESH)
     for ref in grads:
         ref[...] = jnp.zeros_like(ref)
+    make_maps(*maps)
     loads[0].wait()
     loads[1].wait()
     prepare_critics(
         critic_ref, flat_ref, pad_ref, C0, w1_ref, w2f_ref, w2b_ref, b2_ref, w3_ref, b3_ref, w1a_ref
     )
     prepare_actor(
-        A, actor_ref, flat_ref, pad_ref, w1_ref, w2f_ref, w2b_ref, b2_ref, w3t_ref, w3b_ref, b3a_ref
+        A, maps, actor_ref, flat_ref, pad_ref, w1_ref, w2f_ref, w2b_ref, b2_ref, w3t_ref, w3b_ref, b3a_ref
     )
     loads[2].wait()
 
@@ -760,7 +770,7 @@
                 critic_t_ref, flat_ref, pad_ref, T0, w1_ref, w2f_ref, w2b_ref, b2_ref, w3_ref, b3_ref, w1a_ref
             )
             prepare_actor(
-                AT, actor_t_ref, flat_ref, pad_ref, w1_ref, w2f_ref, w2b_ref, b2_ref, w3t_ref, w3b_ref, b3a_ref
+                AT, maps, actor_t_ref, flat_ref, pad_ref, w1_ref, w2f_ref, w2b_ref, b2_ref, w3t_ref, w3b_ref, b3a_ref
             )
 
         for stage in range(1, 4):
@@ -773,7 +783,7 @@
         return carry
 
     lax.fori_loop(0, blocks, actors, 0)
-    pack_actor(pack_ref, grads)
+    pack_actor(pack_ref, maps, grads)
     late = CriticSum(place, pack_ref, out_hbm, buffers[:5], sems.at[0])
     early = ActorSum(place, pack_ref, buffers[5 : len(SUM_BUFFERS)], sems.at[1])
     early.swap().start()
@@ -805,8 +815,10 @@
         return carry
 
     lax.fori_loop(0, blocks, critics, 0)
-    pack_critics(pack_ref, grads)
-    late.swap()
+    pack_w2(pack_ref, grads)
+    late.swap(0)
+    pack_rest(pack_ref, grads)
+    late.swap(1)
     prios = pltpu.make_async_copy(prio_ref, out_hbm.at[pl.ds(AT_PRIO, 2)], in_sems.at[0])
     prios.start()
     late.scatter()
@@ -956,7 +968,8 @@
         + WEIGHTS
         + GRADS
         + SUM_BUFFERS
-        + NOISE_BUFFERS,
+        + NOISE_BUFFERS
+        + MAPS,
         compiler_params=pltpu.CompilerParams(
             collective_id=0, has_side_effects=True, vmem_limit_bytes=56 << 20
         ),

time: 78.5 us -> 78.3 us (level)
  no operation moved by 1% of the time
where the time goes in v11:
time: 78.3 us; the launch traced here: 78.1 us
  Pallas kernels  77.2 us (99%)
  between operations  0.94 us (1%)
    pallas_call x1, Pallas kernels, local(): pl.pallas_call(functools.partial(step_kernel, WIDTH), out_shape=SDS(RESUL...  73.1 us
    pallas_call x1, Pallas kernels, local(): pl.pallas_call(update_kernel, out_shape=tuple(shapes + places), in_specs=...  4.11 us

profile of v11, /device:TPU:1, one launch (start us, length us, event | category | flops | bytes accessed | tf_op | source)
XLA Modules:
  0.0 78.1 jit_solution(319497388413503774)
XLA Ops:
  0.6 0.0 copy-start.1
  0.7 0.0 copy-start.3
  0.7 0.0 copy-start
  0.7 0.0 copy-start.2
  0.7 0.0 copy-start.5
  0.7 0.0 copy-start.7
  0.7 0.0 copy-start.4
  0.7 0.0 copy-start.6
  0.7 73.1 %td3_step.1.sum_hbm = f32[3700,16,128]{2,1,0:T(8,128)} custom-call(f32[42,8192]{1,0:T(8,128)} %bitcast.12, s32[32,128]{1,0:T(8,128)} %bitcast.14, f32[6,32,128]{2,1,0:T(8,128)} %bitcast.13, s32[1,128]{1,0:T(1,128)} %count_hbm.1, f32[71942]{0:T(1024)} %refs_0_.1, f32[71942]{0:T(1024)} %refs_6_.1, f32[2,72193]{1,0:T(2,128)} %refs_1_.1, f32[2,72193]{1,0:T(2,128)} %refs_7_.1), custom_call_target="tpu_custom_call" | custom-call | tf_op jit(solution)/shard_map/td3_step/pallas_call | solution.py:939
  73.8 0.0 copy-done.1
  73.8 0.0 copy-done.3
  73.8 0.0 copy-done
  73.8 0.0 copy-done.2
  73.8 0.0 copy-done.5
  73.8 0.0 copy-done.7
  73.9 0.0 copy-done.4
  73.9 0.0 copy-done.6
  73.9 4.1 %update.1 = (f32[2]{0:T(128)}, f32[2,16,128]{2,1,0:T(8,128)}, f32[71942]{0:T(1024)}, f32[2,72193]{1,0:T(2,128)}, f32[71942]{0:T(1024)}, /*index=5*/f32[2,72193]{...) custom-call(f32[3700,16,128]{2,1,0:T(8,128)} %td3_step.1.sum_hbm, ...), custom_call_target="tpu_custom_call" | custom-call | tf_op jit(solution)/shard_map/update/pallas_call | solution.py:989
Async XLA Ops:
  0.6 73.1 %copy-start.1 = (f32[2,72193]{1,0:T(2,128)S(1)}, f32[2,72193]{1,0:T(2,128)}, u32[]{:S(2)}) copy-start(f32[2,72193]{1,0:T(2,128)} %refs_7_.1) | copy-start | bytes 1732636
  0.7 73.1 %copy-start.3 = (f32[71942]{0:T(1024)S(1)}, f32[71942]{0:T(1024)}, u32[]{:S(2)}) copy-start(f32[71942]{0:T(1024)} %refs_6_.1) | copy-start | bytes 863308
  0.7 73.1 %copy-start = (f32[2,72193]{1,0:T(2,128)S(1)}, f32[2,72193]{1,0:T(2,128)}, u32[]{:S(2)}) copy-start(f32[2,72193]{1,0:T(2,128)} %refs_1_.1) | copy-start | bytes 1732636
  0.7 73.1 %copy-start.2 = (f32[71942]{0:T(1024)S(1)}, f32[71942]{0:T(1024)}, u32[]{:S(2)}) copy-start(f32[71942]{0:T(1024)} %refs_0_.1) | copy-start | bytes 863308
  0.7 73.1 %copy-start.5 = (f32[2,72193]{1,0:T(2,128)S(1)}, f32[2,72193]{1,0:T(2,128)}, u32[]{:S(2)}) copy-start(f32[2,72193]{1,0:T(2,128)} %refs_5_.1) | copy-start | bytes 1732636
  0.7 73.1 %copy-start.7 = (f32[71942]{0:T(1024)S(1)}, f32[71942]{0:T(1024)}, u32[]{:S(2)}) copy-start(f32[71942]{0:T(1024)} %refs_4_.1) | copy-start | bytes 863308
  0.7 73.1 %copy-start.4 = (f32[2,72193]{1,0:T(2,128)S(1)}, f32[2,72193]{1,0:T(2,128)}, u32[]{:S(2)}) copy-start(f32[2,72193]{1,0:T(2,128)} %refs_3_.1) | copy-start | bytes 1732636
  0.7 73.1 %copy-start.6 = (f32[71942]{0:T(1024)S(1)}, f32[71942]{0:T(1024)}, u32[]{:S(2)}) copy-start(f32[71942]{0:T(1024)} %refs_2_.1) | copy-start | bytes 863308

commit v12 on v11

--- a/solution.py
+++ b/solution.py
@@ -754,11 +754,14 @@
     loads[5].wait()
     turn_noise(noise_ref, q_ref, noise.buffers[0])
 
-    def actors(i, carry):
+    def actors(i):
         x = turn_rows(width, picked_ref)
         x_ref[:, pl.ds(pl.multiple_of(i * width, width), width)] = x
         actor_block(i, width, x, count_ref, weights, grads)
-        pick_rows(lax.rem(i + 1, blocks), width, index_ref, rows_ref, picked_ref)
+
+    def actors_and_pick(i, carry):
+        actors(i)
+        pick_rows(i + 1, width, index_ref, rows_ref, picked_ref)
 
         @pl.when(i == 0)
         def _():
@@ -773,7 +776,7 @@
                 AT, maps, actor_t_ref, flat_ref, pad_ref, w1_ref, w2f_ref, w2b_ref, b2_ref, w3t_ref, w3b_ref, b3a_ref
             )
 
-        for stage in range(1, 4):
+        for stage in range(1, blocks - 1):
 
             @pl.when(i == stage)
             def _():
@@ -782,7 +785,10 @@
 
         return carry
 
-    lax.fori_loop(0, blocks, actors, 0)
+    lax.fori_loop(0, blocks - 1, actors_and_pick, 0)
+    actors(blocks - 1)
+    noise.wait(2)
+    noise.start(3)
     pack_actor(pack_ref, maps, grads)
     late = CriticSum(place, pack_ref, out_hbm, buffers[:5], sems.at[0])
     early = ActorSum(place, pack_ref, buffers[5 : len(SUM_BUFFERS)], sems.at[1])

time: 78.3 us -> 78.7 us (level)
  no operation moved by 1% of the time
where the time goes in v12:
time: 78.7 us; the launch traced here: 78.5 us
  Pallas kernels  77.6 us (99%)
  between operations  0.94 us (1%)
    pallas_call x1, Pallas kernels, local(): pl.pallas_call(functools.partial(step_kernel, WIDTH), out_shape=SDS(RESUL...  73.4 us
    pallas_call x1, Pallas kernels, local(): pl.pallas_call(update_kernel, out_shape=tuple(shapes + places), in_specs=...  4.11 us

profile of v12, /device:TPU:1, one launch (start us, length us, event | category | flops | bytes accessed | tf_op | source)
XLA Modules:
  0.0 78.5 jit_solution(8543081070346851168)
XLA Ops:
  0.6 0.0 copy-start.1
  0.7 0.0 copy-start.3
  0.7 0.0 copy-start
  0.7 0.0 copy-start.2
  0.7 0.0 copy-start.5
  0.7 0.0 copy-start.7
  0.7 0.0 copy-start.4
  0.7 0.0 copy-start.6
  0.7 73.4 %td3_step.1.sum_hbm = f32[3700,16,128]{2,1,0:T(8,128)} custom-call(f32[42,8192]{1,0:T(8,128)} %bitcast.12, s32[32,128]{1,0:T(8,128)} %bitcast.14, f32[6,32,128]{2,1,0:T(8,128)} %bitcast.13, s32[1,128]{1,0:T(1,128)} %count_hbm.1, f32[71942]{0:T(1024)} %refs_0_.1, f32[71942]{0:T(1024)} %refs_6_.1, f32[2,72193]{1,0:T(2,128)} %refs_1_.1, f32[2,72193]{1,0:T(2,128)} %refs_7_.1), custom_call_target="tpu_custom_call" | custom-call | tf_op jit(solution)/shard_map/td3_step/pallas_call | solution.py:945
  74.2 0.0 copy-done.1
  74.2 0.0 copy-done.3
  74.2 0.0 copy-done
  74.2 0.0 copy-done.2
  74.2 0.0 copy-done.5
  74.2 0.0 copy-done.7
  74.2 0.0 copy-done.4
  74.3 0.0 copy-done.6
  74.3 4.1 %update.1 = (f32[2]{0:T(128)}, f32[2,16,128]{2,1,0:T(8,128)}, f32[71942]{0:T(1024)}, f32[2,72193]{1,0:T(2,128)}, f32[71942]{0:T(1024)}, /*index=5*/f32[2,72193]{...) custom-call(f32[3700,16,128]{2,1,0:T(8,128)} %td3_step.1.sum_hbm, ...), custom_call_target="tpu_custom_call" | custom-call | tf_op jit(solution)/shard_map/update/pallas_call | solution.py:995
Async XLA Ops:
  0.6 73.5 %copy-start.1 = (f32[2,72193]{1,0:T(2,128)S(1)}, f32[2,72193]{1,0:T(2,128)}, u32[]{:S(2)}) copy-start(f32[2,72193]{1,0:T(2,128)} %refs_7_.1) | copy-start | bytes 1732636
  0.7 73.5 %copy-start.3 = (f32[71942]{0:T(1024)S(1)}, f32[71942]{0:T(1024)}, u32[]{:S(2)}) copy-start(f32[71942]{0:T(1024)} %refs_6_.1) | copy-start | bytes 863308
  0.7 73.5 %copy-start = (f32[2,72193]{1,0:T(2,128)S(1)}, f32[2,72193]{1,0:T(2,128)}, u32[]{:S(2)}) copy-start(f32[2,72193]{1,0:T(2,128)} %refs_1_.1) | copy-start | bytes 1732636
  0.7 73.5 %copy-start.2 = (f32[71942]{0:T(1024)S(1)}, f32[71942]{0:T(1024)}, u32[]{:S(2)}) copy-start(f32[71942]{0:T(1024)} %refs_0_.1) | copy-start | bytes 863308
  0.7 73.5 %copy-start.5 = (f32[2,72193]{1,0:T(2,128)S(1)}, f32[2,72193]{1,0:T(2,128)}, u32[]{:S(2)}) copy-start(f32[2,72193]{1,0:T(2,128)} %refs_5_.1) | copy-start | bytes 1732636
  0.7 73.5 %copy-start.7 = (f32[71942]{0:T(1024)S(1)}, f32[71942]{0:T(1024)}, u32[]{:S(2)}) copy-start(f32[71942]{0:T(1024)} %refs_4_.1) | copy-start | bytes 863308
  0.7 73.5 %copy-start.4 = (f32[2,72193]{1,0:T(2,128)S(1)}, f32[2,72193]{1,0:T(2,128)}, u32[]{:S(2)}) copy-start(f32[2,72193]{1,0:T(2,128)} %refs_3_.1) | copy-start | bytes 1732636
  0.7 73.5 %copy-start.6 = (f32[71942]{0:T(1024)S(1)}, f32[71942]{0:T(1024)}, u32[]{:S(2)}) copy-start(f32[71942]{0:T(1024)} %refs_2_.1) | copy-start | bytes 863308
